TPU v7x, 32 devices: a whole 2x2x4 slice. The times are simulated.
32 devices in a mesh: dp: 2 (over core), row: 4 (over y, x), col: 4 (over z).
Axes of the slice: x: 2, y: 2, z: 4, core: 2. Of those that a mesh axis runs over, the one named last changes fastest.
Arguments:
- block_input: bfloat16 [20480, 2048], P(('dp', 'col'), 'row'), may hold values from -45 to 45
- cotangent: bfloat16 [20480, 2048], P(('dp', 'col'), 'row'), may hold values from -6 to 6
- attn_gain: bfloat16 [2048], P('row'), may hold values from 0.25 to 1.75
- attn_shift: bfloat16 [2048], P('row'), may hold values from -0.14941406 to 0.14941406
- query_weight: bfloat16 [2048, 2048], P('row', 'col'), may hold values from -0.125 to 0.125
- query_bias: bfloat16 [2048], P('col'), may hold values from -2.5 to 2.5
- keyval_weight: bfloat16 [2048, 256], P('row'), may hold values from -0.125 to 0.125
- value_bias: bfloat16 [128], replicated, may hold values from -0.14941406 to 0.14941406
- output_weight: bfloat16 [2048, 2048], P('col', 'row'), may hold values from -6 to 6
- output_bias: bfloat16 [2048], P('row'), may hold values from -4 to 4
- mlp_gain: bfloat16 [2048], P('row'), may hold values from 0.25 to 1.75
- mlp_shift: bfloat16 [2048], P('row'), may hold values from -1.5 to 1.5
- expand_weight: bfloat16 [2048, 8192], P('row', 'col'), may hold values from -0.125 to 0.125
- expand_bias: bfloat16 [8192], P('col'), may hold values from -2.5 to 2.5
- shrink_weight: bfloat16 [8192, 2048], P('col', 'row'), may hold values from -0.0625 to 0.0625
- shrink_bias: bfloat16 [2048], P('row'), may hold values from -4 to 4
- seg_parent: int32 [4, 13], P('dp'), may hold values from -1 to 12, as said below
- seg_start: int32 [4, 13], P('dp'), may hold values from 0 to 4864, as said below
- seg_length: int32 [4, 13], P('dp'), may hold values from 256 to 2048, as said below
Outputs:
- block_output: bfloat16 [20480, 2048], P(('dp', 'col'), 'row')
- input_grad: float32 [20480, 2048], P(('dp', 'col'), 'row')
- attn_gain_grad: float32 [2048], P('row')
- attn_shift_grad: float32 [2048], P('row')
- query_weight_grad: float32 [2048, 2048], P('row', 'col')
- query_bias_grad: float32 [2048], P('col')
- keyval_weight_grad: float32 [2048, 256], P('row')
- value_bias_grad: float32 [128], replicated
- output_weight_grad: float32 [2048, 2048], P('col', 'row')
- output_bias_grad: float32 [2048], P('row')
- mlp_gain_grad: float32 [2048], P('row')
- mlp_shift_grad: float32 [2048], P('row')
- expand_weight_grad: float32 [2048, 8192], P('row', 'col')
- expand_bias_grad: float32 [8192], P('col')
- shrink_weight_grad: float32 [8192, 2048], P('col', 'row')
- shrink_bias_grad: float32 [2048], P('row')
Inputs may be any that keep to these rules, and one draw needn't show every extreme that they name: `seg_parent`: each tree has 13 segments in slots listed in memory order: one trunk (parent -1), 4 branches whose parent is the trunk and 2 leaves under each branch; the order of the slots is drawn, except that the last slot of every tree holds a branch. `seg_start`: segments are contiguous and tile the tree's 5120 tokens in slot order. `seg_length`: the trunk has 2048 tokens, every branch and leaf 256.
All inputs are finite; a program needn't handle non-finite values.
Results may differ from a plain program's by a relative error of at most 0.02.
Values may be sent and summed in bfloat16 or wider, within the bound.
No kernel may reach another device: no remote copies, remote signals or barrier semaphores. Data moves between devices by JAX's collectives and lax.ppermute only.
A program may use at most 448 MiB of HBM per device.

v0:
```python
import jax
import jax.numpy as jnp
from jax import lax
from jax.sharding import PartitionSpec as P

HD = 128
SEGS = 13
TREE_TOK = 5120


EPSILON = 1e-05


def matmul(first_arr, second_arr):
    return jnp.dot(first_arr, second_arr, preferred_element_type=jnp.float32)


def feature_sums(first_sum, second_sum):
    return lax.psum((first_sum, second_sum), "row")


def gather_cols(local_block):
    return lax.all_gather(local_block, "col", axis=0, tiled=True)


def row_product(tokens_all, weight_block, contract_dim):
    tokens_mine = lax.all_to_all(tokens_all, "row", split_axis=0, concat_axis=1, tiled=True)
    if contract_dim == 0:
        weight_full = lax.all_gather(weight_block, "row", axis=0, tiled=True)
        return matmul(tokens_mine, weight_full)
    weight_full = lax.all_gather(weight_block, "row", axis=1, tiled=True)
    return jnp.einsum("td,fd->tf", tokens_mine, weight_full, preferred_element_type=jnp.float32)


def gather_rows(local_block):
    return lax.all_gather(local_block, "row", axis=0, tiled=True)


def reduce_cols(partial_value):
    return lax.psum_scatter(
        partial_value.astype(jnp.bfloat16), "col", scatter_dimension=0, tiled=True
    ).astype(jnp.float32)


def norm_forward(values_in, gain_vec, shift_vec):
    full_width = values_in.shape[1] * lax.axis_size("row")
    total_sum, square_sum = feature_sums(
        jnp.sum(values_in, axis=1), jnp.sum(values_in * values_in, axis=1)
    )
    row_mean = total_sum / full_width
    inv_std = lax.rsqrt(square_sum / full_width - row_mean * row_mean + EPSILON)
    centred = (values_in - row_mean[:, None]) * inv_std[:, None]
    return (centred * gain_vec + shift_vec, centred, inv_std)


def norm_backward(grad_normed, centred, inv_std, gain_vec):
    full_width = grad_normed.shape[1] * lax.axis_size("row")
    scaled = grad_normed * gain_vec
    first_sum, second_sum = feature_sums(jnp.sum(scaled, axis=1), jnp.sum(scaled * centred, axis=1))
    grad_values = inv_std[:, None] * (
        scaled - first_sum[:, None] / full_width - centred * second_sum[:, None] / full_width
    )
    return (grad_values, jnp.sum(grad_normed * centred, axis=0), jnp.sum(grad_normed, axis=0))


def segment_tables(seg_parent, seg_start, seg_length):
    trees_here = seg_parent.shape[0]
    combo_count = trees_here * SEGS
    places = jnp.arange(trees_here * TREE_TOK, dtype=jnp.int32)
    tree_of = places // TREE_TOK
    in_tree = places % TREE_TOK
    combo_ids = jnp.arange(combo_count, dtype=jnp.int32)
    combo_tree = combo_ids // SEGS
    starts_flat = seg_start.reshape(combo_count)
    ends_flat = starts_flat + seg_length.reshape(combo_count)
    member = (
        (tree_of[None, :] == combo_tree[:, None])
        & (in_tree[None, :] >= starts_flat[:, None])
        & (in_tree[None, :] < ends_flat[:, None])
    )
    parent_flat = seg_parent.reshape(combo_count)
    parent_combo = jnp.where(parent_flat >= 0, combo_tree * SEGS + parent_flat, -1)
    grand_combo = jnp.where(parent_combo >= 0, parent_combo[jnp.maximum(parent_combo, 0)], -1)
    strict = (parent_combo[:, None] == combo_ids[None, :]) | (
        grand_combo[:, None] == combo_ids[None, :]
    )
    return (member.astype(jnp.float32), strict.astype(jnp.float32))


def block_mask(key_onehot, strict, first_row, block_rows):
    query_onehot = lax.dynamic_slice_in_dim(key_onehot, first_row, block_rows, 1)
    ancestors = jnp.dot(query_onehot.T, strict)
    reach = jnp.dot(ancestors, key_onehot)
    same_seg = jnp.dot(query_onehot.T, key_onehot)
    query_pos = first_row + jnp.arange(block_rows, dtype=jnp.int32)
    key_pos = jnp.arange(key_onehot.shape[1], dtype=jnp.int32)
    return (reach > 0.5) | (same_seg > 0.5) & (key_pos[None, :] <= query_pos[:, None])


def pick_rows(query_rows):
    for candidate in range(min(query_rows, 640), 0, -1):
        if query_rows % candidate == 0:
            return candidate
    return query_rows


def attention_forward(queries, keyval, key_onehot, strict, row_base, block_rows):
    keys_part = keyval[:, :HD]
    values_part = keyval[:, HD:]
    query_rows = queries.shape[0]
    heads_here = queries.shape[1] // HD
    score_scale = HD ** (-0.5)

    def one_block(blk_index):
        blk_start = blk_index * block_rows
        query_blk = lax.dynamic_slice_in_dim(queries, blk_start, block_rows, 0)
        query_blk = query_blk.reshape(block_rows, heads_here, HD).transpose(1, 0, 2)
        visible = block_mask(key_onehot, strict, row_base + blk_start, block_rows)

        def one_head(query_head):
            scores = (
                jnp.einsum("qd,kd->qk", query_head, keys_part, preferred_element_type=jnp.float32)
                * score_scale
            )
            masked = jnp.where(visible, scores, -1e30)
            row_top = jnp.max(masked, axis=1, keepdims=True)
            exp_scores = jnp.exp(masked - row_top)
            row_total = jnp.sum(exp_scores, axis=1, keepdims=True)
            weights_low = (exp_scores / row_total).astype(jnp.bfloat16)
            head_out = jnp.dot(weights_low, values_part, preferred_element_type=jnp.float32)
            return (head_out, (row_top + jnp.log(row_total))[:, 0])

        head_outs, log_sums = lax.map(one_head, query_blk)
        return (head_outs.transpose(1, 0, 2).reshape(block_rows, heads_here * HD), log_sums)

    out_blocks, log_sums = lax.map(one_block, jnp.arange(query_rows // block_rows, dtype=jnp.int32))
    return (out_blocks.reshape(query_rows, heads_here * HD).astype(jnp.bfloat16), log_sums)


def attention_backward(
    queries, keyval, grad_attended, log_sums, key_onehot, strict, row_base, block_rows
):
    keys_part = keyval[:, :HD]
    values_part = keyval[:, HD:]
    query_rows = queries.shape[0]
    heads_here = queries.shape[1] // HD
    score_scale = HD ** (-0.5)

    def one_block(carried, blk_index):
        blk_start = blk_index * block_rows
        query_blk = lax.dynamic_slice_in_dim(queries, blk_start, block_rows, 0)
        query_blk = query_blk.reshape(block_rows, heads_here, HD).transpose(1, 0, 2)
        grad_blk = lax.dynamic_slice_in_dim(grad_attended, blk_start, block_rows, 0)
        grad_blk = grad_blk.reshape(block_rows, heads_here, HD).transpose(1, 0, 2)
        visible = block_mask(key_onehot, strict, row_base + blk_start, block_rows)
        lse_blk = log_sums[blk_index]

        def one_head(head_acc, head_parts):
            query_head, grad_head, lse_head = head_parts
            scores = (
                jnp.einsum("qd,kd->qk", query_head, keys_part, preferred_element_type=jnp.float32)
                * score_scale
            )
            weights = jnp.exp(jnp.where(visible, scores - lse_head[:, None], -1e30))
            grad_weights = jnp.einsum(
                "qd,kd->qk", grad_head, values_part, preferred_element_type=jnp.float32
            )
            row_dot = jnp.sum(grad_weights * weights, axis=1, keepdims=True)
            grad_scores = (weights * (grad_weights - row_dot)).astype(jnp.bfloat16)
            grad_query = (
                jnp.dot(grad_scores, keys_part, preferred_element_type=jnp.float32) * score_scale
            )
            grad_keys = (
                jnp.einsum("qk,qd->kd", grad_scores, query_head, preferred_element_type=jnp.float32)
                * score_scale
            )
            grad_values = jnp.einsum(
                "qk,qd->kd",
                weights.astype(jnp.bfloat16),
                grad_head,
                preferred_element_type=jnp.float32,
            )
            return (head_acc + jnp.concatenate([grad_keys, grad_values], axis=1), grad_query)

        carried, grad_heads = lax.scan(one_head, carried, (query_blk, grad_blk, lse_blk))
        return (carried, grad_heads.transpose(1, 0, 2).reshape(block_rows, heads_here * HD))

    zero_grads = jnp.zeros((keyval.shape[0], 2 * HD), jnp.float32)
    grad_keyval, grad_blocks = lax.scan(
        one_block, zero_grads, jnp.arange(query_rows // block_rows, dtype=jnp.int32)
    )
    return (grad_blocks.reshape(query_rows, heads_here * HD), grad_keyval)


def gelu_tanh(values_in):
    return jax.nn.gelu(values_in, approximate=True)


def on_device(
    block_input,
    cotangent,
    attn_gain,
    attn_shift,
    query_weight,
    query_bias,
    keyval_weight,
    value_bias,
    output_weight,
    output_bias,
    mlp_gain,
    mlp_shift,
    expand_weight,
    expand_bias,
    shrink_weight,
    shrink_bias,
    seg_parent,
    seg_start,
    seg_length,
):
    local_rows = block_input.shape[0]
    col_index = lax.axis_index("col")
    key_onehot, strict = segment_tables(seg_parent, seg_start, seg_length)
    resid_in = block_input.astype(jnp.float32)
    attn_gain_f = attn_gain.astype(jnp.float32)
    mlp_gain_f = mlp_gain.astype(jnp.float32)
    normed_f, centred_one, inv_std_one = norm_forward(
        resid_in, attn_gain_f, attn_shift.astype(jnp.float32)
    )
    normed = normed_f.astype(jnp.bfloat16)
    normed_all = gather_cols(normed)
    query_sum = row_product(normed_all, query_weight, 0)
    queries = (query_sum + query_bias.astype(jnp.float32)).astype(jnp.bfloat16)
    value_shift = jnp.concatenate([jnp.zeros((HD,), jnp.float32), value_bias.astype(jnp.float32)])
    kv_part = matmul(normed_all, keyval_weight)
    kv_total = lax.psum(kv_part, "row")
    keyval = (kv_total + value_shift).astype(jnp.bfloat16)
    query_rows = queries.shape[0]
    block_rows = pick_rows(query_rows)
    row_base = lax.axis_index("row") * query_rows
    attended, log_sums = attention_forward(
        queries, keyval, key_onehot, strict, row_base, block_rows
    )
    attended_all = gather_rows(attended)
    middle = (
        resid_in
        + reduce_cols(matmul(attended_all, output_weight))
        + output_bias.astype(jnp.float32)
    )
    normed_two_f, centred_two, inv_std_two = norm_forward(
        middle, mlp_gain_f, mlp_shift.astype(jnp.float32)
    )
    normed_two_all = gather_cols(normed_two_f.astype(jnp.bfloat16))
    pre_act = row_product(normed_two_all, expand_weight, 0) + expand_bias.astype(jnp.float32)
    activ = gelu_tanh(pre_act).astype(jnp.bfloat16)
    activ_all = gather_rows(activ)
    branch_two = reduce_cols(matmul(activ_all, shrink_weight)) + shrink_bias.astype(jnp.float32)
    block_output = (middle + branch_two).astype(jnp.bfloat16)
    grad_out_all = gather_cols(cotangent)
    shrink_weight_part = jnp.einsum(
        "tf,td->fd", activ_all, grad_out_all, preferred_element_type=jnp.float32
    )
    shrink_bias_part = jnp.sum(grad_out_all, axis=0, dtype=jnp.float32)
    grad_activ = row_product(grad_out_all, shrink_weight, 1)
    ignored, gelu_pull = jax.vjp(gelu_tanh, pre_act)
    grad_pre = gelu_pull(grad_activ)[0].astype(jnp.bfloat16)
    grad_pre_all = gather_rows(grad_pre)
    expand_weight_part = jnp.einsum(
        "td,tf->df", normed_two_all, grad_pre_all, preferred_element_type=jnp.float32
    )
    expand_bias_part = jnp.sum(grad_pre_all, axis=0, dtype=jnp.float32)
    grad_normed_two = reduce_cols(
        jnp.einsum("tf,df->td", grad_pre_all, expand_weight, preferred_element_type=jnp.float32)
    )
    grad_mid_norm, mlp_gain_part, mlp_shift_part = norm_backward(
        grad_normed_two, centred_two, inv_std_two, mlp_gain_f
    )
    grad_middle = cotangent.astype(jnp.float32) + grad_mid_norm
    grad_mid_all = gather_cols(grad_middle.astype(jnp.bfloat16))
    output_weight_part = jnp.einsum(
        "te,td->ed", attended_all, grad_mid_all, preferred_element_type=jnp.float32
    )
    output_bias_part = jnp.sum(grad_mid_all, axis=0, dtype=jnp.float32)
    grad_attended = row_product(grad_mid_all, output_weight, 1).astype(jnp.bfloat16)
    grad_queries, grad_kv_part = attention_backward(
        queries, keyval, grad_attended, log_sums, key_onehot, strict, row_base, block_rows
    )
    grad_q_all = gather_rows(grad_queries.astype(jnp.bfloat16))
    query_weight_part = jnp.einsum(
        "td,te->de", normed_all, grad_q_all, preferred_element_type=jnp.float32
    )
    query_bias_part = jnp.sum(grad_q_all, axis=0, dtype=jnp.float32)
    grad_normed = reduce_cols(
        jnp.einsum("te,de->td", grad_q_all, query_weight, preferred_element_type=jnp.float32)
    )
    grad_kv = lax.psum(grad_kv_part, ("row", "col")).astype(jnp.bfloat16)
    grad_kv_mine = lax.dynamic_slice_in_dim(grad_kv, col_index * local_rows, local_rows, 0)
    keyval_weight_part = jnp.einsum(
        "td,tk->dk", normed, grad_kv_mine, preferred_element_type=jnp.float32
    )
    value_bias_part = jnp.sum(grad_kv_mine[:, HD:], axis=0, dtype=jnp.float32)
    grad_normed = grad_normed + jnp.einsum(
        "tk,dk->td", grad_kv_mine, keyval_weight, preferred_element_type=jnp.float32
    )
    grad_in_norm, attn_gain_part, attn_shift_part = norm_backward(
        grad_normed, centred_one, inv_std_one, attn_gain_f
    )
    input_grad = grad_middle + grad_in_norm
    (
        query_weight_grad,
        query_bias_grad,
        output_weight_grad,
        output_bias_grad,
        expand_weight_grad,
        expand_bias_grad,
        shrink_weight_grad,
        shrink_bias_grad,
    ) = (
        lax.psum(query_weight_part.astype(jnp.bfloat16), "dp").astype(jnp.float32),
        lax.psum(query_bias_part.astype(jnp.bfloat16), "dp").astype(jnp.float32),
        lax.psum(output_weight_part.astype(jnp.bfloat16), "dp").astype(jnp.float32),
        lax.psum(output_bias_part.astype(jnp.bfloat16), "dp").astype(jnp.float32),
        lax.psum(expand_weight_part.astype(jnp.bfloat16), "dp").astype(jnp.float32),
        lax.psum(expand_bias_part.astype(jnp.bfloat16), "dp").astype(jnp.float32),
        lax.psum(shrink_weight_part.astype(jnp.bfloat16), "dp").astype(jnp.float32),
        lax.psum(shrink_bias_part.astype(jnp.bfloat16), "dp").astype(jnp.float32),
    )
    (
        attn_gain_grad,
        attn_shift_grad,
        keyval_weight_grad,
        value_bias_grad,
        mlp_gain_grad,
        mlp_shift_grad,
    ) = (
        lax.psum(attn_gain_part.astype(jnp.bfloat16), ("dp", "col")).astype(jnp.float32),
        lax.psum(attn_shift_part.astype(jnp.bfloat16), ("dp", "col")).astype(jnp.float32),
        lax.psum(keyval_weight_part.astype(jnp.bfloat16), ("dp", "col")).astype(jnp.float32),
        lax.psum(value_bias_part.astype(jnp.bfloat16), ("dp", "col")).astype(jnp.float32),
        lax.psum(mlp_gain_part.astype(jnp.bfloat16), ("dp", "col")).astype(jnp.float32),
        lax.psum(mlp_shift_part.astype(jnp.bfloat16), ("dp", "col")).astype(jnp.float32),
    )
    return (
        block_output,
        input_grad,
        attn_gain_grad,
        attn_shift_grad,
        query_weight_grad,
        query_bias_grad,
        keyval_weight_grad,
        value_bias_grad,
        output_weight_grad,
        output_bias_grad,
        mlp_gain_grad,
        mlp_shift_grad,
        expand_weight_grad,
        expand_bias_grad,
        shrink_weight_grad,
        shrink_bias_grad,
    )


def solution(mesh):
    return jax.shard_map(
        on_device,
        mesh=mesh,
        in_specs=(
            P(("dp", "col"), "row"),
            P(("dp", "col"), "row"),
            P("row"),
            P("row"),
            P("row", "col"),
            P("col"),
            P("row", None),
            P(),
            P("col", "row"),
            P("row"),
            P("row"),
            P("row"),
            P("row", "col"),
            P("col"),
            P("col", "row"),
            P("row"),
            P("dp", None),
            P("dp", None),
            P("dp", None),
        ),
        out_specs=(
            P(("dp", "col"), "row"),
            P(("dp", "col"), "row"),
            P("row"),
            P("row"),
            P("row", "col"),
            P("col"),
            P("row", None),
            P(),
            P("col", "row"),
            P("row"),
            P("row"),
            P("row"),
            P("row", "col"),
            P("col"),
            P("col", "row"),
            P("row"),
        ),
        check_vma=False,
    )
```

profile of v0, /device:TPU:0, one launch (start us, length us, event | category | flops | bytes accessed | tf_op | source)
XLA Modules:
  0.0 6112.8 jit_solution(17172566041869343324)
XLA Ops:
  34.1 182.7 %all-gather.13.cloned.1.call-done = bf16[10240,512]{1,0:T(8,128)(2,1)} async-done(((bf16[2560,512]{1,0:T(8,128)(2,1)}), bf16[10240,512]{1,0:T(8,128)(2,1)}) %all-gather.13.cloned.1.call-update) | async-done | bytes 10485776 | tf_op jit(solution)/shard_map/all_gather | solution.py:23
  417.5 145.6 %all-reduce.13.cloned.1.call-done = f32[10240,256]{1,0:T(8,128)} async-done(((f32[10240,256]{1,0:T(8,128)}), f32[10240,256]{1,0:T(8,128)}) %all-reduce.13.cloned.1.call-update) | async-done | bytes 10485776 | tf_op jit(solution)/shard_map/psum | solution.py:235
  571.8 758.8 %while.53 = (s32[]{:T(128)}, bf16[4,640,512]{2,1,0:T(8,128)(2,1)}, f32[4,4,640]{2,1,0:T(4,128)}, s32[4]{0:T(128)}, bf16[2560,512]{0,1:T(8,128)(2,1)}, /*index=5*...) while((s32[]{:T(128)}, bf16[4,640,512]{2,1,0:T(8,128)(2,1)}, ...), condition=%wide.region_10.11_spmd.clone, body=%wide.region_5.10_spmd.clone.sunk | while | flops 4123082496 | bytes 172339232 | solution.py:136
  603.4 152.2 %while.56 = (s32[]{:T(128)}, bf16[4,640,128]{2,1,0:T(8,128)(2,1)}, f32[4,640]{1,0:T(4,128)}, bf16[4,640,128]{1,2,0:T(8,128)(2,1)S(1)}, bf16[10240,128]{1,0:T(8,1...) while((s32[]{:T(128)}, bf16[4,640,128]{2,1,0:T(8,128)(2,1)}, ...), condition=%wide.region_9.9_spmd, body=%wide.region_6.8_spmd.sunk | while | flops 3407871488 | bytes 106693824 | solution.py:133
  792.9 152.2 %while.56 = (s32[]{:T(128)}, bf16[4,640,128]{2,1,0:T(8,128)(2,1)}, f32[4,640]{1,0:T(4,128)}, bf16[4,640,128]{1,2,0:T(8,128)(2,1)S(1)}, bf16[10240,128]{1,0:T(8,1...) while((s32[]{:T(128)}, bf16[4,640,128]{2,1,0:T(8,128)(2,1)}, ...), condition=%wide.region_9.9_spmd, body=%wide.region_6.8_spmd.sunk | while | flops 3407871488 | bytes 106693824 | solution.py:133
  982.5 152.2 %while.56 = (s32[]{:T(128)}, bf16[4,640,128]{2,1,0:T(8,128)(2,1)}, f32[4,640]{1,0:T(4,128)}, bf16[4,640,128]{1,2,0:T(8,128)(2,1)S(1)}, bf16[10240,128]{1,0:T(8,1...) while((s32[]{:T(128)}, bf16[4,640,128]{2,1,0:T(8,128)(2,1)}, ...), condition=%wide.region_9.9_spmd, body=%wide.region_6.8_spmd.sunk | while | flops 3407871488 | bytes 106693824 | solution.py:133
  1172.0 152.2 %while.56 = (s32[]{:T(128)}, bf16[4,640,128]{2,1,0:T(8,128)(2,1)}, f32[4,640]{1,0:T(4,128)}, bf16[4,640,128]{1,2,0:T(8,128)(2,1)S(1)}, bf16[10240,128]{1,0:T(8,1...) while((s32[]{:T(128)}, bf16[4,640,128]{2,1,0:T(8,128)(2,1)}, ...), condition=%wide.region_9.9_spmd, body=%wide.region_6.8_spmd.sunk | while | flops 3407871488 | bytes 106693824 | solution.py:133
  1330.6 105.5 %all-gather.17.cloned.1.call-done = bf16[10240,512]{1,0:T(8,128)(2,1)} async-done(((bf16[2560,512]{1,0:T(8,128)(2,1)}), bf16[10240,512]{1,0:T(8,128)(2,1)}) %all-gather.17.cloned.1.call-update) | async-done | bytes 10485776 | tf_op jit(solution)/shard_map/all_gather | solution.py:36
  1447.7 177.5 %reduce-scatter.5.cloned.1.call-done = bf16[2560,512]{1,0:T(8,128)(2,1)} async-done(((bf16[10240,512]{1,0:T(8,128)(2,1)}), bf16[2560,512]{1,0:T(8,128)(2,1)}) %reduce-scatter.5.cloned.1.call-update) | async-done | bytes 2621456 | tf_op jit(solution)/shard_map/reduce_scatter | solution.py:40
  1649.9 161.7 %all-gather.25.cloned.1.call-done = bf16[10240,512]{1,0:T(8,128)(2,1)} async-done(((bf16[2560,512]{1,0:T(8,128)(2,1)}), bf16[10240,512]{1,0:T(8,128)(2,1)}) %all-gather.25.cloned.1.call-update) | async-done | bytes 10485776 | tf_op jit(solution)/shard_map/all_gather | solution.py:23
  1818.3 177.6 %all-gather.19.cloned.1.call-done = bf16[10240,512]{1,0:T(8,128)(2,1)} async-done(((bf16[2560,512]{1,0:T(8,128)(2,1)}), bf16[10240,512]{1,0:T(8,128)(2,1)}) %all-gather.19.cloned.1.call-update) | async-done | bytes 10485776 | tf_op jit(solution)/shard_map/all_gather | solution.py:23
  2030.1 158.2 %all-gather.21.cloned.1.call-done = bf16[2048,2048]{1,0:T(8,128)(2,1)} async-done(((bf16[512,2048]{1,0:T(8,128)(2,1)}), bf16[2048,2048]{1,0:T(8,128)(2,1)}) %all-gather.21.cloned.1.call-update) | async-done | bytes 8388624 | tf_op jit(solution)/shard_map/all_gather | solution.py:29
  2324.7 366.9 %all-gather.29.cloned.1.call-done = bf16[10240,2048]{1,0:T(8,128)(2,1)} async-done(((bf16[2560,2048]{1,0:T(8,128)(2,1)}), bf16[10240,2048]{1,0:T(8,128)(2,1)}) %all-gather.29.cloned.1.call-update) | async-done | bytes 41943056 | tf_op jit(solution)/shard_map/all_gather | solution.py:36
  2724.5 336.5 %all-gather.23.cloned.1.call-done = bf16[10240,2048]{1,0:T(8,128)(2,1)} async-done(((bf16[2560,2048]{1,0:T(8,128)(2,1)}), bf16[10240,2048]{1,0:T(8,128)(2,1)}) %all-gather.23.cloned.1.call-update) | async-done | bytes 41943056 | tf_op jit(solution)/shard_map/all_gather | solution.py:36
  3091.1 150.2 %reduce-scatter.9.cloned.1.call-done = bf16[2560,512]{1,0:T(8,128)(2,1)} async-done(((bf16[10240,512]{1,0:T(8,128)(2,1)}), bf16[2560,512]{1,0:T(8,128)(2,1)}) %reduce-scatter.9.cloned.1.call-update) | async-done | bytes 2621456 | tf_op jit(solution)/shard_map/reduce_scatter | solution.py:40
  3263.4 159.3 %reduce-scatter.7.cloned.1.call-done = bf16[2560,512]{1,0:T(8,128)(2,1)} async-done(((bf16[10240,512]{1,0:T(8,128)(2,1)}), bf16[2560,512]{1,0:T(8,128)(2,1)}) %reduce-scatter.7.cloned.1.call-update) | async-done | bytes 2621456 | tf_op jit(solution)/shard_map/reduce_scatter | solution.py:40
  3433.3 185.1 %all-gather.31.cloned.1.call-done = bf16[10240,512]{1,0:T(8,128)(2,1)} async-done(((bf16[2560,512]{1,0:T(8,128)(2,1)}), bf16[10240,512]{1,0:T(8,128)(2,1)}) %all-gather.31.cloned.1.call-update) | async-done | bytes 10485776 | tf_op jit(solution)/shard_map/all_gather | solution.py:23
  3789.2 1515.6 %while.55 = (s32[]{:T(128)}, f32[10240,256]{0,1:T(8,128)}, bf16[4,640,512]{2,1,0:T(8,128)(2,1)}, s32[4]{0:T(128)}, bf16[2560,512]{0,1:T(8,128)(2,1)}, /*index=5*...) while((s32[]{:T(128)}, f32[10240,256]{0,1:T(8,128)}, ...), condition=%wide.region_26.27_spmd.clone, body=%wide.region_22.26_spmd.clone.sunk | while | flops 9169436672 | bytes 343286528 | solution.py:189
  3827.9 335.3 %while.57 = (s32[]{:T(128)}, f32[10240,256]{0,1:T(8,128)}, bf16[4,640,128]{2,1,0:T(8,128)(2,1)}, bf16[4,640,128]{1,2,0:T(8,128)(2,1)}, bf16[10240,128]{1,0:T(8,1...) while((s32[]{:T(128)}, f32[10240,256]{0,1:T(8,128)}, ...), condition=%wide.region_25.25_spmd, body=%wide.region_23.24_spmd.sunk | while | flops 8454225408 | bytes 275018496 | solution.py:185
  4206.7 335.3 %while.57 = (s32[]{:T(128)}, f32[10240,256]{0,1:T(8,128)}, bf16[4,640,128]{2,1,0:T(8,128)(2,1)}, bf16[4,640,128]{1,2,0:T(8,128)(2,1)}, bf16[10240,128]{1,0:T(8,1...) while((s32[]{:T(128)}, f32[10240,256]{0,1:T(8,128)}, ...), condition=%wide.region_25.25_spmd, body=%wide.region_23.24_spmd.sunk | while | flops 8454225408 | bytes 275018496 | solution.py:185
  4585.4 335.3 %while.57 = (s32[]{:T(128)}, f32[10240,256]{0,1:T(8,128)}, bf16[4,640,128]{2,1,0:T(8,128)(2,1)}, bf16[4,640,128]{1,2,0:T(8,128)(2,1)}, bf16[10240,128]{1,0:T(8,1...) while((s32[]{:T(128)}, f32[10240,256]{0,1:T(8,128)}, ...), condition=%wide.region_25.25_spmd, body=%wide.region_23.24_spmd.sunk | while | flops 8454225408 | bytes 275018496 | solution.py:185
  4964.2 335.3 %while.57 = (s32[]{:T(128)}, f32[10240,256]{0,1:T(8,128)}, bf16[4,640,128]{2,1,0:T(8,128)(2,1)}, bf16[4,640,128]{1,2,0:T(8,128)(2,1)}, bf16[10240,128]{1,0:T(8,1...) while((s32[]{:T(128)}, f32[10240,256]{0,1:T(8,128)}, ...), condition=%wide.region_25.25_spmd, body=%wide.region_23.24_spmd.sunk | while | flops 8454225408 | bytes 275018496 | solution.py:185
  5346.3 436.1 %all-reduce.18 = bf16[10240,256]{0,1:T(8,128)(2,1)} all-reduce(f32[10240,256]{0,1:T(8,128)} %get-tuple-element.1012), channel_id=1, replica_groups=mesh['dp'=2,'row'=4,'col'=4] {'row','col'}, use_global_device_ids=true, to_apply=%region_28.29 | all-reduce | flops 2621440 | bytes 15728640 | tf_op jit(solution)/shard_map/psum | solution.py:295
  5884.1 170.2 %reduce-scatter.11.cloned.1.call-done = bf16[2560,512]{1,0:T(8,128)(2,1)} async-done(((bf16[10240,512]{1,0:T(8,128)(2,1)}), bf16[2560,512]{1,0:T(8,128)(2,1)}) %reduce-scatter.11.cloned.1.call-update) | async-done | bytes 2621456 | tf_op jit(solution)/shard_map/reduce_scatter | solution.py:40
  (868 shorter events, 3168.3 us)
Async XLA Ops:
  7.2 209.6 %all-gather.13.cloned.1.call-start = ((), (), s32[]{:S(2)}) async-start(), calls=%async_computation.8 | async-start | bytes 13107200 | tf_op jit(solution)/shard_map/all_gather | solution.py:23
  33.3 276.4 %all-gather.15.cloned.1.call-start = ((), (), s32[]{:S(2)}) async-start(), calls=%async_computation.9 | async-start | bytes 2621440 | tf_op jit(solution)/shard_map/all_gather | solution.py:29
  34.1 529.0 %all-reduce.13.cloned.1.call-start = ((), (), s32[]{:S(2)}) async-start(), calls=%async_computation.10 | async-start | bytes 20971520 | tf_op jit(solution)/shard_map/psum | solution.py:235
  241.4 164.1 %all-to-all-start = ((bf16[4,2560,512]{1,2,0:T(8,128)(2,1)}), bf16[4,2560,512]{1,2,0:T(8,128)(2,1)}, u32[]{:S(2)}, u32[]{:S(2)}) async-start(bf16[4,2560,512]{1,2,0:T(8,128)(2,1)} %copy.53), calls=%async_computation | async-start | bytes 20971520 | tf_op jit(solution)/shard_map/all_to_all | solution.py:27
  247.6 1188.6 %all-gather.17.cloned.1.call-start = ((), (), s32[]{:S(2)}) async-start(), calls=%async_computation.11 | async-start | bytes 13107200 | tf_op jit(solution)/shard_map/all_gather | solution.py:36
  1330.6 294.6 %reduce-scatter.5.cloned.1.call-start = ((), (), s32[]{:S(2)}) async-start(), calls=%async_computation.12 | async-start | bytes 13107200 | tf_op jit(solution)/shard_map/reduce_scatter | solution.py:40
  1447.0 364.6 %all-gather.25.cloned.1.call-start = ((), (), s32[]{:S(2)}) async-start(), calls=%async_computation.17 | async-start | bytes 13107200 | tf_op jit(solution)/shard_map/all_gather | solution.py:23
  1447.6 548.3 %all-gather.19.cloned.1.call-start = ((), (), s32[]{:S(2)}) async-start(), calls=%async_computation.13 | async-start | bytes 13107200 | tf_op jit(solution)/shard_map/all_gather | solution.py:23
  1649.1 539.1 %all-gather.21.cloned.1.call-start = ((), (), s32[]{:S(2)}) async-start(), calls=%async_computation.14 | async-start | bytes 10485760 | tf_op jit(solution)/shard_map/all_gather | solution.py:29
  1811.6 198.5 %all-to-all-start.2 = ((bf16[4,2560,512]{2,1,0:T(8,128)(2,1)}), bf16[4,2560,512]{2,1,0:T(8,128)(2,1)}, u32[]{:S(2)}, u32[]{:S(2)}) async-start(bf16[4,2560,512]{2,1,0:T(8,128)(2,1)} %bitcast.167), calls=%async_computation.4 | async-start | bytes 20971520 | tf_op jit(solution)/shard_map/all_to_all | solution.py:27
  1817.5 460.0 %all-gather.27.cloned.1.call-start = ((), (), s32[]{:S(2)}) async-start(), calls=%async_computation.18 | async-start | bytes 10485760 | tf_op jit(solution)/shard_map/all_gather | solution.py:31
  2010.0 178.2 %all-to-all-start.1 = ((bf16[4,2560,512]{1,2,0:T(8,128)(2,1)}), bf16[4,2560,512]{1,2,0:T(8,128)(2,1)}, u32[]{:S(2)}, u32[]{:S(2)}) async-start(bf16[4,2560,512]{1,2,0:T(8,128)(2,1)} %copy.55), calls=%async_computation.2 | async-start | bytes 20971520 | tf_op jit(solution)/shard_map/all_to_all | solution.py:27
  2016.1 675.5 %all-gather.29.cloned.1.call-start = ((), (), s32[]{:S(2)}) async-start(), calls=%async_computation.19 | async-start | bytes 52428800 | tf_op jit(solution)/shard_map/all_gather | solution.py:36
  2323.9 737.1 %all-gather.23.cloned.1.call-start = ((), (), s32[]{:S(2)}) async-start(), calls=%async_computation.15 | async-start | bytes 52428800 | tf_op jit(solution)/shard_map/all_gather | solution.py:36
  2324.7 916.6 %reduce-scatter.9.cloned.1.call-start = ((), (), s32[]{:S(2)}) async-start(), calls=%async_computation.20 | async-start | bytes 13107200 | tf_op jit(solution)/shard_map/reduce_scatter | solution.py:40
  2724.4 698.3 %reduce-scatter.7.cloned.1.call-start = ((), (), s32[]{:S(2)}) async-start(), calls=%async_computation.16 | async-start | bytes 13107200 | tf_op jit(solution)/shard_map/reduce_scatter | solution.py:40
  3090.5 528.0 %all-gather.31.cloned.1.call-start = ((), (), s32[]{:S(2)}) async-start(), calls=%async_computation.21 | async-start | bytes 13107200 | tf_op jit(solution)/shard_map/all_gather | solution.py:23
  3632.1 138.3 %all-to-all-start.3 = ((bf16[4,2560,512]{1,2,0:T(8,128)(2,1)}), bf16[4,2560,512]{1,2,0:T(8,128)(2,1)}, u32[]{:S(2)}, u32[]{:S(2)}) async-start(bf16[4,2560,512]{1,2,0:T(8,128)(2,1)} %copy.57), calls=%async_computation.6 | async-start | bytes 20971520 | tf_op jit(solution)/shard_map/all_to_all | solution.py:27
  3638.3 98.0 %all-gather.33.cloned.1.call-start = ((), (), s32[]{:S(2)}) async-start(), calls=%async_computation.22 | async-start | bytes 2621440 | tf_op jit(solution)/shard_map/all_gather | solution.py:31
  3638.9 2147.6 %all-gather.35.cloned.1.call-start = ((), (), s32[]{:S(2)}) async-start(), calls=%async_computation.23 | async-start | bytes 13107200 | tf_op jit(solution)/shard_map/all_gather | solution.py:36
  5304.9 534.4 %all-reduce.15.cloned.1.call-start = ((), (), s32[]{:S(2)}) async-start(), calls=%async_computation.25 | async-start | bytes 524288 | tf_op jit(solution)/shard_map/psum | solution.py:337
  5346.3 438.5 %copy-start.18 = (bf16[2560,512]{1,0:T(8,128)(2,1)S(1)}, bf16[2560,512]{1,0:T(8,128)(2,1)}, u32[]{:S(2)}) copy-start(bf16[2560,512]{1,0:T(8,128)(2,1)} %fusion.89) | copy-start | bytes 7864324
  5786.5 86.3 %all-reduce.17.cloned.1.call-start = ((), (), s32[]{:S(2)}) async-start(), calls=%async_computation.26 | async-start | bytes 10485760 | tf_op jit(solution)/shard_map/psum | solution.py:318
  5798.7 255.6 %reduce-scatter.11.cloned.1.call-start = ((), (), s32[]{:S(2)}) async-start(), calls=%async_computation.24 | async-start | bytes 13107200 | tf_op jit(solution)/shard_map/reduce_scatter | solution.py:40
  (197 other events, 6862.1 us)
Sparse Core Ops, SparseCore 0:
  33.4 183.3 all-gather.12
  218.6 91.0 all-gather.14
  313.2 249.7 all-reduce.12
  1330.7 105.4 all-gather.16
  1447.1 178.0 reduce-scatter.4
  1626.6 184.9 all-gather.24
  1813.7 182.1 all-gather.18
  1997.7 190.5 all-gather.20
  2190.1 87.4 all-gather.26
  2324.1 367.5 all-gather.28
  2693.5 367.4 all-gather.22
  3063.2 178.0 reduce-scatter.8
  3243.6 179.0 reduce-scatter.6
  3433.4 184.9 all-gather.30
  3640.6 95.5 all-gather.32
  5305.0 154.1 all-gather.34
  5786.6 52.7 all-reduce.14
  5843.4 29.3 all-reduce.16
  5875.2 179.1 reduce-scatter.10
where the time goes:
time: 6130 us; the launch traced here: 6110 us
  waiting for transfers between devices  2820 us (46%)
  matrix products  1810 us (30%)
  other arithmetic  712 us (12%)
  blocking collectives  522 us (9%)
  local copies, waits for them, and re-layouts  194 us (3%)
    all_gather x4, waiting for transfers between devices, gather_rows(): return lax.all_gather(local_block, 'row', axis=0, tiled=True)  809 us
    all_gather x4, waiting for transfers between devices, gather_cols(): return lax.all_gather(local_block, 'col', axis=0, tiled=True)  707 us
    reduce_scatter x4, waiting for transfers between devices, reduce_cols(): lax.psum_scatter(partial_value.astype(jnp.bfloat16), 'col', scatter_dimen...  657 us
    dot_general x32, matrix products, one_head(): jnp.einsum('qd,kd->qk', query_head, keys_part, preferred_element_type=jnp...  453 us
    psum x1, blocking collectives, on_device(): grad_kv = lax.psum(grad_kv_part, ('row', 'col')).astype(jnp.bfloat16)  436 us
    dot_general x16, matrix products, one_head(): jnp.einsum('qd,kd->qk', grad_head, values_part, preferred_element_type=jn...  347 us
    convert_element_type x16, other arithmetic, one_head(): grad_scores = (weights * (grad_weights - row_dot)).astype(jnp.bfloat16)  275 us
    all_gather x2, waiting for transfers between devices, row_product(): weight_full = lax.all_gather(weight_block, 'row', axis=0, tiled=True)  217 us
  transfers between devices with their start and end apart: 23, of which 20 were waited for; matrix products, arithmetic and copies ran while one was open for 5% of the time, Pallas kernels for 0%

commit v1 on v0

v1 whole, which is shorter than its diff:
```python
import functools
import math

import jax
import jax.numpy as jnp
from jax import lax
from jax.experimental import pallas as pl
from jax.experimental.pallas import tpu as pltpu
from jax.sharding import PartitionSpec as P

HD = 128
TREE_TOK = 5120
TRUNK = 2048
EPSILON = 1e-05
SCALE = HD**-0.5
SCALE2 = SCALE * math.log2(math.e)
NEG = -1e30
TILE = 512
BF = jnp.bfloat16
F32 = jnp.float32
VMEM_BYTES = 60 * 1024 * 1024


def dot(a, b, out=F32):
    return jnp.dot(a, b, preferred_element_type=F32).astype(out)


def dot_t(a, b, out=F32):
    return lax.dot_general(a, b, (((1,), (1,)), ((), ())), preferred_element_type=F32).astype(out)


def dot_0(a, b, out=F32):
    return lax.dot_general(a, b, (((0,), (0,)), ((), ())), preferred_element_type=F32).astype(out)


def tail_rows(tab, i):
    return pl.ds(pl.multiple_of(tab[2, i], 128), TILE // 2), pl.ds(
        pl.multiple_of(tab[4, i], 128), TILE // 2
    )


def fwd_kernel(tab, q_ref, k_ref, v_ref, o_ref, lse_ref, *, bs, heads, hg):
    i = pl.program_id(0)
    full, base = tab[0, i], tab[1, i]
    lim0, lim1 = tab[3, i], tab[5, i]
    half = TILE // 2
    r0, r1 = tail_rows(tab, i)
    row = lax.broadcasted_iota(jnp.int32, (hg * bs, TILE), 0) & (bs - 1)
    col = lax.broadcasted_iota(jnp.int32, (hg * bs, TILE), 1)
    mask = col <= row + jnp.where(col < half, lim0, lim1 + half)
    for g in range(heads // hg):
        cols = [slice((g * hg + h) * HD, (g * hg + h + 1) * HD) for h in range(hg)]
        q = jnp.concatenate([q_ref[:, c] for c in cols], axis=0)
        kt = jnp.concatenate([k_ref[r0, :], k_ref[r1, :]], axis=0)
        vt = jnp.concatenate([v_ref[r0, :], v_ref[r1, :]], axis=0)
        s = jnp.where(mask, dot_t(q, kt) * SCALE2, NEG)
        top = jnp.max(s, axis=1, keepdims=True)
        acc = dot(jnp.exp2(s - top).astype(BF), vt)

        def body(t, carry):
            top, acc = carry
            rr = pl.ds(pl.multiple_of(base + t * TILE, 128), TILE)
            s = dot_t(q, k_ref[rr, :]) * SCALE2
            new = jnp.maximum(top, jnp.max(s, axis=1, keepdims=True))
            p = jnp.exp2(s - new).astype(BF)
            return new, acc * jnp.exp2(top - new) + dot(p, v_ref[rr, :])

        top, acc = lax.fori_loop(0, full, body, (top, acc))
        total = acc[:, HD:]
        out = (acc[:, :HD] / total).astype(BF)
        lse = top + jnp.log2(total)
        for h in range(hg):
            o_ref[:, cols[h]] = out[h * bs : (h + 1) * bs]
            lse_ref[0, g * hg + h : g * hg + h + 1, :] = jnp.transpose(lse[h * bs : (h + 1) * bs])[0:1, :]


def attention_forward(tab, q, k, v_ext, blocks):
    tokens, width = q.shape
    bs, heads = tokens // blocks, width // HD
    return pl.pallas_call(
        functools.partial(fwd_kernel, bs=bs, heads=heads, hg=heads),
        grid_spec=pltpu.PrefetchScalarGridSpec(
            num_scalar_prefetch=1,
            grid=(blocks,),
            in_specs=[
                pl.BlockSpec((bs, width), lambda i, t: (i, 0)),
                pl.BlockSpec(k.shape, lambda i, t: (0, 0)),
                pl.BlockSpec(v_ext.shape, lambda i, t: (0, 0)),
            ],
            out_specs=[
                pl.BlockSpec((bs, width), lambda i, t: (i, 0)),
                pl.BlockSpec((1, heads, bs), lambda i, t: (i, 0, 0)),
            ],
        ),
        out_shape=[
            jax.ShapeDtypeStruct((tokens, width), BF),
            jax.ShapeDtypeStruct((blocks, heads, bs), F32),
        ],
        compiler_params=pltpu.CompilerParams(vmem_limit_bytes=VMEM_BYTES),
        cost_estimate=pl.CostEstimate(
            flops=int(4 * tokens * heads * 2304 * 2 * HD), bytes_accessed=10_000_000, transcendentals=tokens * heads * 2304
        ),
        name="attn_fwd",
    )(tab, q, k, v_ext)


def bwd_kernel(tab, q_ref, da_ref, a_ref, lse_ref, k_ref, v_ref, dq_ref, dkv_ref, *, bs, heads, hg):
    i = pl.program_id(0)
    full, base = tab[0, i], tab[1, i]
    lim0, lim1 = tab[3, i], tab[5, i]
    half = TILE // 2
    r0, r1 = tail_rows(tab, i)
    row = lax.broadcasted_iota(jnp.int32, (TILE, hg * bs), 1) & (bs - 1)
    col = lax.broadcasted_iota(jnp.int32, (TILE, hg * bs), 0)
    mask = col <= row + jnp.where(col < half, lim0, lim1 + half)

    @pl.when(i == 0)
    def _():
        dkv_ref[...] = jnp.zeros_like(dkv_ref)

    for g in range(heads // hg):
        cols = [slice((g * hg + h) * HD, (g * hg + h + 1) * HD) for h in range(hg)]
        q = jnp.concatenate([q_ref[:, c] for c in cols], axis=0)
        da = jnp.concatenate([da_ref[:, c] for c in cols], axis=0)
        lse = jnp.concatenate([lse_ref[0, g * hg + h : g * hg + h + 1, :] for h in range(hg)], axis=1)
        delta = jnp.concatenate(
            [
                jnp.sum(
                    jnp.transpose(da_ref[:, c].astype(F32) * a_ref[:, c].astype(F32)), axis=0, keepdims=True
                )
                for c in cols
            ],
            axis=1,
        )

        def tile(kt, vt, visible):
            st = dot_t(kt, q) * SCALE2 - lse
            if visible is not None:
                st = jnp.where(visible, st, NEG)
            pt = jnp.exp2(st)
            dst = (pt * (dot_t(vt, da) - delta)).astype(BF)
            return dot(dst, q) * SCALE, dot(pt.astype(BF), da), dot_0(dst, kt)

        kt = jnp.concatenate([k_ref[r0, :], k_ref[r1, :]], axis=0)
        vt = jnp.concatenate([v_ref[r0, :], v_ref[r1, :]], axis=0)
        dk, dv, dq = tile(kt, vt, mask)
        dkv_ref[r0, :HD] += dk[:half]
        dkv_ref[r0, HD:] += dv[:half]
        dkv_ref[r1, :HD] += dk[half:]
        dkv_ref[r1, HD:] += dv[half:]

        def body(t, dq):
            rr = pl.ds(pl.multiple_of(base + t * TILE, 128), TILE)
            dk, dv, more = tile(k_ref[rr, :], v_ref[rr, :], None)
            dkv_ref[rr, :HD] += dk
            dkv_ref[rr, HD:] += dv
            return dq + more

        dq = (lax.fori_loop(0, full, body, dq) * SCALE).astype(BF)
        for h in range(hg):
            dq_ref[:, cols[h]] = dq[h * bs : (h + 1) * bs]


def attention_backward(tab, q, da, a, lse, k, v, blocks):
    tokens, width = q.shape
    bs, heads = tokens // blocks, width // HD
    qs = pl.BlockSpec((bs, width), lambda i, t: (i, 0))
    ks = pl.BlockSpec(k.shape, lambda i, t: (0, 0))
    return pl.pallas_call(
        functools.partial(bwd_kernel, bs=bs, heads=heads, hg=heads),
        grid_spec=pltpu.PrefetchScalarGridSpec(
            num_scalar_prefetch=1,
            grid=(blocks,),
            in_specs=[qs, qs, qs, pl.BlockSpec((1, heads, bs), lambda i, t: (i, 0, 0)), ks, ks],
            out_specs=[qs, pl.BlockSpec((k.shape[0], 2 * HD), lambda i, t: (0, 0))],
        ),
        out_shape=[
            jax.ShapeDtypeStruct((tokens, width), BF),
            jax.ShapeDtypeStruct((k.shape[0], 2 * HD), F32),
        ],
        compiler_params=pltpu.CompilerParams(vmem_limit_bytes=VMEM_BYTES),
        cost_estimate=pl.CostEstimate(
            flops=int(10 * tokens * heads * 2304 * 2 * HD), bytes_accessed=20_000_000, transcendentals=tokens * heads * 2304
        ),
        name="attn_bwd",
    )(tab, q, da, a, lse, k, v)


def block_table(parent, start, places):
    slots = jnp.arange(parent.shape[0], dtype=jnp.int32)
    length = jnp.where(parent < 0, TRUNK, TILE // 2)
    mine = (places[:, None] >= start[None, :]) & (places[:, None] < (start + length)[None, :])
    pick = lambda sel, vals: jnp.sum(jnp.where(sel, vals[None, :], 0), axis=1)
    seg = pick(mine, slots)
    own = pick(mine, start)
    par = pick(mine, parent)
    is_par = slots[None, :] == par[:, None]
    par_start = pick(is_par, start)
    grand = jnp.where(par < 0, -1, pick(is_par, parent))
    trunk = jnp.sum(jnp.where(parent < 0, start, 0))
    off = places - own
    in_trunk, leaf = par < 0, grand >= 0
    full = jnp.where(in_trunk, off // TILE, TRUNK // TILE)
    half = TILE // 2
    first = jnp.where(in_trunk, trunk + full * TILE, jnp.where(leaf, par_start, own))
    lim_first = jnp.where(in_trunk, off - full * TILE, jnp.where(leaf, 2 * TILE, off))
    second = jnp.where(in_trunk, trunk + full * TILE + half, own)
    lim_second = jnp.where(in_trunk, off - full * TILE - half, jnp.where(leaf, off, -2 * TILE))
    return jnp.stack([full, jnp.full_like(full, trunk), first, lim_first, second, lim_second]).astype(jnp.int32)


def normalise(x):
    mean = jnp.mean(x, axis=1, keepdims=True)
    cent = x - mean
    inv = lax.rsqrt(jnp.mean(cent * cent, axis=1, keepdims=True) + EPSILON)
    return mean, inv


def norm_back(grad, xhat, inv, gain):
    c = grad * gain
    return inv * (c - jnp.mean(c, axis=1, keepdims=True) - xhat * jnp.mean(c * xhat, axis=1, keepdims=True))


def gelu_both(u):
    k, a = math.sqrt(2 / math.pi), 0.044715
    t = jnp.tanh(k * (u + a * u * u * u))
    return 0.5 * u * (1 + t), 0.5 * (1 + t) + 0.5 * u * (1 - t * t) * (k * (1 + 3 * a * u * u))


def on_device(
    block_input,
    cotangent,
    attn_gain,
    attn_shift,
    query_weight,
    query_bias,
    keyval_weight,
    value_bias,
    output_weight,
    output_bias,
    mlp_gain,
    mlp_shift,
    expand_weight,
    expand_bias,
    shrink_weight,
    shrink_bias,
    seg_parent,
    seg_start,
    seg_length,
):
    rows, cols = lax.axis_size("row"), lax.axis_size("col")
    core, me, z = lax.axis_index("dp"), lax.axis_index("row"), lax.axis_index("col")
    local, feat = block_input.shape
    width = feat * rows
    tokens = local // rows
    bs = math.gcd(tokens, 128)
    blocks = tokens // bs
    ev = query_weight.shape[1]
    ff = expand_weight.shape[1]
    eh, fh = ev // 2, ff // 2
    swap = lambda x: lax.ppermute(x, "dp", [(0, 1), (1, 0)])
    z_one = lambda x: lax.ppermute(x, "col", [(i, i ^ 1) for i in range(cols)])
    z_two = lambda x: lax.ppermute(x, "col", [(i, i ^ 2) for i in range(cols)])

    def to_rows(x):
        x = x.reshape(blocks, rows, bs, feat).transpose(1, 0, 2, 3).reshape(local, feat)
        return lax.all_to_all(x, "row", split_axis=0, concat_axis=1, tiled=True)

    def from_rows(x):
        x = lax.all_to_all(x, "row", split_axis=1, concat_axis=0, tiled=True)
        return x.reshape(rows, blocks, bs, feat).transpose(1, 0, 2, 3).reshape(local, feat)

    def by_core(own, other, axis):
        return jnp.where(
            core == 0, jnp.concatenate([own, other], axis), jnp.concatenate([other, own], axis)
        )

    vectors = jnp.stack([attn_gain, attn_shift, output_bias, mlp_gain, mlp_shift, shrink_bias])
    vectors = lax.all_gather(vectors, "row", axis=1, tiled=True).astype(F32)
    gain_one, shift_one, out_bias, gain_two, shift_two, down_bias = (vectors[i : i + 1] for i in range(6))
    q_bias = lax.all_gather(query_bias, "col", axis=0, tiled=True).astype(F32).reshape(cols, 2, eh)
    half_of = lambda x, c, size, axis: lax.dynamic_slice_in_dim(x, c * size, size, axis)
    q_bias = jnp.concatenate(
        [lax.dynamic_index_in_dim(q_bias, c, 1, False).reshape(1, cols * eh) for c in (core, 1 - core)], axis=1
    )
    up_bias = half_of(expand_bias, core, fh, 0)
    up_bias = [up_bias.astype(F32)[None], z_two(up_bias).astype(F32)[None]]

    x = to_rows(block_input).astype(F32)
    kv_weight = lax.all_gather(keyval_weight, "row", axis=0, tiled=True)

    def gather_square(block):
        own = lax.all_gather(block, ("row", "col"), axis=0, tiled=False)
        own = own.reshape(rows, cols, feat, eh).transpose(0, 2, 1, 3).reshape(width, cols * eh)
        return jnp.concatenate([own, swap(own)], axis=1)

    wq = gather_square(half_of(query_weight, core, eh, 1))
    wo_t = gather_square(half_of(output_weight, core, eh, 0).T)

    mean_one, inv_one = normalise(x)
    normed = ((x - mean_one) * inv_one * gain_one + shift_one).astype(BF)
    kv_shift = jnp.concatenate([jnp.zeros((HD,), F32), value_bias.astype(F32)])[None]
    kv = (dot(normed, kv_weight) + kv_shift).astype(BF)
    kv_other = z_one(kv)
    odd = z % 2
    kv_pair = jnp.where(odd == 0, jnp.stack([kv, kv_other]), jnp.stack([kv_other, kv]))
    kv_all = lax.all_gather(kv_pair, "row", axis=0, tiled=False)
    kv_all = kv_all.reshape(rows, 2, blocks, bs, 2 * HD).transpose(1, 2, 0, 3, 4).reshape(2 * local, 2 * HD)
    keys, values = kv_all[:, :HD], kv_all[:, HD:]
    q = (dot(normed, wq) + q_bias).astype(BF)

    up = half_of(expand_weight, core, fh, 1)
    down_t = half_of(shrink_weight, core, fh, 0).T
    gather_rows = lambda w: lax.all_gather(w, "row", axis=0, tiled=True)
    up_w = [gather_rows(up), gather_rows(z_two(up))]
    down_w = [gather_rows(down_t), gather_rows(z_two(down_t))]

    dy = to_rows(cotangent)

    def quad(x):
        far = z_one(x)
        return jnp.concatenate([x, swap(x)]), jnp.concatenate([far, swap(far)])

    dy_all = quad(dy)

    tree = z // 2
    tree_row = lambda t: lax.dynamic_index_in_dim(t, tree, 0, False)
    places = odd * local + (jnp.arange(blocks, dtype=jnp.int32) * rows + me) * bs
    tab = block_table(tree_row(seg_parent), tree_row(seg_start), places)
    v_ext = jnp.concatenate([values, jnp.ones_like(values)], axis=1)
    att, lse = attention_forward(tab, q, keys, v_ext, blocks)
    mid = x + dot_t(att, wo_t) + out_bias

    mean_two, inv_two = normalise(mid)
    xhat_two = (mid - mean_two) * inv_two
    normed_two = (xhat_two * gain_two + shift_two).astype(BF)
    n2 = quad(normed_two)
    act, slope = [[None] * 2, [None] * 2], [[None] * 2, [None] * 2]
    for a in range(2):
        for c in range(2):
            g, s = gelu_both(dot(n2[a], up_w[c]) + up_bias[c])
            act[a][c], slope[a][c] = g.astype(BF), s.astype(BF)

    def reduce_quad(near, far):
        far_got = swap(far[tokens:].astype(BF))
        far_sum = z_one((far[:tokens] + far_got.astype(F32)).astype(BF))
        near_got = swap(near[tokens:].astype(BF))
        return near[:tokens] + near_got.astype(F32) + far_sum.astype(F32)

    dpre = [[None] * 2, [None] * 2]
    for a in range(2):
        for c in range(2):
            dpre[a][c] = (dot(dy_all[a], down_w[c]) * slope[a][c].astype(F32)).astype(BF)
    dn2 = reduce_quad(*[dot_t(dpre[a][0], up_w[0]) + dot_t(dpre[a][1], up_w[1]) for a in (0, 1)])

    branch = reduce_quad(*[dot_t(act[a][0], down_w[0]) + dot_t(act[a][1], down_w[1]) for a in (0, 1)])
    block_output = from_rows((mid + branch + down_bias).astype(BF))

    scatter_rows = lambda w: lax.psum_scatter(w, "row", scatter_dimension=0, tiled=True)

    def hidden_grads(left, right):
        part = [
            scatter_rows((dot_0(left[0], right[0][c]) + dot_0(left[1], right[1][c])).astype(BF)) for c in (1, 0)
        ]
        return (part[1].astype(F32) + z_two(part[0]).astype(F32)).astype(BF)

    d_down = hidden_grads(dy_all, act)
    d_up = hidden_grads(n2, dpre)
    expand_weight_grad = by_core(d_up, swap(d_up), 1).astype(F32)
    shrink_weight_grad = by_core(d_down.T, swap(d_down.T), 0).astype(F32)

    dmid = dy.astype(F32) + norm_back(dn2, xhat_two, inv_two, gain_two)
    dmid_low = dmid.astype(BF)
    datt = dot(dmid_low, wo_t, BF)
    dq, dkv_part = attention_backward(tab, q, datt, att, lse, keys, values, blocks)

    def square_grad(left, right):
        mine, other = right[:, : cols * eh], right[:, cols * eh :]
        got = swap(dot_0(left, other, BF))
        full = scatter_rows((dot_0(left, mine) + got.astype(F32)).astype(BF))
        full = full.reshape(feat, cols, eh).transpose(1, 0, 2)
        return lax.psum_scatter(full, "col", scatter_dimension=0, tiled=False)

    d_out = square_grad(dmid_low, att)
    output_weight_grad = by_core(d_out.T, swap(d_out.T), 0).astype(F32)
    dkv_half = dkv_part.reshape(2, local, 2 * HD).astype(BF)
    dkv_got = z_one(lax.dynamic_index_in_dim(dkv_half, 1 - odd, 0, False))
    dkv_sum = half_of(dkv_part, odd, local, 0) + dkv_got.astype(F32)
    dkv_sum = dkv_sum.astype(BF).reshape(blocks, rows, bs, 2 * HD).transpose(1, 0, 2, 3).reshape(local, 2 * HD)
    dkv = scatter_rows(dkv_sum)
    d_query = square_grad(normed, dq)
    query_weight_grad = by_core(d_query, swap(d_query), 1).astype(F32)

    dn1 = dot_t(dq, wq) + dot_t(dkv, kv_weight)
    xhat_one = (x - mean_one) * inv_one
    input_grad = from_rows((dmid + norm_back(dn1, xhat_one, inv_one, gain_one)).astype(BF)).astype(F32)
    d_kv_weight = scatter_rows(dot_0(normed, dkv, BF))
    keyval_weight_grad = lax.psum(d_kv_weight, ("dp", "col")).astype(F32)

    everyone = ("dp", "row", "col")
    total = lambda t: jnp.sum(t.astype(F32), axis=0)
    bias_up = jnp.zeros((cols, 2, fh), F32)
    for c, where in ((0, z), (1, z ^ 2)):
        bias_up = lax.dynamic_update_slice(
            bias_up, (total(dpre[0][c]) + total(dpre[1][c]))[None, None], (where, core, 0)
        )
    early = jnp.concatenate(
        [total(dn2 * xhat_two), total(dn2), total(dmid_low), total(dy), bias_up.reshape(-1)]
    )
    early = lax.psum(early, everyone)
    dq_sum = total(dq).reshape(2, cols, eh)
    dq_sum = jnp.where(core == 0, dq_sum, dq_sum[::-1]).transpose(1, 0, 2).reshape(-1)
    late = jnp.concatenate([total(dn1 * xhat_one), total(dn1), dq_sum, total(dkv[:, HD:])])
    late = lax.psum(late, everyone)
    row_part = lambda v, n: half_of(v[n * width : (n + 1) * width], me, feat, 0)
    return (
        block_output,
        input_grad,
        row_part(late, 0),
        row_part(late, 1),
        query_weight_grad,
        half_of(late[2 * width : 3 * width], z, ev, 0),
        keyval_weight_grad,
        late[3 * width :],
        output_weight_grad,
        row_part(early, 2),
        row_part(early, 0),
        row_part(early, 1),
        expand_weight_grad,
        half_of(early[4 * width :], z, ff, 0),
        shrink_weight_grad,
        row_part(early, 3),
    )


def solution(mesh):
    tokens, row, col = P(("dp", "col"), "row"), P("row"), P("col")
    tree = P("dp", None)
    return jax.shard_map(
        on_device,
        mesh=mesh,
        in_specs=(
            tokens, tokens, row, row, P("row", "col"), col, P("row", None), P(), P("col", "row"), row,
            row, row, P("row", "col"), col, P("col", "row"), row, tree, tree, tree,
        ),
        out_specs=(
            tokens, tokens, row, row, P("row", "col"), col, P("row", None), P(), P("col", "row"), row,
            row, row, P("row", "col"), col, P("col", "row"), row,
        ),
        check_vma=False,
    )
```

time: 6130 us -> 1690 us (0.28)
  waiting for transfers between devices: 2820 us -> 688 us
  matrix products: 1810 us -> 326 us
  other arithmetic: 712 us -> 80.3 us
  blocking collectives: 522 us -> 230 us
  Pallas kernels: 0 us -> 162 us
  local copies, waits for them, and re-layouts: 194 us -> 123 us
    all_gather x12 -> x8, waiting for transfers between devices: 1860 us -> 0.03 us  [the longest x4 0.02 us: on_device(): gather_rows = lambda w: lax.all_gather(w, 'row', axis=0, tiled=True)]
    dot_general x143 -> x35, matrix products: 1810 us -> 326 us  [the longest x11 113 us: dot(): return jnp.dot(a, b, preferred_element_type=F32).astype(out)]
    psum x7 -> x1, blocking collectives: 522 us -> 41.1 us  [on_device(): late = lax.psum(late, everyone)]
    reduce_scatter x4 -> x10, waiting for transfers between devices: 657 us -> 251 us  [the longest x8 217 us: on_device(): lax.psum_scatter(w, 'row', scatter_dimension=0, tiled=True)]
    convert_element_type x43 -> x16, other arithmetic: 319 us -> 44.1 us  [the longest x2 10.5 us: reduce_quad(): far_sum = z_one((far[:tokens] + far_got.astype(F32)).astype(BF))]
    ppermute x0 -> x27, waiting for transfers between devices: none -> 271 us  [the longest x5 133 us: on_device(): z_two = lambda x: lax.ppermute(x, 'col', [(i, i ^ 2) for i in range(cols)])]
    reduce_sum x25 -> x11, other arithmetic: 232 us -> 30.1 us  [the longest x5 21.8 us: on_device(): total = lambda t: jnp.sum(t.astype(F32), axis=0)]
    pallas_call x0 -> x2, Pallas kernels: none -> 162 us  [the longest x1 89.7 us: attention_backward(): pl.pallas_call(functools.partial(bwd_kernel, bs=bs, heads=heads, hg=heads...]
  transfers between devices with their start and end apart: 23 -> 50, of which waited for: 20 -> 17; matrix products, arithmetic and copies ran while one was open for 5% -> 29% of each run, Pallas kernels for 0% -> 4%
where the time goes in v1:
time: 1690 us; the launch traced here: 1680 us
  waiting for transfers between devices  688 us (41%)
  matrix products  326 us (19%)
  blocking collectives  230 us (14%)
  Pallas kernels  162 us (10%)
  local copies, waits for them, and re-layouts  123 us (7%)
  other arithmetic  80.3 us (5%)
  starting transfers between devices  57.5 us (3%)
    reduce_scatter x8, waiting for transfers between devices, on_device(): lax.psum_scatter(w, 'row', scatter_dimension=0, tiled=True)  217 us
    ppermute x5, waiting for transfers between devices, on_device(): z_two = lambda x: lax.ppermute(x, 'col', [(i, i ^ 2) for i in range(cols)])  133 us
    ppermute x6, waiting for transfers between devices, on_device(): z_one = lambda x: lax.ppermute(x, 'col', [(i, i ^ 1) for i in range(cols)])  125 us
    psum x1, waiting for transfers between devices, on_device(): early = lax.psum(early, everyone)  122 us
    dot_general x11, matrix products, dot(): return jnp.dot(a, b, preferred_element_type=F32).astype(out)  113 us
    all_gather x1, blocking collectives, on_device(): lax.all_gather(query_bias, 'col', axis=0, tiled=True).astype(F32)  109 us
    dot_general x11, matrix products, dot_t(): lax.dot_general(a, b, (((1,), (1,)), ((), ())), preferred_element_type=F32)  108 us
    dot_general x13, matrix products, dot_0(): lax.dot_general(a, b, (((0,), (0,)), ((), ())), preferred_element_type=F32)  105 us
  transfers between devices with their start and end apart: 50, of which 17 were waited for; matrix products, arithmetic and copies ran while one was open for 29% of the time, Pallas kernels for 4%

profile of v1, /device:TPU:0, one launch (start us, length us, event | category | flops | bytes accessed | tf_op | source)
XLA Modules:
  0.0 1684.1 jit_solution(17624959018537871322)
XLA Ops:
  18.6 41.6 %all_gather.37 = bf16[6,2048]{1,0:T(8,128)(2,1)S(1)} all-gather(bf16[6,512]{1,0:T(8,128)(2,1)S(1)} %stack.50), channel_id=1, replica_groups=mesh['dp'=2,'row'=4,'col'=4] {'row'}, dimensions={1}, use_global_device_ids=true | all-gather | bytes 30720 | tf_op jit(solution)/shard_map/all_gather | solution.py:279
  92.3 76.1 %collective-permute-done.4 = bf16[512,1024]{1,0:T(8,128)(2,1)S(1)} collective-permute-done((bf16[512,1024]{1,0:T(8,128)(2,1)S(1)}, bf16[512,1024]{1,0:T(8,128)(2,1)S(1)}, u32[]{:S(2)}, u32[]{:S(2)}) %collective-permute-start.4) | collective-permute-done | bytes 1048608 | tf_op jit(solution)/shard_map/ppermute | solution.py:263
  172.0 38.2 %all_to_all.61 = bf16[4,640,512]{2,1,0:T(8,128)(2,1)S(1)} all-to-all(bf16[4,640,512]{2,1,0:T(8,128)(2,1)S(1)} %bitcast.213), channel_id=1, replica_groups=mesh['dp'=2,'row'=4,'col'=4] {'row'}, dimensions={0} | all-to-all | bytes 5242880 | tf_op jit(solution)/shard_map/all_to_all | solution.py:267
  229.2 109.4 %all-gather.2 = bf16[4,1,512]{2,1,0:T(2,128)(2,1)S(1)} all-gather(bf16[1,1,512]{2,1,0:T(2,128)(2,1)S(1)} %reshape.469), channel_id=1, replica_groups=mesh['dp'=2,'row'=4,'col'=4] {'col'}, dimensions={0}, use_global_device_ids=true | all-gather | bytes 5120 | tf_op jit(solution)/shard_map/all_gather | solution.py:281
  389.5 72.3 %attn_fwd.1 = (bf16[640,2048]{1,0:T(8,128)(2,1)}, f32[5,16,128]{2,1,0:T(8,128)}) custom-call(s32[6,5]{1,0:T(8,128)} %stack.43.tab, bf16[640,2048]{1,0:T(8,128)(2,1)} %add_convert_fusion.8.q_ref, bf16[5120,128]{1,0:T(8,128)(2,1)} %get-tuple-element.130.k_ref, bf16[5120,256]{1,0:T(8,128)(2,1)} %concatenate.77.v_ref), custom_call_target="tpu_custom_call" | custom-call | flops 24159191040 | bytes 10000000 | tf_op jit(solution)/shard_map/attn_fwd/pallas_call | solution.py:80
  475.8 56.6 %collective-permute-done.5 = bf16[1024]{0:T(1024)(128)(2,1)S(1)} collective-permute-done((bf16[1024]{0:T(1024)(128)(2,1)S(1)}, bf16[1024]{0:T(1024)(128)(2,1)S(1)}, u32[]{:S(2)}, u32[]{:S(2)}) %collective-permute-start.5) | collective-permute-done | bytes 2080 | tf_op jit(solution)/shard_map/ppermute | solution.py:263
  568.2 14.7 convert_reduce_fusion.4
  582.9 14.1 convert_reduce_fusion.2
  635.6 15.2 convert_reduce_fusion.3
  650.8 13.5 convert_reduce_fusion.1
  747.6 37.7 %collective-permute-done.17 = bf16[640,2048]{1,0:T(8,128)(2,1)} collective-permute-done((bf16[640,2048]{1,0:T(8,128)(2,1)}, bf16[640,2048]{1,0:T(8,128)(2,1)}, u32[]{:S(2)}, u32[]{:S(2)}) %collective-permute-start.17) | collective-permute-done | bytes 2621472 | tf_op jit(solution)/shard_map/ppermute | solution.py:262
  793.2 47.6 %collective-permute-done.11 = bf16[640,2048]{1,0:T(8,128)(2,1)} collective-permute-done((bf16[640,2048]{1,0:T(8,128)(2,1)}, bf16[640,2048]{1,0:T(8,128)(2,1)}, u32[]{:S(2)}, u32[]{:S(2)}) %collective-permute-start.11) | collective-permute-done | bytes 2621472 | tf_op jit(solution)/shard_map/ppermute | solution.py:262
  861.4 89.7 %attn_bwd.1 = (bf16[640,2048]{1,0:T(8,128)(2,1)}, f32[5120,256]{1,0:T(8,128)}) custom-call(s32[6,5]{1,0:T(8,128)} %stack.43.tab, bf16[640,2048]{1,0:T(8,128)(2,1)} %add_convert_fusion.8.q_ref, bf16[640,2048]{1,0:T(8,128)(2,1)} %convolution_convert_fusion.2.da_ref, bf16[640,2048]{1,0:T(8,128)(2,1)} %get-tuple-element.20.a_ref, ...), custom_call_target="tpu_custom_call" | custom-call | flops 60397977600 | bytes 20000000 | tf_op jit(solution)/shard_map/attn_bwd/pallas_call | solution.py:169
  954.1 30.0 %collective-permute-done.18 = bf16[2560,256]{1,0:T(8,128)(2,1)S(1)} collective-permute-done((bf16[2560,256]{1,0:T(8,128)(2,1)S(1)}, bf16[2560,256]{1,0:T(8,128)(2,1)S(1)}, u32[]{:S(2)}, u32[]{:S(2)}) %collective-permute-start.18) | collective-permute-done | bytes 1310752 | tf_op jit(solution)/shard_map/ppermute | solution.py:262
  1125.5 24.9 %collective-permute-start.23 = (bf16[512,1024]{1,0:T(8,128)(2,1)}, bf16[512,1024]{1,0:T(8,128)(2,1)S(1)}, u32[]{:S(2)}, u32[]{:S(2)}) collective-permute-start(bf16[512,1024]{1,0:T(8,128)(2,1)} %reduce-scatter.25.cloned.1.call-done), channel_id=1, source_target_pairs={{0,2},{1,3},{2,0},{3,1},{4,6},{5,7},{6,4},{7,5},{8,10},{9,11},{10,... | collective-permute-start | bytes 3145736 | tf_op jit(solution)/shard_map/ppermute | solution.py:263
  1153.5 51.7 %reduce-scatter.19.cloned.1.call-done = bf16[512,1024]{1,0:T(8,128)(2,1)} async-done(((bf16[2048,1024]{1,0:T(8,128)(2,1)}), bf16[512,1024]{1,0:T(8,128)(2,1)}) %reduce-scatter.19.cloned.1.call-update) | async-done | bytes 1048592 | tf_op jit(solution)/shard_map/reduce_scatter | solution.py:359
  1207.9 13.7 multiply_reduce_fusion.1
  1221.6 40.2 %reduce-scatter.13.cloned.1.call-done = bf16[512,1024]{1,0:T(8,128)(2,1)} async-done(((bf16[2048,1024]{1,0:T(8,128)(2,1)}), bf16[512,1024]{1,0:T(8,128)(2,1)}) %reduce-scatter.13.cloned.1.call-update) | async-done | bytes 1048592 | tf_op jit(solution)/shard_map/reduce_scatter | solution.py:359
  1277.0 67.5 %reduce-scatter.27.cloned.1.call-done = bf16[512,1024]{1,0:T(8,128)(2,1)} async-done(((bf16[2048,1024]{1,0:T(8,128)(2,1)}), bf16[512,1024]{1,0:T(8,128)(2,1)}) %reduce-scatter.27.cloned.1.call-update) | async-done | bytes 1048592 | tf_op jit(solution)/shard_map/reduce_scatter | solution.py:359
  1346.5 53.8 %reduce-scatter.23.cloned.1.call-done = bf16[512,1024]{1,0:T(8,128)(2,1)} async-done(((bf16[2048,1024]{1,0:T(8,128)(2,1)}), bf16[512,1024]{1,0:T(8,128)(2,1)}) %reduce-scatter.23.cloned.1.call-update) | async-done | bytes 1048592 | tf_op jit(solution)/shard_map/reduce_scatter | solution.py:359
  1402.0 121.8 %all-reduce.7.cloned.1.call-done = f32[16384]{0:T(1024)} async-done(((f32[16384]{0:T(1024)}), f32[16384]{0:T(1024)}) %all-reduce.7.cloned.1.call-update) | async-done | bytes 65552 | tf_op jit(solution)/shard_map/psum | solution.py:410
  1532.1 41.1 %psum.21 = f32[6272]{0:T(1024)S(1)} all-reduce(f32[6272]{0:T(1024)S(1)} %pad_maximum_fusion.1), channel_id=1, replica_groups=mesh['dp'=2,'row'=4,'col'=4] {'dp','row','col'}, use_global_device_ids=true, to_apply=%region_18.19 | all-reduce | flops 6272 | bytes 50176 | tf_op jit(solution)/shard_map/psum | solution.py:414
  1586.1 28.7 %reduce-scatter.15.cloned.1.call-done = bf16[1,512,256]{2,1,0:T(8,128)(2,1)} async-done(((bf16[4,512,256]{2,1,0:T(8,128)(2,1)}), bf16[1,512,256]{2,1,0:T(8,128)(2,1)}) %reduce-scatter.15.cloned.1.call-update) | async-done | bytes 262160 | tf_op jit(solution)/shard_map/reduce_scatter | solution.py:382
  1628.5 42.3 %all-reduce.5.cloned.1.call-done = bf16[512,256]{1,0:T(8,128)(2,1)} async-done(((bf16[512,256]{1,0:T(8,128)(2,1)}), bf16[512,256]{1,0:T(8,128)(2,1)}) %all-reduce.5.cloned.1.call-update) | async-done | bytes 262160 | tf_op jit(solution)/shard_map/psum | solution.py:398
  (420 shorter events, 525.5 us)
Async XLA Ops:
  7.9 209.0 %all-gather.24.cloned.1.call-start = ((), (), s32[]{:S(2)}) async-start(), calls=%async_computation.32 | async-start | bytes 4456448 | tf_op jit(solution)/shard_map/all_gather | solution.py:293
  18.4 323.9 %all-gather.14.cloned.1.call-start = ((), (), s32[]{:S(2)}) async-start(), calls=%async_computation.15 | async-start | bytes 3276800 | tf_op jit(solution)/shard_map/all_gather | solution.py:307
  88.4 257.6 %all-gather.26.cloned.1.call-start = ((), (), s32[]{:S(2)}) async-start(), calls=%async_computation.33 | async-start | bytes 4456448 | tf_op jit(solution)/shard_map/all_gather | solution.py:293
  89.2 457.8 %all-gather.20.cloned.1.call-start = ((), (), s32[]{:S(2)}) async-start(), calls=%async_computation.18 | async-start | bytes 5242880 | tf_op jit(solution)/shard_map/all_gather | solution.py:314
  169.4 388.3 %all-gather.16.cloned.1.call-start = ((), (), s32[]{:S(2)}) async-start(), calls=%async_computation.16 | async-start | bytes 5242880 | tf_op jit(solution)/shard_map/all_gather | solution.py:314
  170.0 398.2 %all-gather.18.cloned.1.call-start = ((), (), s32[]{:S(2)}) async-start(), calls=%async_computation.17 | async-start | bytes 5242880 | tf_op jit(solution)/shard_map/all_gather | solution.py:314
  225.6 250.0 %collective-permute-start.6 = (bf16[512,1024]{0,1:T(8,128)(2,1)S(1)}, bf16[512,1024]{0,1:T(8,128)(2,1)}, u32[]{:S(2)}, u32[]{:S(2)}) collective-permute-start(bf16[512,1024]{0,1:T(8,128)(2,1)S(1)} %dynamic-slice_bitcast_fusion.1), channel_id=1, source_target_pairs={{0,2},{1,3},{2,0},{3,1},{4,6},{5,7},{6,4},{7,5},{8,10},{9,11},{10,... | collective-permute-start | bytes 3145736 | tf_op jit(solution)/shard_map/ppermute | solution.py:263
  229.1 353.8 %all-gather.22.cloned.1.call-start = ((), (), s32[]{:S(2)}) async-start(), calls=%async_computation.19 | async-start | bytes 5242880 | tf_op jit(solution)/shard_map/all_gather | solution.py:314
  341.7 197.9 %collective-permute-start.12 = (bf16[640,2048]{1,0:T(8,128)(2,1)}, bf16[640,2048]{1,0:T(8,128)(2,1)}, u32[]{:S(2)}, u32[]{:S(2)}) collective-permute-start(bf16[640,2048]{1,0:T(8,128)(2,1)} %bitcast.76), channel_id=1, source_target_pairs={{0,16},{16,0},{1,17},{17,1},{2,18},{18,2},{3,19},{19,3},{4,20},{20... | collective-permute-start | bytes 7864328 | tf_op jit(solution)/shard_map/ppermute | solution.py:261
  341.8 201.6 %collective-permute-start.15 = (bf16[640,2048]{1,0:T(8,128)(2,1)}, bf16[640,2048]{1,0:T(8,128)(2,1)}, u32[]{:S(2)}, u32[]{:S(2)}) collective-permute-start(bf16[640,2048]{1,0:T(8,128)(2,1)} %collective-permute-done.14), channel_id=1, source_target_pairs={{0,16},{16,0},{1,17},{17,1},{2,18},{18,2},{3,19},{19,3},{4,20},{20... | collective-permute-start | bytes 7864328 | tf_op jit(solution)/shard_map/ppermute | solution.py:261
  475.5 632.1 %reduce-scatter.11.cloned.1.call-start = ((), (), s32[]{:S(2)}) async-start(), calls=%async_computation.20 | async-start | bytes 1638400 | tf_op jit(solution)/shard_map/reduce_scatter | solution.py:359
  1045.9 215.9 %reduce-scatter.13.cloned.1.call-start = ((), (), s32[]{:S(2)}) async-start(), calls=%async_computation.21 | async-start | bytes 5242880 | tf_op jit(solution)/shard_map/reduce_scatter | solution.py:359
  1064.3 280.2 %reduce-scatter.27.cloned.1.call-start = ((), (), s32[]{:S(2)}) async-start(), calls=%async_computation.30 | async-start | bytes 5242880 | tf_op jit(solution)/shard_map/reduce_scatter | solution.py:359
  1084.9 315.4 %reduce-scatter.23.cloned.1.call-start = ((), (), s32[]{:S(2)}) async-start(), calls=%async_computation.28 | async-start | bytes 5242880 | tf_op jit(solution)/shard_map/reduce_scatter | solution.py:359
  1104.4 419.4 %all-reduce.7.cloned.1.call-start = ((), (), s32[]{:S(2)}) async-start(), calls=%async_computation.27 | async-start | bytes 131072 | tf_op jit(solution)/shard_map/psum | solution.py:410
  1107.6 472.5 %reduce-scatter.17.cloned.1.call-start = ((), (), s32[]{:S(2)}) async-start(), calls=%async_computation.23 | async-start | bytes 1310720 | tf_op jit(solution)/shard_map/reduce_scatter | solution.py:359
  1121.9 464.2 %reduce-scatter.21.cloned.1.call-start = ((), (), s32[]{:S(2)}) async-start(), calls=%async_computation.26 | async-start | bytes 1310720 | tf_op jit(solution)/shard_map/reduce_scatter | solution.py:382
  1122.0 222.4 %collective-permute-start.25 = (bf16[512,1024]{1,0:T(8,128)(2,1)}, bf16[512,1024]{1,0:T(8,128)(2,1)}, u32[]{:S(2)}, u32[]{:S(2)}) collective-permute-start(bf16[512,1024]{1,0:T(8,128)(2,1)} %reduce-scatter.29.cloned.1.call-done), channel_id=1, source_target_pairs={{0,2},{1,3},{2,0},{3,1},{4,6},{5,7},{6,4},{7,5},{8,10},{9,11},{10,... | collective-permute-start | bytes 3145736 | tf_op jit(solution)/shard_map/ppermute | solution.py:263
  1125.5 274.8 %collective-permute-start.23 = (bf16[512,1024]{1,0:T(8,128)(2,1)}, bf16[512,1024]{1,0:T(8,128)(2,1)S(1)}, u32[]{:S(2)}, u32[]{:S(2)}) collective-permute-start(bf16[512,1024]{1,0:T(8,128)(2,1)} %reduce-scatter.25.cloned.1.call-done), channel_id=1, source_target_pairs={{0,2},{1,3},{2,0},{3,1},{4,6},{5,7},{6,4},{7,5},{8,10},{9,11},{10,... | collective-permute-start | bytes 3145736 | tf_op jit(solution)/shard_map/ppermute | solution.py:263
  1207.6 407.3 %reduce-scatter.15.cloned.1.call-start = ((), (), s32[]{:S(2)}) async-start(), calls=%async_computation.22 | async-start | bytes 1310720 | tf_op jit(solution)/shard_map/reduce_scatter | solution.py:382
  1272.3 350.6 %all-to-all-start.3 = ((bf16[640,4,512]{2,0,1:T(8,128)(2,1)}), bf16[640,4,512]{2,0,1:T(8,128)(2,1)}, u32[]{:S(2)}, u32[]{:S(2)}) async-start(bf16[640,4,512]{2,0,1:T(8,128)(2,1)} %bitcast.209), calls=%async_computation.4 | async-start | bytes 5242880 | tf_op jit(solution)/shard_map/all_to_all | solution.py:270
  1276.9 393.8 %all-reduce.5.cloned.1.call-start = ((), (), s32[]{:S(2)}) async-start(), calls=%async_computation.24 | async-start | bytes 524288 | tf_op jit(solution)/shard_map/psum | solution.py:398
  1346.4 229.3 %collective-permute-start.26 = (bf16[1024,512]{0,1:T(8,128)(2,1)S(1)}, bf16[1024,512]{0,1:T(8,128)(2,1)}, u32[]{:S(2)}, u32[]{:S(2)}) collective-permute-start(bf16[1024,512]{0,1:T(8,128)(2,1)S(1)} %fusion.50), channel_id=1, source_target_pairs={{0,16},{16,0},{1,17},{17,1},{2,18},{18,2},{3,19},{19,3},{4,20},{20... | collective-permute-start | bytes 3145736 | tf_op jit(solution)/shard_map/ppermute | solution.py:261
  1401.9 212.9 %collective-permute-start.24 = (bf16[512,1024]{1,0:T(8,128)(2,1)S(1)}, bf16[512,1024]{1,0:T(8,128)(2,1)S(1)}, u32[]{:S(2)}, u32[]{:S(2)}) collective-permute-start(bf16[512,1024]{1,0:T(8,128)(2,1)S(1)} %add_convert_fusion.12), channel_id=1, source_target_pairs={{0,16},{16,0},{1,17},{17,1},{2,18},{18,2},{3,19},{19,3},{4,20},{20... | collective-permute-start | bytes 3145736 | tf_op jit(solution)/shard_map/ppermute | solution.py:261
  (104 other events, 4445.4 us)
Sparse Core Ops, SparseCore 0:
  9.9 48.8 all-gather.11
  62.1 109.7 all-gather.23
  174.3 54.4 all-gather.13
  231.4 109.0 all-gather.25
  342.2 51.9 all-gather.19
  396.4 52.6 all-gather.15
  451.6 52.5 all-gather.17
  506.0 52.5 all-gather.21
  987.5 26.4 reduce-scatter.10
  1016.8 52.6 reduce-scatter.28
  1072.8 52.6 reduce-scatter.24
  1128.9 76.3 reduce-scatter.18
  1209.1 52.6 reduce-scatter.12
  1264.6 79.7 reduce-scatter.26
  1347.5 52.6 reduce-scatter.22
  1406.3 117.4 all-reduce.6
  1527.1 28.9 reduce-scatter.16
  1559.0 27.1 reduce-scatter.20
  1589.0 25.7 reduce-scatter.14
  1617.1 53.5 all-reduce.4

commit v2 on v1

v2 whole, which is shorter than its diff:
```python
import functools
import math

import jax
import jax.numpy as jnp
from jax import lax
from jax.experimental import pallas as pl
from jax.experimental.pallas import tpu as pltpu
from jax.sharding import PartitionSpec as P

HD = 128
TREE_TOK = 5120
TRUNK = 2048
EPSILON = 1e-05
SCALE = HD**-0.5
SCALE2 = SCALE * math.log2(math.e)
NEG = -1e30
TILE = 512
BF = jnp.bfloat16
F32 = jnp.float32
VMEM_BYTES = 60 * 1024 * 1024


def dot(a, b, out=F32):
    return jnp.dot(a, b, preferred_element_type=F32).astype(out)


def dot_t(a, b, out=F32):
    return lax.dot_general(a, b, (((1,), (1,)), ((), ())), preferred_element_type=F32).astype(out)


def dot_0(a, b, out=F32):
    return lax.dot_general(a, b, (((0,), (0,)), ((), ())), preferred_element_type=F32).astype(out)


def tail_rows(tab, i):
    return pl.ds(pl.multiple_of(tab[2, i], 128), TILE // 2), pl.ds(
        pl.multiple_of(tab[4, i], 128), TILE // 2
    )


def place_of(head, heads):
    half = heads // 2
    return head // half, slice(head % half * HD, (head % half + 1) * HD)


def fwd_kernel(tab, *refs, bs, heads, hg):
    qa_ref, qb_ref, k_ref, v_ref = refs[:4]
    oa_ref, ob_ref, lse_ref = refs[-3:]
    i = pl.program_id(0)
    full, base = tab[0, i], tab[1, i]
    lim0, lim1 = tab[3, i], tab[5, i]
    half = TILE // 2
    r0, r1 = tail_rows(tab, i)
    row = lax.broadcasted_iota(jnp.int32, (hg * bs, TILE), 0) & (bs - 1)
    col = lax.broadcasted_iota(jnp.int32, (hg * bs, TILE), 1)
    mask = col <= row + jnp.where(col < half, lim0, lim1 + half)
    for g in range(heads // hg):
        at = [place_of(g * hg + h, heads) for h in range(hg)]
        q = jnp.concatenate([(qa_ref, qb_ref)[w][:, c] for w, c in at], axis=0)
        kt = jnp.concatenate([k_ref[r0, :], k_ref[r1, :]], axis=0)
        vt = jnp.concatenate([v_ref[r0, :], v_ref[r1, :]], axis=0)
        s = jnp.where(mask, dot_t(q, kt) * SCALE2, NEG)
        top = jnp.max(s, axis=1, keepdims=True)
        acc = dot(jnp.exp2(s - top).astype(BF), vt)

        def body(t, carry):
            top, acc = carry
            rr = pl.ds(pl.multiple_of(base + t * TILE, 128), TILE)
            s = dot_t(q, k_ref[rr, :]) * SCALE2
            new = jnp.maximum(top, jnp.max(s, axis=1, keepdims=True))
            p = jnp.exp2(s - new).astype(BF)
            return new, acc * jnp.exp2(top - new) + dot(p, v_ref[rr, :])

        top, acc = lax.fori_loop(0, full, body, (top, acc))
        total = acc[:, HD:]
        out = (acc[:, :HD] / total).astype(BF)
        lse = top + jnp.log2(total)
        for h in range(hg):
            (oa_ref, ob_ref)[at[h][0]][:, at[h][1]] = out[h * bs : (h + 1) * bs]
            lse_ref[0, g * hg + h : g * hg + h + 1, :] = jnp.transpose(lse[h * bs : (h + 1) * bs])[0:1, :]


def attention_forward(tab, q, k, v_ext, blocks, *needs):
    tokens, width = q[0].shape
    bs, heads = tokens // blocks, 2 * width // HD
    qs = pl.BlockSpec((bs, width), lambda i, t: (i, 0))
    return pl.pallas_call(
        functools.partial(fwd_kernel, bs=bs, heads=heads, hg=heads),
        grid_spec=pltpu.PrefetchScalarGridSpec(
            num_scalar_prefetch=1,
            grid=(blocks,),
            in_specs=[
                qs,
                qs,
                pl.BlockSpec(k.shape, lambda i, t: (0, 0)),
                pl.BlockSpec(v_ext.shape, lambda i, t: (0, 0)),
            ]
            + [ANY] * len(needs),
            out_specs=[
                qs,
                qs,
                pl.BlockSpec((1, heads, bs), lambda i, t: (i, 0, 0)),
            ],
        ),
        out_shape=[
            jax.ShapeDtypeStruct((tokens, width), BF),
            jax.ShapeDtypeStruct((tokens, width), BF),
            jax.ShapeDtypeStruct((blocks, heads, bs), F32),
        ],
        compiler_params=pltpu.CompilerParams(vmem_limit_bytes=VMEM_BYTES),
        cost_estimate=SMALL,
        name="attn_fwd",
    )(tab, *q, k, v_ext, *needs)


def bwd_kernel(tab, *refs, bs, heads, hg, more):
    qa_ref, qb_ref, daa_ref, dab_ref, aa_ref, ab_ref, lse_ref, k_ref, v_ref = refs[:9]
    dqa_ref, dqb_ref, dkv_ref = refs[-3:]
    i = pl.program_id(0)
    full, base = tab[0, i], tab[1, i]
    lim0, lim1 = tab[3, i], tab[5, i]
    half = TILE // 2
    r0, r1 = tail_rows(tab, i)
    row = lax.broadcasted_iota(jnp.int32, (TILE, hg * bs), 1) & (bs - 1)
    col = lax.broadcasted_iota(jnp.int32, (TILE, hg * bs), 0)
    mask = col <= row + jnp.where(col < half, lim0, lim1 + half)

    @pl.when(i == 0)
    def _():
        dkv_ref[...] = refs[9][...] if more else jnp.zeros_like(dkv_ref)

    for g in range(heads // hg):
        at = [place_of(g * hg + h, heads) for h in range(hg)]
        q = jnp.concatenate([(qa_ref, qb_ref)[w][:, c] for w, c in at], axis=0)
        da = jnp.concatenate([(daa_ref, dab_ref)[w][:, c] for w, c in at], axis=0)
        lse = jnp.concatenate([lse_ref[0, g * hg + h : g * hg + h + 1, :] for h in range(hg)], axis=1)
        delta = jnp.concatenate(
            [
                jnp.sum(
                    jnp.transpose((daa_ref, dab_ref)[w][:, c].astype(F32) * (aa_ref, ab_ref)[w][:, c].astype(F32)),
                    axis=0,
                    keepdims=True,
                )
                for w, c in at
            ],
            axis=1,
        )

        def tile(kt, vt, visible):
            st = dot_t(kt, q) * SCALE2 - lse
            if visible is not None:
                st = jnp.where(visible, st, NEG)
            pt = jnp.exp2(st)
            dst = (pt * (dot_t(vt, da) - delta)).astype(BF)
            return dot(dst, q) * SCALE, dot(pt.astype(BF), da), dot_0(dst, kt)

        kt = jnp.concatenate([k_ref[r0, :], k_ref[r1, :]], axis=0)
        vt = jnp.concatenate([v_ref[r0, :], v_ref[r1, :]], axis=0)
        dk, dv, dq = tile(kt, vt, mask)
        dkv_ref[r0, :HD] += dk[:half]
        dkv_ref[r0, HD:] += dv[:half]
        dkv_ref[r1, :HD] += dk[half:]
        dkv_ref[r1, HD:] += dv[half:]

        def body(t, dq):
            rr = pl.ds(pl.multiple_of(base + t * TILE, 128), TILE)
            dk, dv, more = tile(k_ref[rr, :], v_ref[rr, :], None)
            dkv_ref[rr, :HD] += dk
            dkv_ref[rr, HD:] += dv
            return dq + more

        dq = (lax.fori_loop(0, full, body, dq) * SCALE).astype(BF)
        for h in range(hg):
            (dqa_ref, dqb_ref)[at[h][0]][:, at[h][1]] = dq[h * bs : (h + 1) * bs]


def attention_backward(tab, q, da, a, lse, k, v, blocks, first, count, so_far, *needs):
    tokens, width = q[0].shape
    bs, heads = tokens // blocks, 2 * width // HD
    qs = pl.BlockSpec((bs, width), lambda i, t: (i + first, 0))
    ks = pl.BlockSpec(k.shape, lambda i, t: (0, 0))
    whole = pl.BlockSpec((k.shape[0], 2 * HD), lambda i, t: (0, 0))
    out = pl.BlockSpec((bs, width), lambda i, t: (i, 0))
    more = [] if so_far is None else [so_far]
    return pl.pallas_call(
        functools.partial(bwd_kernel, bs=bs, heads=heads, hg=heads, more=bool(more)),
        grid_spec=pltpu.PrefetchScalarGridSpec(
            num_scalar_prefetch=1,
            grid=(count,),
            in_specs=[qs] * 6
            + [pl.BlockSpec((1, heads, bs), lambda i, t: (i + first, 0, 0)), ks, ks]
            + [whole] * len(more)
            + [ANY] * len(needs),
            out_specs=[out, out, whole],
        ),
        out_shape=[
            jax.ShapeDtypeStruct((count * bs, width), BF),
            jax.ShapeDtypeStruct((count * bs, width), BF),
            jax.ShapeDtypeStruct((k.shape[0], 2 * HD), F32),
        ],
        compiler_params=pltpu.CompilerParams(vmem_limit_bytes=VMEM_BYTES),
        cost_estimate=SMALL,
        name="attn_bwd",
    )(tab[:, first : first + count], *q, *da, *a, lse, k, v, *more, *needs)


def block_table(parent, start, places):
    slots = jnp.arange(parent.shape[0], dtype=jnp.int32)
    length = jnp.where(parent < 0, TRUNK, TILE // 2)
    mine = (places[:, None] >= start[None, :]) & (places[:, None] < (start + length)[None, :])
    pick = lambda sel, vals: jnp.sum(jnp.where(sel, vals[None, :], 0), axis=1)
    seg = pick(mine, slots)
    own = pick(mine, start)
    par = pick(mine, parent)
    is_par = slots[None, :] == par[:, None]
    par_start = pick(is_par, start)
    grand = jnp.where(par < 0, -1, pick(is_par, parent))
    trunk = jnp.sum(jnp.where(parent < 0, start, 0))
    off = places - own
    in_trunk, leaf = par < 0, grand >= 0
    full = jnp.where(in_trunk, off // TILE, TRUNK // TILE)
    half = TILE // 2
    first = jnp.where(in_trunk, trunk + full * TILE, jnp.where(leaf, par_start, own))
    lim_first = jnp.where(in_trunk, off - full * TILE, jnp.where(leaf, 2 * TILE, off))
    second = jnp.where(in_trunk, trunk + full * TILE + half, own)
    lim_second = jnp.where(in_trunk, off - full * TILE - half, jnp.where(leaf, off, -2 * TILE))
    return jnp.stack([full, jnp.full_like(full, trunk), first, lim_first, second, lim_second]).astype(jnp.int32)


SMALL = pl.CostEstimate(flops=1_000_000, bytes_accessed=1_000_000, transcendentals=0)
ANY = pl.BlockSpec(memory_space=pl.ANY)


def hold(values, *needs):
    values = list(values)
    n, m = len(values), len(needs)
    out = pl.pallas_call(
        lambda *refs: None,
        in_specs=[ANY] * (n + m),
        out_specs=[ANY] * n,
        out_shape=[jax.ShapeDtypeStruct(v.shape, v.dtype) for v in values],
        input_output_aliases={i: i for i in range(n)},
        cost_estimate=SMALL,
        name="hold",
    )(*values, *needs)
    return list(out)


def up_kernel(*refs, half, step):
    xa, xb, ya, yb, w, b = refs[:6]
    g_ref, du_ref = refs[-2:]

    def go(x, y):
        for j in range(0, w.shape[2], step):
            c = slice(j, j + step)
            u = dot(x[...], w[0, :, c]) + b[:, c]
            d = dot(y[...], w[1, :, c])
            g, slope = gelu_both(u)
            g_ref[:, c] = g.astype(BF)
            du_ref[:, c] = (d * slope).astype(BF)

    pl.when(pl.program_id(0) < half)(lambda: go(xa, ya))
    pl.when(pl.program_id(0) >= half)(lambda: go(xb, yb))


def up(x, dy, w, b, *needs):
    tokens, width = x[0].shape
    hidden = w.shape[2]
    tm, half = tokens // 2, 2
    first = pl.BlockSpec((tm, width), lambda i: (jnp.minimum(i, half - 1), 0))
    second = pl.BlockSpec((tm, width), lambda i: (jnp.maximum(i - half, 0), 0))
    return pl.pallas_call(
        functools.partial(up_kernel, half=half, step=512),
        grid=(2 * half,),
        in_specs=[first, second, first, second, pl.BlockSpec(w.shape, lambda i: (0, 0, 0)), pl.BlockSpec((1, hidden), lambda i: (0, 0))]
        + [ANY] * len(needs),
        out_specs=[pl.BlockSpec((tm, hidden), lambda i: (i, 0))] * 2,
        out_shape=[jax.ShapeDtypeStruct((2 * tokens, hidden), BF)] * 2,
        compiler_params=pltpu.CompilerParams(vmem_limit_bytes=VMEM_BYTES),
        cost_estimate=SMALL,
        name="hidden_up",
    )(*x, *dy, w, b, *needs)


def down_kernel(*refs, half, step):
    la, lb, wa, wb = refs[:4]
    own, other = refs[-2:]

    def go(o):
        for j in range(0, o.shape[1], step):
            c = slice(j, j + step)
            o[:, c] = (dot_t(la[...], wa[0, c, :]) + dot_t(lb[...], wb[0, c, :])).astype(o.dtype)

    pl.when(pl.program_id(0) < half)(lambda: go(own))
    pl.when(pl.program_id(0) >= half)(lambda: go(other))


def down(left, weights, which, *needs):
    rows, hidden = left[0].shape
    width = weights[0].shape[1]
    half = 2
    tm = rows // 4
    lefts = pl.BlockSpec((tm, hidden), lambda i: (i, 0))
    ws = pl.BlockSpec((1, width, hidden), lambda i: (which, 0, 0))
    return pl.pallas_call(
        functools.partial(down_kernel, half=half, step=512),
        grid=(2 * half,),
        in_specs=[lefts, lefts, ws, ws] + [ANY] * len(needs),
        out_specs=[
            pl.BlockSpec((tm, width), lambda i: (jnp.minimum(i, half - 1), 0)),
            pl.BlockSpec((tm, width), lambda i: (jnp.maximum(i - half, 0), 0)),
        ],
        out_shape=[jax.ShapeDtypeStruct((rows // 2, width), F32), jax.ShapeDtypeStruct((rows // 2, width), BF)],
        compiler_params=pltpu.CompilerParams(vmem_limit_bytes=VMEM_BYTES),
        cost_estimate=SMALL,
        name="hidden_down",
    )(*left, *weights, *needs)


def grads_kernel(*refs):
    xs, ys, dus, gs, o_ref = refs[:4], refs[4:8], refs[8:10], refs[10:12], refs[-1]

    def go(left, right):
        lhs = jnp.concatenate([r[...] for r in left], axis=0)
        rhs = jnp.concatenate([r[...] for r in right], axis=0)
        o_ref[0] = dot_0(lhs, rhs).astype(BF)

    pl.when(pl.program_id(0) == 0)(lambda: go(xs, dus))
    pl.when(pl.program_id(0) == 1)(lambda: go(ys, gs))


def weight_grads(x, dy, du, g, *needs):
    tokens, width = x[0].shape
    hidden = du[0].shape[1]
    tm = min(256, width)
    last = width // tm - 1
    xs = pl.BlockSpec((tokens, tm), lambda j, i: (0, jnp.where(j == 0, i, last)))
    ys = pl.BlockSpec((tokens, tm), lambda j, i: (0, jnp.where(j == 0, 0, i)))
    rs = pl.BlockSpec((2 * tokens, hidden), lambda j, i: (0, 0))
    return pl.pallas_call(
        grads_kernel,
        grid=(2, width // tm),
        in_specs=[xs] * 4 + [ys] * 4 + [rs] * 4 + [ANY] * len(needs),
        out_specs=pl.BlockSpec((1, tm, hidden), lambda j, i: (j, i, 0)),
        out_shape=jax.ShapeDtypeStruct((2, width, hidden), BF),
        compiler_params=pltpu.CompilerParams(vmem_limit_bytes=VMEM_BYTES),
        cost_estimate=SMALL,
        name="hidden_grads",
    )(*x, *dy, *du, *g, *needs)


def normalise(x):
    mean = jnp.mean(x, axis=1, keepdims=True)
    cent = x - mean
    inv = lax.rsqrt(jnp.mean(cent * cent, axis=1, keepdims=True) + EPSILON)
    return mean, inv


def norm_back(grad, xhat, inv, gain):
    c = grad * gain
    return inv * (c - jnp.mean(c, axis=1, keepdims=True) - xhat * jnp.mean(c * xhat, axis=1, keepdims=True))


def gelu_both(u):
    k, a = math.sqrt(2 / math.pi), 0.044715
    square = u * u
    t = jnp.tanh(u * (k + (k * a) * square))
    h = 0.5 * (1 + t)
    return u * h, h + (0.5 * u) * (1 - t * t) * (k + (3 * k * a) * square)


def on_device(
    block_input,
    cotangent,
    attn_gain,
    attn_shift,
    query_weight,
    query_bias,
    keyval_weight,
    value_bias,
    output_weight,
    output_bias,
    mlp_gain,
    mlp_shift,
    expand_weight,
    expand_bias,
    shrink_weight,
    shrink_bias,
    seg_parent,
    seg_start,
    seg_length,
):
    rows, cols = lax.axis_size("row"), lax.axis_size("col")
    core, me, z = lax.axis_index("dp"), lax.axis_index("row"), lax.axis_index("col")
    local, feat = block_input.shape
    width = feat * rows
    tokens = local // rows
    bs = math.gcd(tokens, 128)
    blocks = tokens // bs
    eh = query_weight.shape[1] // 2
    fh = expand_weight.shape[1] // 2
    order = (0, 2, 1, 3)

    def send(x, axis, bits):
        n = lax.axis_size(axis)
        return lax.ppermute(x, axis, [(i, i ^ bits) for i in range(n)])

    swap = lambda x: send(x, "dp", 1)
    z_one = lambda x: send(x, "col", 1)
    z_two = lambda x: send(x, "col", 2)
    half_of = lambda x, c, size, axis: lax.dynamic_slice_in_dim(x, c * size, size, axis)

    def absolute(parts, index):
        bit = 1
        while bit < len(parts):
            odd = (index & bit) != 0
            parts = [jnp.where(odd, parts[j ^ bit], parts[j]) for j in range(len(parts))]
            bit *= 2
        return parts

    def to_rows(x, needs=(), then=()):
        x = x.reshape(blocks, rows, bs, feat)
        parts = [lax.dynamic_index_in_dim(x, me ^ k, 1, False).reshape(tokens, feat) for k in range(rows)]
        if needs:
            parts = hold(parts, *needs)
        parts = parts[:1] + [send(parts[k], "row", k) for k in range(1, rows)]
        return parts if needs else jnp.concatenate(absolute(parts, me), axis=1)

    def from_rows(x):
        piece = lambda k: half_of(x, me ^ k, feat, 1)
        parts = [piece(0)] + [send(piece(k), "row", k) for k in range(1, rows)]
        parts = [p.reshape(blocks, 1, bs, feat) for p in absolute(parts, me)]
        return jnp.concatenate(parts, axis=1).reshape(local, feat)

    def by_core(own, other, axis):
        return jnp.where(
            core == 0, jnp.concatenate([own, other], axis), jnp.concatenate([other, own], axis)
        )

    x_low = to_rows(block_input)
    x = x_low.astype(F32)

    vectors = jnp.stack([attn_gain, attn_shift, output_bias, mlp_gain, mlp_shift, shrink_bias] + [attn_gain] * 2)
    packed = jnp.concatenate([keyval_weight, vectors.reshape(-1, 2 * HD)], axis=0)
    packed = [packed] + [send(packed, "row", k) for k in range(1, rows)]
    packs = packed[1:]
    packed = jnp.stack(absolute(packed, me))
    up_bias = half_of(expand_bias, core, fh, 0).astype(F32)[None]
    up_bias = [up_bias, z_two(up_bias)]
    kv_weight = packed[:, :feat].reshape(width, 2 * HD)
    vectors = packed[:, feat:].reshape(rows, 8, feat).transpose(1, 0, 2).reshape(8, width).astype(F32)
    gain_one, shift_one, out_bias, gain_two, shift_two, down_bias = (vectors[i : i + 1] for i in range(6))

    gather_rows = lambda w, axis=0: lax.all_gather(w, "row", axis=axis, tiled=True)

    def four(block):
        return [block] + [send(block, "col", k) for k in order[1:]]

    q_bias = jnp.concatenate([jnp.stack(four(query_bias)).reshape(cols, 2, eh)], axis=0).astype(F32)
    q_bias = [lax.dynamic_index_in_dim(q_bias, c, 1, False).reshape(1, cols * eh) for c in (core, 1 - core)]

    def gather_square(four_blocks):
        own = gather_rows(jnp.concatenate(four_blocks, axis=1))
        return own, swap(own)

    query_blocks = four(half_of(query_weight, core, eh, 1))
    out_blocks = four(half_of(output_weight, core, eh, 0).T)
    query_blocks[1:] = hold(query_blocks[1:], x_low, up_bias[1], *packs)
    wq = gather_square(query_blocks)
    dy_parts = to_rows(cotangent, [x_low])

    hidden = jnp.stack([half_of(expand_weight, core, fh, 1), half_of(shrink_weight, core, fh, 0).T])

    hidden_z = z_two(hidden)

    mean_one, inv_one = normalise(x)
    normed = ((x - mean_one) * inv_one * gain_one + shift_one).astype(BF)
    kv_shift = jnp.concatenate([jnp.zeros((HD,), F32), value_bias.astype(F32)])[None]
    kv = (dot(normed, kv_weight) + kv_shift).astype(BF)
    out_blocks[1:] = hold(out_blocks[1:], kv)
    wo_t = gather_square(out_blocks)
    odd = z % 2
    kv_pair = jnp.stack(absolute([kv, z_one(kv)], odd))
    halves = [[kv_pair[:, : tokens // 2]], [kv_pair[:, tokens // 2 :]]]
    bits = [1 << i for i in range(rows.bit_length() - 1)]
    for step in range(len(bits)):
        for h, turn in ((0, bits), (1, bits[::-1])):
            halves[h] = halves[h] + [send(p, "row", turn[step]) for p in halves[h]]
    flip = lambda turn: [sum(turn[b] for b in range(len(bits)) if (i >> b) & 1) for i in range(rows)]
    for h, turn in ((0, bits), (1, bits[::-1])):
        held = flip(turn)
        halves[h] = jnp.stack(absolute([halves[h][held.index(k)] for k in range(rows)], me))
    kv_all = jnp.concatenate(halves, axis=2)
    kv_all = kv_all.reshape(rows, 2, blocks, bs, 2 * HD).transpose(1, 2, 0, 3, 4).reshape(2 * local, 2 * HD)
    keys, values = kv_all[:, :HD], kv_all[:, HD:]
    hidden_near = hold([half_of(expand_weight, core, fh, 1), half_of(shrink_weight, core, fh, 0).T], out_blocks[1])
    hidden_near = gather_rows(jnp.stack(hidden_near), 1)
    q = [(dot(normed, w) + v).astype(BF) for w, v in zip(wq, q_bias)]

    dy = jnp.concatenate(absolute(dy_parts, me), axis=1)
    dy_far = z_one(dy)

    tree = z // 2
    tree_row = lambda t: lax.dynamic_index_in_dim(t, tree, 0, False)
    places = odd * local + (jnp.arange(blocks, dtype=jnp.int32) * rows + me) * bs
    tab = block_table(tree_row(seg_parent), tree_row(seg_start), places)
    v_ext = jnp.concatenate([values, jnp.ones_like(values)], axis=1)
    *att, lse = attention_forward(tab, q, keys, v_ext, blocks, dy)
    (hidden_z,) = hold([hidden_z], att[0])
    hidden_w = [hidden_near, gather_rows(hidden_z, 1)]
    mid = x + dot_t(att[0], wo_t[0]) + dot_t(att[1], wo_t[1]) + out_bias

    mean_two, inv_two = normalise(mid)
    xhat_two = (mid - mean_two) * inv_two
    normed_two = (xhat_two * gain_two + shift_two).astype(BF)
    n2_far = z_one(normed_two)
    n2 = [(normed_two, swap(normed_two)), None]
    dy_all = [(dy, swap(dy)), None]
    act, dpre = [[None] * 2, [None] * 2], [[None] * 2, [None] * 2]
    scatter_rows = lambda w, axis=0: lax.psum_scatter(w, "row", scatter_dimension=axis, tiled=True)
    grads, last = [None] * 2, []
    for c in range(2):
        for a in range(2):
            act[a][c], dpre[a][c] = up(n2[a], dy_all[a], hidden_w[c], up_bias[c], *last)
            last = [dpre[a][c]]
            if n2[1] is None:
                n2_far, dy_far = hold([n2_far, dy_far], dpre[0][0])
                n2[1] = (n2_far, swap(n2_far))
                dy_all[1] = (dy_far, swap(dy_far))
        if c == 1:
            dn2_own, dn2_other = down(dpre[1], hidden_w, 0)
            dn2_far = (dn2_own + swap(dn2_other).astype(F32)).astype(BF)
            dn2_own, dn2_other = down(dpre[0], hidden_w, 0, dn2_own)
            (dn2_far,) = hold([dn2_far], dn2_own)
            last = [dn2_far]
            dn2_far = z_one(dn2_far)
        grads[c] = weight_grads(n2[0] + n2[1], dy_all[0] + dy_all[1], [d[c] for d in dpre], [g[c] for g in act], *last)
        last = [grads[c]]
    d_hidden_near = scatter_rows(grads[0], 1)
    (grads[1],) = hold([grads[1]], d_hidden_near)
    d_hidden_far = scatter_rows(grads[1], 1)
    branch_own, branch_other = down(act[1], hidden_w, 1, grads[1])
    near_own, near_other = down(act[0], hidden_w, 1, branch_own)
    (dn2_far,) = hold([dn2_far], near_own)
    dn2 = dn2_own + swap(dn2_other).astype(F32) + dn2_far.astype(F32)
    (branch_far,) = hold([(branch_own + swap(branch_other).astype(F32)).astype(BF)], dn2_far)
    branch_far = z_one(branch_far)
    branch_near = near_own + swap(near_other).astype(F32)

    dmid = dy.astype(F32) + norm_back(dn2, xhat_two, inv_two, gain_two)
    dmid_low = dmid.astype(BF)
    datt = [dot(dmid_low, w, BF) for w in wo_t]

    def halve(x, axis, mesh_axis, bits):
        parts = jnp.split(x, len(bits), axis=axis)
        got = [send(p, mesh_axis, b) for p, b in zip(parts[1:], bits[1:])]
        return sum((g.astype(F32) for g in got), parts[0].astype(F32)).astype(BF)

    def square_part(left, right):
        other = dot_0(left, right[1], BF)
        return (dot_0(left, right[0]) + swap(other).astype(F32)).astype(BF), other

    d_out = scatter_rows(square_part(dmid_low, att)[0])
    cut = blocks - 1
    *dq_a, dkv_part = attention_backward(tab, q, datt, att, lse, keys, values, blocks, 0, cut, None, d_hidden_far)
    (branch_far,) = hold([branch_far], dq_a[0])
    d_hidden_got = z_two(d_hidden_far)
    *dq_b, dkv_part = attention_backward(tab, q, datt, att, lse, keys, values, blocks, cut, blocks - cut, dkv_part, d_hidden_got)
    dq = [jnp.concatenate([u, v]) for u, v in zip(dq_a, dq_b)]
    d_hidden = d_hidden_near.astype(F32) + d_hidden_got.astype(F32)
    d_hidden = d_hidden.astype(BF)
    d_up, d_down = d_hidden[0], d_hidden[1]
    expand_weight_grad = by_core(d_up, swap(d_up), 1).astype(F32)
    shrink_weight_grad = by_core(d_down.T, swap(d_down.T), 0).astype(F32)

    branch = branch_near + branch_far.astype(F32)
    block_output = from_rows((mid + branch + down_bias).astype(BF))
    d_query, d_query_other = square_part(normed, dq)
    d_query = scatter_rows(d_query)
    parts = dkv_part.astype(BF).reshape(2, blocks, rows, bs, 2 * HD)
    pair = lambda k: lax.dynamic_index_in_dim(parts, odd ^ k, 0, False)
    dkv_sum = pair(0).astype(F32) + z_one(pair(1)).astype(F32)
    dkv_sum = dkv_sum.astype(BF)
    relative = lambda k: lax.dynamic_index_in_dim(dkv_sum, me ^ k, 1, False).reshape(tokens, 2 * HD)
    done = []
    for h, turn in ((0, bits), (1, bits[::-1])):
        cut = slice(h * tokens // 2, (h + 1) * tokens // 2)
        held = [relative(k)[cut] for k in flip(turn[::-1])]
        for step in range(len(bits)):
            n = len(held) // 2
            got = [send(p, "row", turn[::-1][len(bits) - 1 - step]) for p in held[n:]]
            held = [(p.astype(F32) + g.astype(F32)).astype(BF) for p, g in zip(held[:n], got)]
        done.append(held[0])
    dkv = jnp.concatenate(done, axis=0)
    (d_out,) = hold([d_out], dkv)
    d_out = halve(d_out, 1, "col", order)
    output_weight_grad = by_core(d_out.T, swap(d_out.T), 0).astype(F32)
    d_query = halve(d_query, 1, "col", order)
    query_weight_grad = by_core(d_query, swap(d_query), 1).astype(F32)

    (dkv,) = hold([dkv], block_output)
    dn1 = dot_t(dq[0], wq[0]) + dot_t(dq[1], wq[1]) + dot_t(dkv, kv_weight)
    xhat_one = (x - mean_one) * inv_one
    input_grad = (dmid + norm_back(dn1, xhat_one, inv_one, gain_one)).astype(BF)
    (dkv,) = hold([dkv], input_grad)
    input_grad = from_rows(input_grad).astype(F32)

    total = lambda t: jnp.sum(t.astype(F32), axis=0)
    fill = -feat % (2 * HD)
    place = lambda v: jnp.pad(v.reshape(rows, feat), ((0, 0), (0, fill))).reshape(rows, -1, 2 * HD)
    same = lambda v: jnp.broadcast_to(v.reshape(1, -1, 2 * HD), (rows, v.size // (2 * HD), 2 * HD))
    dq_sum = jnp.stack([total(dq[0]), total(dq[1])]).reshape(2, cols, eh)
    dq_sum = absolute([dq_sum[:, order.index(k)] for k in range(cols)], z)
    dq_sum = jnp.stack([jnp.stack(absolute([d[0], d[1]], core)) for d in dq_sum]).reshape(-1)
    up_sums = [total(dpre[0][c]) + total(dpre[1][c]) for c in (0, 1)]
    zero = jnp.zeros_like(up_sums[0])
    up_sums = absolute([up_sums[0], zero, up_sums[1], zero], z)
    up_sums = jnp.stack([jnp.stack(absolute([u, zero], core)) for u in up_sums]).reshape(-1)
    v_sum = jnp.concatenate([total(dkv[:, HD:]), jnp.zeros((HD,), F32)])
    vecs = [place(total(dn1 * xhat_one)), place(total(dn1)), place(total(dn2 * xhat_two)), place(total(dn2)),
            place(total(dmid_low)), place(total(dy)), same(dq_sum), same(up_sums), same(v_sum)]
    sizes = [v.shape[1] for v in vecs]
    pad = -sum(sizes) % 16
    vecs.append(jnp.zeros((rows, pad, 2 * HD), F32))
    packs = [dot_0(normed, dkv, BF).reshape(rows, feat, 2 * HD), jnp.concatenate(vecs, axis=1).astype(BF)]
    add_up = lambda first, others: sum((o.astype(F32) for o in others), first.astype(F32)).astype(BF)
    for i, pack in enumerate(packs):
        held = [lax.dynamic_index_in_dim(pack, me ^ k, 0, False) for k in range(rows)]
        pack = add_up(held[0], [send(held[k], "row", k) for k in range(1, rows)])
        pack = add_up(pack, [swap(pack)])
        packs[i] = add_up(pack, [send(pack, "col", k) for k in range(1, cols)])
    keyval_weight_grad = packs[0].astype(F32)
    pack = packs[1]
    ends, at = [], 0
    for n in sizes:
        ends.append(pack[at : at + n].astype(F32).reshape(-1))
        at += n
    return (
        block_output,
        input_grad,
        ends[0][:feat],
        ends[1][:feat],
        query_weight_grad,
        half_of(ends[6], z, 2 * eh, 0),
        keyval_weight_grad,
        ends[8][:HD],
        output_weight_grad,
        ends[4][:feat],
        ends[2][:feat],
        ends[3][:feat],
        expand_weight_grad,
        half_of(ends[7], z, 2 * fh, 0),
        shrink_weight_grad,
        ends[5][:feat],
    )


def solution(mesh):
    tokens, row, col = P(("dp", "col"), "row"), P("row"), P("col")
    tree = P("dp", None)
    return jax.shard_map(
        on_device,
        mesh=mesh,
        in_specs=(
            tokens, tokens, row, row, P("row", "col"), col, P("row", None), P(), P("col", "row"), row,
            row, row, P("row", "col"), col, P("col", "row"), row, tree, tree, tree,
        ),
        out_specs=(
            tokens, tokens, row, row, P("row", "col"), col, P("row", None), P(), P("col", "row"), row,
            row, row, P("row", "col"), col, P("col", "row"), row,
        ),
        check_vma=False,
    )
```

time: 1690 us -> 1090 us (0.64)
  waiting for transfers between devices: 688 us -> 355 us
  matrix products: 326 us -> 85 us
  blocking collectives: 230 us -> 0 us
  Pallas kernels: 162 us -> 340 us
  starting transfers between devices: 57.5 us -> 121 us
  local copies, waits for them, and re-layouts: 123 us -> 66.1 us
  other arithmetic: 80.3 us -> 103 us
    reduce_scatter x10 -> x4, waiting for transfers between devices: 251 us -> 0.02 us  [on_device(): lax.psum_scatter(w, 'row', scatter_dimension=axis, tiled=True)]
    pallas_call x0 -> x24, Pallas kernels: none -> 211 us  [the longest x4 74.4 us: up(): pl.pallas_call(functools.partial(up_kernel, half=half, step=512), grid=(2...]
    psum x2 -> x0, waiting for transfers between devices: 164 us -> none  [the longest x1 122 us: on_device(): early = lax.psum(early, everyone)]
    all_gather x2 -> x0, blocking collectives: 151 us -> none  [the longest x1 109 us: on_device(): lax.all_gather(query_bias, 'col', axis=0, tiled=True).astype(F32)]
    dot_general x11 -> x5, matrix products: 113 us -> 25.7 us  [dot(): return jnp.dot(a, b, preferred_element_type=F32).astype(out)]
    ppermute x27 -> x81, starting transfers between devices: 41.7 us -> 120 us  [send(): return lax.ppermute(x, axis, [(i, i ^ bits) for i in range(n)])]
    dot_general x11 -> x5, matrix products: 108 us -> 29.8 us  [dot_t(): lax.dot_general(a, b, (((1,), (1,)), ((), ())), preferred_element_type=F32)]
    dot_general x13 -> x5, matrix products: 105 us -> 29.5 us  [dot_0(): lax.dot_general(a, b, (((0,), (0,)), ((), ())), preferred_element_type=F32)]
  transfers between devices with their start and end apart: 50 -> 89, of which waited for: 17 -> 34; matrix products, arithmetic and copies ran while one was open for 29% -> 21% of each run, Pallas kernels for 4% -> 31%
where the time goes in v2:
time: 1090 us
  waiting for transfers between devices  355 us (33%)
  Pallas kernels  340 us (31%)
  starting transfers between devices  121 us (11%)
  other arithmetic  103 us (9%)
  matrix products  85 us (8%)
  local copies, waits for them, and re-layouts  66.1 us (6%)
  between operations  16.1 us (1%)
    ppermute x81, waiting for transfers between devices, send(): return lax.ppermute(x, axis, [(i, i ^ bits) for i in range(n)])  318 us
    ppermute x81, starting transfers between devices, send(): return lax.ppermute(x, axis, [(i, i ^ bits) for i in range(n)])  120 us
    pallas_call x2, Pallas kernels, attention_backward(): pl.pallas_call(functools.partial(bwd_kernel, bs=bs, heads=heads, hg=heads...  76 us
    pallas_call x4, Pallas kernels, up(): pl.pallas_call(functools.partial(up_kernel, half=half, step=512), grid=(2...  74.4 us
    pallas_call x4, Pallas kernels, down(): pl.pallas_call(functools.partial(down_kernel, half=half, step=512), grid=...  71.5 us
    pallas_call x2, Pallas kernels, weight_grads(): pl.pallas_call(grads_kernel, grid=(2, width // tm), in_specs=[xs] * 4 + [...  64.6 us
    pallas_call x1, Pallas kernels, attention_forward(): pl.pallas_call(functools.partial(fwd_kernel, bs=bs, heads=heads, hg=heads...  53.6 us
    all_gather x4, waiting for transfers between devices, on_device(): lax.all_gather(w, 'row', axis=axis, tiled=True)  36.4 us
  transfers between devices with their start and end apart: 89, of which 34 were waited for; matrix products, arithmetic and copies ran while one was open for 21% of the time, Pallas kernels for 31%

profile of v2, /device:TPU:0, one launch (start us, length us, event | category | flops | bytes accessed | tf_op | source)
XLA Modules:
  0.0 1085.5 jit_solution(5218028402501874696)
XLA Ops:
  128.2 23.3 %all-gather.5.cloned.1.call-done = bf16[2048,1024]{1,0:T(8,128)(2,1)} async-done(((bf16[512,1024]{1,0:T(8,128)(2,1)}), bf16[2048,1024]{1,0:T(8,128)(2,1)}) %all-gather.5.cloned.1.call-update) | async-done | bytes 4194320 | tf_op jit(solution)/shard_map/all_gather | solution.py:455
  207.5 53.6 %attn_fwd.1 = (bf16[640,1024]{1,0:T(8,128)(2,1)}, bf16[640,1024]{1,0:T(8,128)(2,1)}, f32[5,16,128]{2,1,0:T(8,128)}) custom-call(s32[6,5]{1,0:T(8,128)} %stack.197.tab, bf16[640,1024]{1,0:T(8,128)(2,1)} %add_convert_fusion.8.refs_0_, bf16[640,1024]{1,0:T(8,128)(2,1)} %add_convert_fusion.7.refs_1_, bf16[5120,128]{1,0:T(8,128)(2,1)} %get-tuple-element.180.refs_2_.refs_7_, ...), custom_call_target="tpu_custom_call" | custom-call | flops 1000000 | bytes 1000000 | tf_op jit(solution)/shard_map/attn_fwd/pallas_call | solution.py:88
  296.3 13.0 %all-gather.9.cloned.1.call-done.refs_4_.refs_2_ = bf16[2,2048,1024]{2,1,0:T(8,128)(2,1)} async-done(((bf16[2,512,1024]{2,1,0:T(8,128)(2,1)}), bf16[2,2048,1024]{2,1,0:T(8,128)(2,1)}) %all-gather.9.cloned.1.call-update) | async-done | bytes 8388624 | tf_op jit(solution)/shard_map/all_gather | solution.py:455
  309.3 18.4 %hidden_up.4 = (bf16[1280,1024]{1,0:T(8,128)(2,1)}, bf16[1280,1024]{1,0:T(8,128)(2,1)}) custom-call(bf16[640,2048]{1,0:T(8,128)(2,1)} %add_convert_fusion.5.refs_0_, bf16[640,2048]{1,0:T(8,128)(2,1)} %collective-permute-done.28.refs_1_, bf16[640,2048]{1,0:T(8,128)(2,1)} %get-tuple-element.142.refs_4_.refs_2_, ...), custom_call_target="tpu_custom_call" | custom-call | flops 1000000 | bytes 1000000 | tf_op jit(solution)/shard_map/hidden_up/pallas_call | solution.py:273
  327.7 26.5 %collective-permute-done.32.refs_1_ = bf16[640,2048]{1,0:T(8,128)(2,1)} collective-permute-done((bf16[640,2048]{1,0:T(8,128)(2,1)}, bf16[640,2048]{1,0:T(8,128)(2,1)}, u32[]{:S(2)}, u32[]{:S(2)}) %collective-permute-start.32) | collective-permute-done | bytes 2621472 | tf_op jit(solution)/shard_map/ppermute | solution.py:407
  354.2 55.9 %collective-permute-done.31.refs_0_ = bf16[640,2048]{1,0:T(8,128)(2,1)} collective-permute-done((bf16[640,2048]{1,0:T(8,128)(2,1)}, bf16[640,2048]{1,0:T(8,128)(2,1)}, u32[]{:S(2)}, u32[]{:S(2)}) %collective-permute-start.31) | collective-permute-done | bytes 2621472 | tf_op jit(solution)/shard_map/ppermute | solution.py:407
  419.1 18.6 %hidden_up.5 = (bf16[1280,1024]{1,0:T(8,128)(2,1)}, bf16[1280,1024]{1,0:T(8,128)(2,1)}) custom-call(bf16[640,2048]{1,0:T(8,128)(2,1)} %get-tuple-element.71.refs_0_.refs_2_, bf16[640,2048]{1,0:T(8,128)(2,1)} %collective-permute-done.33.refs_1_.refs_3_, bf16[640,2048]{1,0:T(8,128)(2,1)} %get-tuple-element.72.refs_2_.refs_6_, ...), custom_call_target="tpu_custom_call" | custom-call | flops 1000000 | bytes 1000000 | tf_op jit(solution)/shard_map/hidden_up/pallas_call | solution.py:273
  437.7 32.1 %hidden_grads.2.refs_6_ = bf16[2,2048,1024]{2,1,0:T(8,128)(2,1)} custom-call(bf16[640,2048]{1,0:T(8,128)(2,1)} %add_convert_fusion.5.refs_0_, bf16[640,2048]{1,0:T(8,128)(2,1)} %collective-permute-done.28.refs_1_, bf16[640,2048]{1,0:T(8,128)(2,1)} %get-tuple-element.71.refs_0_.refs_2_, bf16[640,2048]{1,0:T(8,128)(2,1)} %collective-permute-done.33.refs_1_.refs_3_, ...), custom_call_target="tpu_custom_call" | custom-call | flops 1000000 | bytes 1000000 | tf_op jit(solution)/shard_map/hidden_grads/pallas_call | solution.py:341
  469.9 18.7 %hidden_up.6 = (bf16[1280,1024]{1,0:T(8,128)(2,1)}, bf16[1280,1024]{1,0:T(8,128)(2,1)}) custom-call(bf16[640,2048]{1,0:T(8,128)(2,1)} %add_convert_fusion.5.refs_0_, bf16[640,2048]{1,0:T(8,128)(2,1)} %collective-permute-done.28.refs_1_, bf16[640,2048]{1,0:T(8,128)(2,1)} %get-tuple-element.142.refs_4_.refs_2_, ...), custom_call_target="tpu_custom_call" | custom-call | flops 1000000 | bytes 1000000 | tf_op jit(solution)/shard_map/hidden_up/pallas_call | solution.py:273
  488.6 18.7 %hidden_up.7 = (bf16[1280,1024]{1,0:T(8,128)(2,1)}, bf16[1280,1024]{1,0:T(8,128)(2,1)}) custom-call(bf16[640,2048]{1,0:T(8,128)(2,1)} %get-tuple-element.71.refs_0_.refs_2_, bf16[640,2048]{1,0:T(8,128)(2,1)} %collective-permute-done.33.refs_1_.refs_3_, bf16[640,2048]{1,0:T(8,128)(2,1)} %get-tuple-element.72.refs_2_.refs_6_, ...), custom_call_target="tpu_custom_call" | custom-call | flops 1000000 | bytes 1000000 | tf_op jit(solution)/shard_map/hidden_up/pallas_call | solution.py:273
  507.3 18.4 %hidden_down.4 = (f32[640,2048]{1,0:T(8,128)}, bf16[640,2048]{1,0:T(8,128)(2,1)}) custom-call(bf16[1280,1024]{1,0:T(8,128)(2,1)} %get-tuple-element.73.refs_9_.refs_12_.refs_0_, bf16[1280,1024]{1,0:T(8,128)(2,1)} %get-tuple-element.78.refs_1_.refs_9_, bf16[2,2048,1024]{2,1,0:T(8,128)(2,1)} %all-gather.9.cloned.1.call-done.refs_4_.refs_2_, ...), custom_call_target="tpu_custom_call" | custom-call | flops 1000000 | bytes 1000000 | tf_op jit(solution)/shard_map/hidden_down/pallas_call | solution.py:306
  525.7 17.6 %hidden_down.5 = (f32[640,2048]{1,0:T(8,128)}, bf16[640,2048]{1,0:T(8,128)(2,1)}) custom-call(bf16[1280,1024]{1,0:T(8,128)(2,1)} %get-tuple-element.70.refs_2_.refs_6_.refs_8_.refs_0_, bf16[1280,1024]{1,0:T(8,128)(2,1)} %get-tuple-element.76.refs_6_.refs_1_.refs_8_, bf16[2,2048,1024]{2,1,0:T(8,128)(2,1)} %all-gather.9.cloned.1.call-done.refs_4_.refs_2_, ...), custom_call_target="tpu_custom_call" | custom-call | flops 1000000 | bytes 1000000 | tf_op jit(solution)/shard_map/hidden_down/pallas_call | solution.py:306
  549.4 32.5 %hidden_grads.3.refs_0_ = bf16[2,2048,1024]{2,1,0:T(8,128)(2,1)} custom-call(bf16[640,2048]{1,0:T(8,128)(2,1)} %add_convert_fusion.5.refs_0_, bf16[640,2048]{1,0:T(8,128)(2,1)} %collective-permute-done.28.refs_1_, bf16[640,2048]{1,0:T(8,128)(2,1)} %get-tuple-element.71.refs_0_.refs_2_, bf16[640,2048]{1,0:T(8,128)(2,1)} %collective-permute-done.33.refs_1_.refs_3_, ...), custom_call_target="tpu_custom_call" | custom-call | flops 1000000 | bytes 1000000 | tf_op jit(solution)/shard_map/hidden_grads/pallas_call | solution.py:341
  583.9 17.7 %hidden_down.6 = (f32[640,2048]{1,0:T(8,128)}, bf16[640,2048]{1,0:T(8,128)(2,1)}) custom-call(bf16[1280,1024]{1,0:T(8,128)(2,1)} %get-tuple-element.74.refs_11_.refs_0_, bf16[1280,1024]{1,0:T(8,128)(2,1)} %get-tuple-element.77.refs_11_.refs_1_, bf16[2,2048,1024]{2,1,0:T(8,128)(2,1)} %all-gather.9.cloned.1.call-done.refs_4_.refs_2_, ...), custom_call_target="tpu_custom_call" | custom-call | flops 1000000 | bytes 1000000 | tf_op jit(solution)/shard_map/hidden_down/pallas_call | solution.py:306
  601.9 17.8 %hidden_down.7 = (f32[640,2048]{1,0:T(8,128)}, bf16[640,2048]{1,0:T(8,128)(2,1)}) custom-call(bf16[1280,1024]{1,0:T(8,128)(2,1)} %get-tuple-element.69.refs_10_.refs_0_, bf16[1280,1024]{1,0:T(8,128)(2,1)} %get-tuple-element.75.refs_10_.refs_1_, bf16[2,2048,1024]{2,1,0:T(8,128)(2,1)} %all-gather.9.cloned.1.call-done.refs_4_.refs_2_, ...), custom_call_target="tpu_custom_call" | custom-call | flops 1000000 | bytes 1000000 | tf_op jit(solution)/shard_map/hidden_down/pallas_call | solution.py:306
  619.8 21.8 %collective-permute-done.38.refs_0_ = bf16[640,2048]{1,0:T(8,128)(2,1)} collective-permute-done((bf16[640,2048]{1,0:T(8,128)(2,1)}, bf16[640,2048]{1,0:T(8,128)(2,1)}, u32[]{:S(2)}, u32[]{:S(2)}) %collective-permute-start.38) | collective-permute-done | bytes 2621472 | tf_op jit(solution)/shard_map/ppermute | solution.py:407
  698.2 61.4 %attn_bwd.2 = (bf16[512,1024]{1,0:T(8,128)(2,1)}, bf16[512,1024]{1,0:T(8,128)(2,1)}, f32[5120,256]{1,0:T(8,128)}) custom-call(s32[6,4]{1,0:T(8,128)} %bitcast.321, bf16[640,1024]{1,0:T(8,128)(2,1)} %add_convert_fusion.8.refs_0_, bf16[640,1024]{1,0:T(8,128)(2,1)} %add_convert_fusion.7.refs_1_, bf16[640,1024]{1,0:T(8,128)(2,1)} %convolution_convert_fusion.4.refs_2_, ...), custom_call_target="tpu_custom_call" | custom-call | flops 1000000 | bytes 1000000 | tf_op jit(solution)/shard_map/attn_bwd/pallas_call | solution.py:186
  793.4 19.3 %collective-permute-done.42 = bf16[640,512]{1,0:T(8,128)(2,1)} collective-permute-done((bf16[640,512]{1,0:T(8,128)(2,1)}, bf16[640,512]{1,0:T(8,128)(2,1)}, u32[]{:S(2)}, u32[]{:S(2)}) %collective-permute-start.42) | collective-permute-done | bytes 655392 | tf_op jit(solution)/shard_map/ppermute | solution.py:407
  818.7 14.6 %attn_bwd.3 = (bf16[128,1024]{1,0:T(8,128)(2,1)}, bf16[128,1024]{1,0:T(8,128)(2,1)}, f32[5120,256]{1,0:T(8,128)}) custom-call(s32[6,1]{1,0:T(8,128)} %slice.173.tab, bf16[640,1024]{1,0:T(8,128)(2,1)} %add_convert_fusion.8.refs_0_, bf16[640,1024]{1,0:T(8,128)(2,1)} %add_convert_fusion.7.refs_1_, bf16[640,1024]{1,0:T(8,128)(2,1)} %convolution_convert_fusion.4.refs_2_, ...), custom_call_target="tpu_custom_call" | custom-call | flops 1000000 | bytes 1000000 | tf_op jit(solution)/shard_map/attn_bwd/pallas_call | solution.py:186
  868.6 21.6 %collective-permute-done.45 = bf16[5,4,128,256]{3,2,0,1:T(8,128)(2,1)S(1)} collective-permute-done((bf16[5,4,128,256]{3,2,0,1:T(8,128)(2,1)}, bf16[5,4,128,256]{3,2,0,1:T(8,128)(2,1)S(1)}, u32[]{:S(2)}, u32[]{:S(2)}) %collective-permute-start.45) | collective-permute-done | bytes 1310752 | tf_op jit(solution)/shard_map/ppermute | solution.py:407
  911.0 13.7 %collective-permute-done.50 = bf16[320,256]{1,0:T(8,128)(2,1)S(1)} collective-permute-done((bf16[320,256]{1,0:T(8,128)(2,1)S(1)}, bf16[320,256]{1,0:T(8,128)(2,1)S(1)}, u32[]{:S(2)}, u32[]{:S(2)}) %collective-permute-start.50) | collective-permute-done | bytes 163872 | tf_op jit(solution)/shard_map/ppermute | solution.py:407
  987.4 10.7 collective-permute-done.60
  1032.4 11.4 %collective-permute-done.53 = bf16[640,512]{1,0:T(8,128)(2,1)} collective-permute-done((bf16[640,512]{1,0:T(8,128)(2,1)}, bf16[640,512]{1,0:T(8,128)(2,1)}, u32[]{:S(2)}, u32[]{:S(2)}) %collective-permute-start.53) | collective-permute-done | bytes 655392 | tf_op jit(solution)/shard_map/ppermute | solution.py:407
  1049.7 16.1 %collective-permute-done.63 = bf16[512,256]{0,1:T(8,128)(2,1)S(1)} collective-permute-done((bf16[512,256]{0,1:T(8,128)(2,1)S(1)}, bf16[512,256]{0,1:T(8,128)(2,1)S(1)}, u32[]{:S(2)}, u32[]{:S(2)}) %collective-permute-start.63) | collective-permute-done | bytes 262176 | tf_op jit(solution)/shard_map/ppermute | solution.py:407
  (523 shorter events, 495.9 us)
Async XLA Ops:
  7.2 144.3 %all-gather.5.cloned.1.call-start = ((), (), s32[]{:S(2)}) async-start(), calls=%async_computation.4 | async-start | bytes 5242880 | tf_op jit(solution)/shard_map/all_gather | solution.py:455
  18.2 56.0 %collective-permute-start.5 = (bf16[528,256]{1,0:T(8,128)(2,1)}, bf16[528,256]{1,0:T(8,128)(2,1)S(1)}, u32[]{:S(2)}, u32[]{:S(2)}) collective-permute-start(bf16[528,256]{1,0:T(8,128)(2,1)} %constant_dynamic-update-slice_fusion), channel_id=1, source_target_pairs={{0,4},{4,0},{8,12},{12,8},{1,5},{5,1},{9,13},{13,9},{2,6},{6,2},{1... | collective-permute-start | bytes 811016 | tf_op jit(solution)/shard_map/ppermute | solution.py:407
  20.1 54.1 %collective-permute-start.4 = (bf16[528,256]{1,0:T(8,128)(2,1)}, bf16[528,256]{1,0:T(8,128)(2,1)S(1)}, u32[]{:S(2)}, u32[]{:S(2)}) collective-permute-start(bf16[528,256]{1,0:T(8,128)(2,1)} %constant_dynamic-update-slice_fusion), channel_id=1, source_target_pairs={{0,8},{4,12},{8,0},{12,4},{1,9},{5,13},{9,1},{13,5},{2,10},{6,14},... | collective-permute-start | bytes 811016 | tf_op jit(solution)/shard_map/ppermute | solution.py:407
  77.4 191.1 %all-gather.7.cloned.1.call-start = ((), (), s32[]{:S(2)}) async-start(), calls=%async_computation.5 | async-start | bytes 5242880 | tf_op jit(solution)/shard_map/all_gather | solution.py:455
  104.8 204.4 %all-gather.9.cloned.1.call-start = ((), (), s32[]{:S(2)}) async-start(), calls=%async_computation.6 | async-start | bytes 10485760 | tf_op jit(solution)/shard_map/all_gather | solution.py:455
  114.8 355.1 %all-gather.11.cloned.1.call-start = ((), (), s32[]{:S(2)}) async-start(), calls=%async_computation.7 | async-start | bytes 10485760 | tf_op jit(solution)/shard_map/all_gather | solution.py:455
  151.5 49.8 %collective-permute-start.13 = (bf16[2048,1024]{1,0:T(8,128)(2,1)}, bf16[2048,1024]{1,0:T(8,128)(2,1)}, u32[]{:S(2)}, u32[]{:S(2)}) collective-permute-start(bf16[2048,1024]{1,0:T(8,128)(2,1)} %all-gather.5.cloned.1.call-done), channel_id=1, source_target_pairs={{0,16},{16,0},{1,17},{17,1},{2,18},{18,2},{3,19},{19,3},{4,20},{20... | collective-permute-start | bytes 12582920 | tf_op jit(solution)/shard_map/ppermute | solution.py:407
  177.2 91.2 %collective-permute-start.30 = (bf16[2,512,1024]{2,1,0:T(8,128)(2,1)}, bf16[2,512,1024]{2,1,0:T(8,128)(2,1)}, u32[]{:S(2)}, u32[]{:S(2)}) collective-permute-start(bf16[2,512,1024]{2,1,0:T(8,128)(2,1)} %pad_maximum_fusion.4), channel_id=1, source_target_pairs={{0,2},{1,3},{2,0},{3,1},{4,6},{5,7},{6,4},{7,5},{8,10},{9,11},{10,... | collective-permute-start | bytes 6291464 | tf_op jit(solution)/shard_map/ppermute | solution.py:407
  268.4 313.5 %reduce-scatter.5.cloned.1.call-start = ((), (), s32[]{:S(2)}) async-start(), calls=%async_computation.8 | async-start | bytes 10485760 | tf_op jit(solution)/shard_map/reduce_scatter | solution.py:521
  291.3 62.9 %collective-permute-start.32 = (bf16[640,2048]{1,0:T(8,128)(2,1)}, bf16[640,2048]{1,0:T(8,128)(2,1)}, u32[]{:S(2)}, u32[]{:S(2)}) collective-permute-start(bf16[640,2048]{1,0:T(8,128)(2,1)} %get-tuple-element.142.refs_4_.refs_2_), channel_id=1, source_target_pairs={{0,1},{1,0},{2,3},{3,2},{4,5},{5,4},{6,7},{7,6},{8,9},{9,8},{10,11... | collective-permute-start | bytes 7864328 | tf_op jit(solution)/shard_map/ppermute | solution.py:407
  296.2 113.9 %collective-permute-start.31 = (bf16[640,2048]{1,0:T(8,128)(2,1)}, bf16[640,2048]{1,0:T(8,128)(2,1)}, u32[]{:S(2)}, u32[]{:S(2)}) collective-permute-start(bf16[640,2048]{1,0:T(8,128)(2,1)} %add_convert_fusion.5.refs_0_), channel_id=1, source_target_pairs={{0,1},{1,0},{2,3},{3,2},{4,5},{5,4},{6,7},{7,6},{8,9},{9,8},{10,11... | collective-permute-start | bytes 7864328 | tf_op jit(solution)/shard_map/ppermute | solution.py:407
  469.8 225.8 %reduce-scatter.7.cloned.1.call-start = ((), (), s32[]{:S(2)}) async-start(), calls=%async_computation.9 | async-start | bytes 10485760 | tf_op jit(solution)/shard_map/reduce_scatter | solution.py:521
  581.9 355.9 %reduce-scatter.11.cloned.1.call-start = ((), (), s32[]{:S(2)}) async-start(), calls=%async_computation.11 | async-start | bytes 5242880 | tf_op jit(solution)/shard_map/reduce_scatter | solution.py:521
  582.0 59.6 %collective-permute-start.38 = (bf16[640,2048]{1,0:T(8,128)(2,1)}, bf16[640,2048]{1,0:T(8,128)(2,1)}, u32[]{:S(2)}, u32[]{:S(2)}) collective-permute-start(bf16[640,2048]{1,0:T(8,128)(2,1)} %hold.20.refs_12_), channel_id=1, source_target_pairs={{0,1},{1,0},{2,3},{3,2},{4,5},{5,4},{6,7},{7,6},{8,9},{9,8},{10,11... | collective-permute-start | bytes 7864328 | tf_op jit(solution)/shard_map/ppermute | solution.py:407
  583.7 57.9 %collective-permute-start.40 = (bf16[640,2048]{1,0:T(8,128)(2,1)}, bf16[640,2048]{1,0:T(8,128)(2,1)}, u32[]{:S(2)}, u32[]{:S(2)}) collective-permute-start(bf16[640,2048]{1,0:T(8,128)(2,1)} %get-tuple-element.86), channel_id=1, source_target_pairs={{0,16},{16,0},{1,17},{17,1},{2,18},{18,2},{3,19},{19,3},{4,20},{20... | collective-permute-start | bytes 7864328 | tf_op jit(solution)/shard_map/ppermute | solution.py:407
  601.6 66.0 %collective-permute-start.37 = (bf16[640,2048]{1,0:T(8,128)(2,1)}, bf16[640,2048]{1,0:T(8,128)(2,1)}, u32[]{:S(2)}, u32[]{:S(2)}) collective-permute-start(bf16[640,2048]{1,0:T(8,128)(2,1)} %get-tuple-element.85), channel_id=1, source_target_pairs={{0,16},{16,0},{1,17},{17,1},{2,18},{18,2},{3,19},{19,3},{4,20},{20... | collective-permute-start | bytes 7864328 | tf_op jit(solution)/shard_map/ppermute | solution.py:407
  666.6 101.1 %collective-permute-start.36 = (bf16[640,2048]{1,0:T(8,128)(2,1)}, bf16[640,2048]{1,0:T(8,128)(2,1)}, u32[]{:S(2)}, u32[]{:S(2)}) collective-permute-start(bf16[640,2048]{1,0:T(8,128)(2,1)} %get-tuple-element.84), channel_id=1, source_target_pairs={{0,16},{16,0},{1,17},{17,1},{2,18},{18,2},{3,19},{19,3},{4,20},{20... | collective-permute-start | bytes 7864328 | tf_op jit(solution)/shard_map/ppermute | solution.py:407
  673.4 94.4 %collective-permute-start.39 = (bf16[640,2048]{1,0:T(8,128)(2,1)}, bf16[640,2048]{1,0:T(8,128)(2,1)}, u32[]{:S(2)}, u32[]{:S(2)}) collective-permute-start(bf16[640,2048]{1,0:T(8,128)(2,1)} %hold.23), channel_id=1, source_target_pairs={{0,1},{1,0},{2,3},{3,2},{4,5},{5,4},{6,7},{7,6},{8,9},{9,8},{10,11... | collective-permute-start | bytes 7864328 | tf_op jit(solution)/shard_map/ppermute | solution.py:407
  688.6 338.3 %reduce-scatter.9.cloned.1.call-start = ((), (), s32[]{:S(2)}) async-start(), calls=%async_computation.10 | async-start | bytes 5242880 | tf_op jit(solution)/shard_map/reduce_scatter | solution.py:521
  695.6 121.8 %collective-permute-start.44 = (bf16[2,512,1024]{2,1,0:T(8,128)(2,1)}, bf16[2,512,1024]{2,1,0:T(8,128)(2,1)S(1)}, u32[]{:S(2)}, u32[]{:S(2)}) collective-permute-start(bf16[2,512,1024]{2,1,0:T(8,128)(2,1)} %reduce-scatter.7.cloned.1.call-done.refs_9_), channel_id=1, source_target_pairs={{0,2},{1,3},{2,0},{3,1},{4,6},{5,7},{6,4},{7,5},{8,10},{9,11},{10,... | collective-permute-start | bytes 6291464 | tf_op jit(solution)/shard_map/ppermute | solution.py:407
  842.7 50.3 %collective-permute-start.62 = (bf16[2048,1024]{0,1:T(8,128)(2,1)}, bf16[2048,1024]{0,1:T(8,128)(2,1)}, u32[]{:S(2)}, u32[]{:S(2)}) collective-permute-start(bf16[2048,1024]{0,1:T(8,128)(2,1)} %convolution_convert_fusion.1), channel_id=1, source_target_pairs={{0,16},{16,0},{1,17},{17,1},{2,18},{18,2},{3,19},{19,3},{4,20},{20... | collective-permute-start | bytes 12582920 | tf_op jit(solution)/shard_map/ppermute | solution.py:407
  845.2 81.2 %collective-permute-start.80 = (bf16[1024,512]{0,1:T(8,128)(2,1)}, bf16[1024,512]{0,1:T(8,128)(2,1)}, u32[]{:S(2)}, u32[]{:S(2)}) collective-permute-start(bf16[1024,512]{0,1:T(8,128)(2,1)} %get-tuple-element.189), channel_id=1, source_target_pairs={{0,16},{16,0},{1,17},{17,1},{2,18},{18,2},{3,19},{19,3},{4,20},{20... | collective-permute-start | bytes 3145736 | tf_op jit(solution)/shard_map/ppermute | solution.py:407
  845.7 55.8 %collective-permute-start.79 = (bf16[512,1024]{1,0:T(8,128)(2,1)}, bf16[512,1024]{1,0:T(8,128)(2,1)}, u32[]{:S(2)}, u32[]{:S(2)}) collective-permute-start(bf16[512,1024]{1,0:T(8,128)(2,1)} %get-tuple-element.190), channel_id=1, source_target_pairs={{0,16},{16,0},{1,17},{17,1},{2,18},{18,2},{3,19},{19,3},{4,20},{20... | collective-permute-start | bytes 3145736 | tf_op jit(solution)/shard_map/ppermute | solution.py:407
  1021.7 49.8 %collective-permute-start.73 = (bf16[512,256]{1,0:T(8,128)(2,1)S(1)}, bf16[512,256]{1,0:T(8,128)(2,1)S(1)}, u32[]{:S(2)}, u32[]{:S(2)}) collective-permute-start(bf16[512,256]{1,0:T(8,128)(2,1)S(1)} %add_convert_fusion.11), channel_id=1, source_target_pairs={{0,3},{1,2},{2,1},{3,0},{4,7},{5,6},{6,5},{7,4},{8,11},{9,10},{10,... | collective-permute-start | bytes 786440 | tf_op jit(solution)/shard_map/ppermute | solution.py:407
  (136 other events, 1919.1 us)
Sparse Core Ops, SparseCore 0:
  77.5 74.0 all-gather.4
  154.0 65.7 all-gather.6
  221.6 87.5 all-gather.8
  311.0 87.6 all-gather.10
  470.0 92.1 reduce-scatter.4
  582.0 91.9 reduce-scatter.6
  688.7 57.2 reduce-scatter.10
  900.1 66.0 reduce-scatter.8

commit v3 on v2

--- a/solution.py
+++ b/solution.py
@@ -425,7 +425,7 @@
         if needs:
             parts = hold(parts, *needs)
         parts = parts[:1] + [send(parts[k], "row", k) for k in range(1, rows)]
-        return parts if needs else jnp.concatenate(absolute(parts, me), axis=1)
+        return parts
 
     def from_rows(x):
         piece = lambda k: half_of(x, me ^ k, feat, 1)
@@ -438,7 +438,8 @@
             core == 0, jnp.concatenate([own, other], axis), jnp.concatenate([other, own], axis)
         )
 
-    x_low = to_rows(block_input)
+    x_parts = to_rows(block_input)
+    x_low = jnp.concatenate(absolute(x_parts, me), axis=1)
     x = x_low.astype(F32)
 
     vectors = jnp.stack([attn_gain, attn_shift, output_bias, mlp_gain, mlp_shift, shrink_bias] + [attn_gain] * 2)
@@ -457,7 +458,8 @@
     def four(block):
         return [block] + [send(block, "col", k) for k in order[1:]]
 
-    q_bias = jnp.concatenate([jnp.stack(four(query_bias)).reshape(cols, 2, eh)], axis=0).astype(F32)
+    q_parts = four(query_bias)
+    q_bias = jnp.stack(q_parts).reshape(cols, 2, eh).astype(F32)
     q_bias = [lax.dynamic_index_in_dim(q_bias, c, 1, False).reshape(1, cols * eh) for c in (core, 1 - core)]
 
     def gather_square(four_blocks):
@@ -466,27 +468,31 @@
 
     query_blocks = four(half_of(query_weight, core, eh, 1))
     out_blocks = four(half_of(output_weight, core, eh, 0).T)
-    query_blocks[1:] = hold(query_blocks[1:], x_low, up_bias[1], *packs)
-    wq = gather_square(query_blocks)
+    hidden = jnp.stack([half_of(expand_weight, core, fh, 1), half_of(shrink_weight, core, fh, 0).T])
+    pieces = [z_two(p) for p in jnp.split(hidden, 8, axis=2)]
+    query_blocks[1:] = hold(query_blocks[1:], x_parts[-1], pieces[0])
+    wq_own = gather_rows(jnp.concatenate(query_blocks, axis=1))
     dy_parts = to_rows(cotangent, [x_low])
 
-    hidden = jnp.stack([half_of(expand_weight, core, fh, 1), half_of(shrink_weight, core, fh, 0).T])
-
-    hidden_z = z_two(hidden)
 
     mean_one, inv_one = normalise(x)
     normed = ((x - mean_one) * inv_one * gain_one + shift_one).astype(BF)
     kv_shift = jnp.concatenate([jnp.zeros((HD,), F32), value_bias.astype(F32)])[None]
     kv = (dot(normed, kv_weight) + kv_shift).astype(BF)
-    out_blocks[1:] = hold(out_blocks[1:], kv)
+    out_blocks[1:] = hold(out_blocks[1:], kv, up_bias[1], pieces[1], *q_parts[1:])
     wo_t = gather_square(out_blocks)
     odd = z % 2
     kv_pair = jnp.stack(absolute([kv, z_one(kv)], odd))
-    halves = [[kv_pair[:, : tokens // 2]], [kv_pair[:, tokens // 2 :]]]
+    halves = hold([kv_pair[:, : tokens // 2], kv_pair[:, tokens // 2 :]], pieces[2], dy_parts[-1])
+    halves = [[h] for h in halves]
     bits = [1 << i for i in range(rows.bit_length() - 1)]
     for step in range(len(bits)):
         for h, turn in ((0, bits), (1, bits[::-1])):
             halves[h] = halves[h] + [send(p, "row", turn[step]) for p in halves[h]]
+        if step == 0:
+            n = len(halves[0])
+            both = hold(halves[0] + halves[1], pieces[3], dy_parts[1])
+            halves = [both[:n], both[n:]]
     flip = lambda turn: [sum(turn[b] for b in range(len(bits)) if (i >> b) & 1) for i in range(rows)]
     for h, turn in ((0, bits), (1, bits[::-1])):
         held = flip(turn)
@@ -496,6 +502,8 @@
     keys, values = kv_all[:, :HD], kv_all[:, HD:]
     hidden_near = hold([half_of(expand_weight, core, fh, 1), half_of(shrink_weight, core, fh, 0).T], out_blocks[1])
     hidden_near = gather_rows(jnp.stack(hidden_near), 1)
+    (wq_own,) = hold([wq_own], keys, pieces[4], *dy_parts[2:-1])
+    wq = [wq_own, swap(wq_own)]
     q = [(dot(normed, w) + v).astype(BF) for w, v in zip(wq, q_bias)]
 
     dy = jnp.concatenate(absolute(dy_parts, me), axis=1)
@@ -506,8 +514,9 @@
     places = odd * local + (jnp.arange(blocks, dtype=jnp.int32) * rows + me) * bs
     tab = block_table(tree_row(seg_parent), tree_row(seg_start), places)
     v_ext = jnp.concatenate([values, jnp.ones_like(values)], axis=1)
-    *att, lse = attention_forward(tab, q, keys, v_ext, blocks, dy)
-    (hidden_z,) = hold([hidden_z], att[0])
+    *att, lse = attention_forward(tab, q, keys, v_ext, blocks, dy, pieces[5])
+    *pieces[6:], dy_far = hold(pieces[6:] + [dy_far], att[0])
+    hidden_z = jnp.concatenate(pieces, axis=2)
     hidden_w = [hidden_near, gather_rows(hidden_z, 1)]
     mid = x + dot_t(att[0], wo_t[0]) + dot_t(att[1], wo_t[1]) + out_bias
 
@@ -525,7 +534,7 @@
             act[a][c], dpre[a][c] = up(n2[a], dy_all[a], hidden_w[c], up_bias[c], *last)
             last = [dpre[a][c]]
             if n2[1] is None:
-                n2_far, dy_far = hold([n2_far, dy_far], dpre[0][0])
+                (n2_far,) = hold([n2_far], dpre[0][0])
                 n2[1] = (n2_far, swap(n2_far))
                 dy_all[1] = (dy_far, swap(dy_far))
         if c == 1:
@@ -564,7 +573,6 @@
     d_out = scatter_rows(square_part(dmid_low, att)[0])
     cut = blocks - 1
     *dq_a, dkv_part = attention_backward(tab, q, datt, att, lse, keys, values, blocks, 0, cut, None, d_hidden_far)
-    (branch_far,) = hold([branch_far], dq_a[0])
     d_hidden_got = z_two(d_hidden_far)
     *dq_b, dkv_part = attention_backward(tab, q, datt, att, lse, keys, values, blocks, cut, blocks - cut, dkv_part, d_hidden_got)
     dq = [jnp.concatenate([u, v]) for u, v in zip(dq_a, dq_b)]
@@ -574,6 +582,7 @@
     expand_weight_grad = by_core(d_up, swap(d_up), 1).astype(F32)
     shrink_weight_grad = by_core(d_down.T, swap(d_down.T), 0).astype(F32)
 
+    (branch_far,) = hold([branch_far], dq_b[0])
     branch = branch_near + branch_far.astype(F32)
     block_output = from_rows((mid + branch + down_bias).astype(BF))
     d_query, d_query_other = square_part(normed, dq)
@@ -603,7 +612,14 @@
     dn1 = dot_t(dq[0], wq[0]) + dot_t(dq[1], wq[1]) + dot_t(dkv, kv_weight)
     xhat_one = (x - mean_one) * inv_one
     input_grad = (dmid + norm_back(dn1, xhat_one, inv_one, gain_one)).astype(BF)
-    (dkv,) = hold([dkv], input_grad)
+    add_up = lambda first, others: sum((o.astype(F32) for o in others), first.astype(F32)).astype(BF)
+
+    def over_row(pack):
+        held = [lax.dynamic_index_in_dim(pack, me ^ k, 0, False) for k in range(rows)]
+        return add_up(held[0], [send(held[k], "row", k) for k in range(1, rows)])
+
+    packs = [over_row(dot_0(normed, dkv, BF).reshape(rows, feat, 2 * HD))]
+    (input_grad,) = hold([input_grad], packs[0])
     input_grad = from_rows(input_grad).astype(F32)
 
     total = lambda t: jnp.sum(t.astype(F32), axis=0)
@@ -623,13 +639,11 @@
     sizes = [v.shape[1] for v in vecs]
     pad = -sum(sizes) % 16
     vecs.append(jnp.zeros((rows, pad, 2 * HD), F32))
-    packs = [dot_0(normed, dkv, BF).reshape(rows, feat, 2 * HD), jnp.concatenate(vecs, axis=1).astype(BF)]
-    add_up = lambda first, others: sum((o.astype(F32) for o in others), first.astype(F32)).astype(BF)
-    for i, pack in enumerate(packs):
-        held = [lax.dynamic_index_in_dim(pack, me ^ k, 0, False) for k in range(rows)]
-        pack = add_up(held[0], [send(held[k], "row", k) for k in range(1, rows)])
-        pack = add_up(pack, [swap(pack)])
-        packs[i] = add_up(pack, [send(pack, "col", k) for k in range(1, cols)])
+    packs.append(over_row(jnp.concatenate(vecs, axis=1).astype(BF)))
+    pack = jnp.concatenate(packs, axis=0)
+    pack = add_up(pack, [swap(pack)])
+    pack = add_up(pack, [send(pack, "col", k) for k in range(1, cols)])
+    packs = [pack[:feat], pack[feat:]]
     keyval_weight_grad = packs[0].astype(F32)
     pack = packs[1]
     ends, at = [], 0

time: 1090 us -> 1030 us (0.945)
  waiting for transfers between devices: 355 us -> 273 us
  Pallas kernels: 340 us -> 357 us
  starting transfers between devices: 121 us -> 106 us
  local copies, waits for them, and re-layouts: 66.1 us -> 78.1 us
    ppermute x81 -> x84, waiting for transfers between devices: 318 us -> 273 us  [send(): return lax.ppermute(x, axis, [(i, i ^ bits) for i in range(n)])]
    all_gather x4, waiting for transfers between devices: 36.4 us -> 0.04 us  [on_device(): lax.all_gather(w, 'row', axis=axis, tiled=True)]
    ppermute x81 -> x84, starting transfers between devices: 120 us -> 105 us  [send(): return lax.ppermute(x, axis, [(i, i ^ bits) for i in range(n)])]
    unnamed x159 -> x212, local copies, waits for them, and re-layouts: 32.1 us -> 37.4 us
  transfers between devices with their start and end apart: 89 -> 92, of which waited for: 34 -> 37; matrix products, arithmetic and copies ran while one was open for 21% -> 24% of each run, Pallas kernels for 31% -> 35%
where the time goes in v3:
time: 1030 us; the launch traced here: 1020 us
  Pallas kernels  357 us (35%)
  waiting for transfers between devices  273 us (27%)
  starting transfers between devices  106 us (10%)
  other arithmetic  105 us (10%)
  matrix products  84.1 us (8%)
  local copies, waits for them, and re-layouts  78.1 us (8%)
  between operations  16.4 us (2%)
    ppermute x84, waiting for transfers between devices, send(): return lax.ppermute(x, axis, [(i, i ^ bits) for i in range(n)])  273 us
    ppermute x84, starting transfers between devices, send(): return lax.ppermute(x, axis, [(i, i ^ bits) for i in range(n)])  105 us
    pallas_call x2, Pallas kernels, attention_backward(): pl.pallas_call(functools.partial(bwd_kernel, bs=bs, heads=heads, hg=heads...  84.7 us
    pallas_call x4, Pallas kernels, up(): pl.pallas_call(functools.partial(up_kernel, half=half, step=512), grid=(2...  74.6 us
    pallas_call x4, Pallas kernels, down(): pl.pallas_call(functools.partial(down_kernel, half=half, step=512), grid=...  71.7 us
    pallas_call x2, Pallas kernels, weight_grads(): pl.pallas_call(grads_kernel, grid=(2, width // tm), in_specs=[xs] * 4 + [...  64.4 us
    pallas_call x1, Pallas kernels, attention_forward(): pl.pallas_call(functools.partial(fwd_kernel, bs=bs, heads=heads, hg=heads...  61.5 us
    unnamed x212, local copies, waits for them, and re-layouts  37.4 us
  transfers between devices with their start and end apart: 92, of which 37 were waited for; matrix products, arithmetic and copies ran while one was open for 24% of the time, Pallas kernels for 35%

profile of v3, /device:TPU:0, one launch (start us, length us, event | category | flops | bytes accessed | tf_op | source)
XLA Modules:
  0.0 1019.6 jit_solution(13520695068597696572)
XLA Ops:
  29.3 13.2 %collective-permute-done.6.refs_0_ = bf16[512,256]{1,0:T(8,128)(2,1)} collective-permute-done((bf16[512,256]{1,0:T(8,128)(2,1)S(1)}, bf16[512,256]{1,0:T(8,128)(2,1)}, u32[]{:S(2)}, u32[]{:S(2)}) %collective-permute-start.6) | collective-permute-done | bytes 262176 | tf_op jit(solution)/shard_map/ppermute | solution.py:407
  107.1 15.1 %collective-permute-done.31.refs_4_.refs_5_ = f32[1,1024]{1,0:T(1,128)S(1)} collective-permute-done((f32[1,1024]{1,0:T(1,128)S(1)}, f32[1,1024]{1,0:T(1,128)S(1)}, u32[]{:S(2)}, u32[]{:S(2)}) %collective-permute-start.31) | collective-permute-done | bytes 4128 | tf_op jit(solution)/shard_map/ppermute | solution.py:407
  150.0 14.2 %collective-permute-done.12.refs_3_ = bf16[640,512]{1,0:T(8,128)(2,1)S(1)} collective-permute-done((bf16[640,512]{1,0:T(8,128)(2,1)}, bf16[640,512]{1,0:T(8,128)(2,1)S(1)}, u32[]{:S(2)}, u32[]{:S(2)}) %collective-permute-start.12) | collective-permute-done | bytes 655392 | tf_op jit(solution)/shard_map/ppermute | solution.py:407
  186.5 11.9 %collective-permute-done.13.refs_1_ = bf16[2,320,256]{2,1,0:T(8,128)(2,1)S(1)} collective-permute-done((bf16[2,320,256]{2,1,0:T(8,128)(2,1)}, bf16[2,320,256]{2,1,0:T(8,128)(2,1)S(1)}, u32[]{:S(2)}, u32[]{:S(2)}) %collective-permute-start.13) | collective-permute-done | bytes 327712 | tf_op jit(solution)/shard_map/ppermute | solution.py:407
  244.5 13.0 %collective-permute-done.27.refs_5_ = bf16[2,512,128]{2,1,0:T(8,128)(2,1)} collective-permute-done((bf16[2,512,128]{2,1,0:T(8,128)(2,1)}, bf16[2,512,128]{2,1,0:T(8,128)(2,1)}, u32[]{:S(2)}, u32[]{:S(2)}) %collective-permute-start.27) | collective-permute-done | bytes 262176 | tf_op jit(solution)/shard_map/ppermute | solution.py:407
  271.1 61.5 %attn_fwd.1 = (bf16[640,1024]{1,0:T(8,128)(2,1)}, bf16[640,1024]{1,0:T(8,128)(2,1)}, f32[5,16,128]{2,1,0:T(8,128)}) custom-call(s32[6,5]{1,0:T(8,128)} %stack.197.tab, bf16[640,1024]{1,0:T(8,128)(2,1)} %add_convert_fusion.8.refs_0_, bf16[640,1024]{1,0:T(8,128)(2,1)} %add_convert_fusion.7.refs_1_, ...), custom_call_target="tpu_custom_call" | custom-call | flops 1000000 | bytes 1000000 | tf_op jit(solution)/shard_map/attn_fwd/pallas_call | solution.py:88
  364.4 18.4 %hidden_up.4 = (bf16[1280,1024]{1,0:T(8,128)(2,1)}, bf16[1280,1024]{1,0:T(8,128)(2,1)}) custom-call(bf16[640,2048]{1,0:T(8,128)(2,1)} %add_convert_fusion.5.refs_0_, bf16[640,2048]{1,0:T(8,128)(2,1)} %collective-permute-done.34.refs_1_, bf16[640,2048]{1,0:T(8,128)(2,1)} %get-tuple-element.156.refs_4_.refs_2_, ...), custom_call_target="tpu_custom_call" | custom-call | flops 1000000 | bytes 1000000 | tf_op jit(solution)/shard_map/hidden_up/pallas_call | solution.py:273
  382.8 35.9 %collective-permute-done.39.refs_0_ = bf16[640,2048]{1,0:T(8,128)(2,1)} collective-permute-done((bf16[640,2048]{1,0:T(8,128)(2,1)}, bf16[640,2048]{1,0:T(8,128)(2,1)}, u32[]{:S(2)}, u32[]{:S(2)}) %collective-permute-start.39) | collective-permute-done | bytes 2621472 | tf_op jit(solution)/shard_map/ppermute | solution.py:407
  424.0 18.8 %hidden_up.5 = (bf16[1280,1024]{1,0:T(8,128)(2,1)}, bf16[1280,1024]{1,0:T(8,128)(2,1)}) custom-call(bf16[640,2048]{1,0:T(8,128)(2,1)} %hold.25.refs_0_.refs_2_, bf16[640,2048]{1,0:T(8,128)(2,1)} %collective-permute-done.40.refs_1_.refs_3_, bf16[640,2048]{1,0:T(8,128)(2,1)} %get-tuple-element.86.refs_2_.refs_6_, ...), custom_call_target="tpu_custom_call" | custom-call | flops 1000000 | bytes 1000000 | tf_op jit(solution)/shard_map/hidden_up/pallas_call | solution.py:273
  442.8 32.1 %hidden_grads.2.refs_6_ = bf16[2,2048,1024]{2,1,0:T(8,128)(2,1)} custom-call(bf16[640,2048]{1,0:T(8,128)(2,1)} %add_convert_fusion.5.refs_0_, bf16[640,2048]{1,0:T(8,128)(2,1)} %collective-permute-done.34.refs_1_, bf16[640,2048]{1,0:T(8,128)(2,1)} %hold.25.refs_0_.refs_2_, bf16[640,2048]{1,0:T(8,128)(2,1)} %collective-permute-done.40.refs_1_.refs_3_, ...), custom_call_target="tpu_custom_call" | custom-call | flops 1000000 | bytes 1000000 | tf_op jit(solution)/shard_map/hidden_grads/pallas_call | solution.py:341
  475.0 18.7 %hidden_up.6 = (bf16[1280,1024]{1,0:T(8,128)(2,1)}, bf16[1280,1024]{1,0:T(8,128)(2,1)}) custom-call(bf16[640,2048]{1,0:T(8,128)(2,1)} %add_convert_fusion.5.refs_0_, bf16[640,2048]{1,0:T(8,128)(2,1)} %collective-permute-done.34.refs_1_, bf16[640,2048]{1,0:T(8,128)(2,1)} %get-tuple-element.156.refs_4_.refs_2_, ...), custom_call_target="tpu_custom_call" | custom-call | flops 1000000 | bytes 1000000 | tf_op jit(solution)/shard_map/hidden_up/pallas_call | solution.py:273
  493.7 18.8 %hidden_up.7 = (bf16[1280,1024]{1,0:T(8,128)(2,1)}, bf16[1280,1024]{1,0:T(8,128)(2,1)}) custom-call(bf16[640,2048]{1,0:T(8,128)(2,1)} %hold.25.refs_0_.refs_2_, bf16[640,2048]{1,0:T(8,128)(2,1)} %collective-permute-done.40.refs_1_.refs_3_, bf16[640,2048]{1,0:T(8,128)(2,1)} %get-tuple-element.86.refs_2_.refs_6_, ...), custom_call_target="tpu_custom_call" | custom-call | flops 1000000 | bytes 1000000 | tf_op jit(solution)/shard_map/hidden_up/pallas_call | solution.py:273
  512.5 18.4 %hidden_down.4 = (f32[640,2048]{1,0:T(8,128)}, bf16[640,2048]{1,0:T(8,128)(2,1)}) custom-call(bf16[1280,1024]{1,0:T(8,128)(2,1)} %get-tuple-element.87.refs_9_.refs_12_.refs_0_, bf16[1280,1024]{1,0:T(8,128)(2,1)} %get-tuple-element.92.refs_1_.refs_9_, bf16[2,2048,1024]{2,1,0:T(8,128)(2,1)} %all-gather.9.cloned.1.call-done.refs_4_.refs_2_, ...), custom_call_target="tpu_custom_call" | custom-call | flops 1000000 | bytes 1000000 | tf_op jit(solution)/shard_map/hidden_down/pallas_call | solution.py:306
  530.9 17.7 %hidden_down.5 = (f32[640,2048]{1,0:T(8,128)}, bf16[640,2048]{1,0:T(8,128)(2,1)}) custom-call(bf16[1280,1024]{1,0:T(8,128)(2,1)} %get-tuple-element.85.refs_1_.refs_6_.refs_8_.refs_0_, bf16[1280,1024]{1,0:T(8,128)(2,1)} %get-tuple-element.90.refs_6_.refs_1_.refs_8_, bf16[2,2048,1024]{2,1,0:T(8,128)(2,1)} %all-gather.9.cloned.1.call-done.refs_4_.refs_2_, ...), custom_call_target="tpu_custom_call" | custom-call | flops 1000000 | bytes 1000000 | tf_op jit(solution)/shard_map/hidden_down/pallas_call | solution.py:306
  554.5 32.3 %hidden_grads.3.refs_0_ = bf16[2,2048,1024]{2,1,0:T(8,128)(2,1)} custom-call(bf16[640,2048]{1,0:T(8,128)(2,1)} %add_convert_fusion.5.refs_0_, bf16[640,2048]{1,0:T(8,128)(2,1)} %collective-permute-done.34.refs_1_, bf16[640,2048]{1,0:T(8,128)(2,1)} %hold.25.refs_0_.refs_2_, bf16[640,2048]{1,0:T(8,128)(2,1)} %collective-permute-done.40.refs_1_.refs_3_, ...), custom_call_target="tpu_custom_call" | custom-call | flops 1000000 | bytes 1000000 | tf_op jit(solution)/shard_map/hidden_grads/pallas_call | solution.py:341
  588.4 17.7 %hidden_down.6 = (f32[640,2048]{1,0:T(8,128)}, bf16[640,2048]{1,0:T(8,128)(2,1)}) custom-call(bf16[1280,1024]{1,0:T(8,128)(2,1)} %get-tuple-element.88.refs_11_.refs_0_, bf16[1280,1024]{1,0:T(8,128)(2,1)} %get-tuple-element.91.refs_11_.refs_1_, bf16[2,2048,1024]{2,1,0:T(8,128)(2,1)} %all-gather.9.cloned.1.call-done.refs_4_.refs_2_, ...), custom_call_target="tpu_custom_call" | custom-call | flops 1000000 | bytes 1000000 | tf_op jit(solution)/shard_map/hidden_down/pallas_call | solution.py:306
  606.1 17.9 %hidden_down.7 = (f32[640,2048]{1,0:T(8,128)}, bf16[640,2048]{1,0:T(8,128)(2,1)}) custom-call(bf16[1280,1024]{1,0:T(8,128)(2,1)} %get-tuple-element.82.refs_10_.refs_0_, bf16[1280,1024]{1,0:T(8,128)(2,1)} %get-tuple-element.89.refs_10_.refs_1_, bf16[2,2048,1024]{2,1,0:T(8,128)(2,1)} %all-gather.9.cloned.1.call-done.refs_4_.refs_2_, ...), custom_call_target="tpu_custom_call" | custom-call | flops 1000000 | bytes 1000000 | tf_op jit(solution)/shard_map/hidden_down/pallas_call | solution.py:306
  624.0 22.5 %collective-permute-done.45.refs_0_ = bf16[640,2048]{1,0:T(8,128)(2,1)} collective-permute-done((bf16[640,2048]{1,0:T(8,128)(2,1)}, bf16[640,2048]{1,0:T(8,128)(2,1)}, u32[]{:S(2)}, u32[]{:S(2)}) %collective-permute-start.45) | collective-permute-done | bytes 2621472 | tf_op jit(solution)/shard_map/ppermute | solution.py:407
  701.4 73.4 %attn_bwd.2 = (bf16[512,1024]{1,0:T(8,128)(2,1)}, bf16[512,1024]{1,0:T(8,128)(2,1)}, f32[5120,256]{1,0:T(8,128)}) custom-call(s32[6,4]{1,0:T(8,128)} %bitcast.329, bf16[640,1024]{1,0:T(8,128)(2,1)} %add_convert_fusion.8.refs_0_, bf16[640,1024]{1,0:T(8,128)(2,1)} %add_convert_fusion.7.refs_1_, bf16[640,1024]{1,0:T(8,128)(2,1)} %convolution_convert_fusion.4.refs_2_, ...), custom_call_target="tpu_custom_call" | custom-call | flops 1000000 | bytes 1000000 | tf_op jit(solution)/shard_map/attn_bwd/pallas_call | solution.py:186
  782.7 11.3 %attn_bwd.3 = (bf16[128,1024]{1,0:T(8,128)(2,1)}, bf16[128,1024]{1,0:T(8,128)(2,1)}, f32[5120,256]{1,0:T(8,128)}) custom-call(s32[6,1]{1,0:T(8,128)} %slice.184.tab, bf16[640,1024]{1,0:T(8,128)(2,1)} %add_convert_fusion.8.refs_0_, bf16[640,1024]{1,0:T(8,128)(2,1)} %add_convert_fusion.7.refs_1_, bf16[640,1024]{1,0:T(8,128)(2,1)} %convolution_convert_fusion.4.refs_2_, ...), custom_call_target="tpu_custom_call" | custom-call | flops 1000000 | bytes 1000000 | tf_op jit(solution)/shard_map/attn_bwd/pallas_call | solution.py:186
  818.7 9.3 collective-permute-start.50
  848.4 12.4 %collective-permute-done.50 = bf16[640,512]{1,0:T(8,128)(2,1)} collective-permute-done((bf16[640,512]{1,0:T(8,128)(2,1)}, bf16[640,512]{1,0:T(8,128)(2,1)}, u32[]{:S(2)}, u32[]{:S(2)}) %collective-permute-start.50) | collective-permute-done | bytes 655392 | tf_op jit(solution)/shard_map/ppermute | solution.py:407
  960.0 15.1 %collective-permute-done.70 = bf16[576,256]{1,0:T(8,128)(2,1)} collective-permute-done((bf16[576,256]{1,0:T(8,128)(2,1)S(1)}, bf16[576,256]{1,0:T(8,128)(2,1)}, u32[]{:S(2)}, u32[]{:S(2)}) %collective-permute-start.70) | collective-permute-done | bytes 294944 | tf_op jit(solution)/shard_map/ppermute | solution.py:407
  978.2 17.7 %collective-permute-done.73 = bf16[512,256]{0,1:T(8,128)(2,1)S(1)} collective-permute-done((bf16[512,256]{0,1:T(8,128)(2,1)S(1)}, bf16[512,256]{0,1:T(8,128)(2,1)S(1)}, u32[]{:S(2)}, u32[]{:S(2)}) %collective-permute-start.73) | collective-permute-done | bytes 262176 | tf_op jit(solution)/shard_map/ppermute | solution.py:407
  (587 shorter events, 465.9 us)
Async XLA Ops:
  7.2 217.2 %all-gather.5.cloned.1.call-start = ((), (), s32[]{:S(2)}) async-start(), calls=%async_computation.4 | async-start | bytes 5242880 | tf_op jit(solution)/shard_map/all_gather | solution.py:456
  50.0 286.2 %all-gather.7.cloned.1.call-start = ((), (), s32[]{:S(2)}) async-start(), calls=%async_computation.5 | async-start | bytes 5242880 | tf_op jit(solution)/shard_map/all_gather | solution.py:456
  50.0 50.3 %collective-permute-start.23 = (bf16[512]{0:T(512)(128)(2,1)}, bf16[512]{0:T(512)(128)(2,1)}, u32[]{:S(2)}, u32[]{:S(2)}) collective-permute-start(bf16[512]{0:T(512)(128)(2,1)} %param.24), channel_id=1, source_target_pairs={{0,2},{1,3},{2,0},{3,1},{4,6},{5,7},{6,4},{7,5},{8,10},{9,11},{10,... | collective-permute-start | bytes 3080 | tf_op jit(solution)/shard_map/ppermute | solution.py:407
  50.1 52.5 %collective-permute-start.25 = (bf16[512]{0:T(512)(128)(2,1)}, bf16[512]{0:T(512)(128)(2,1)}, u32[]{:S(2)}, u32[]{:S(2)}) collective-permute-start(bf16[512]{0:T(512)(128)(2,1)} %param.24), channel_id=1, source_target_pairs={{0,3},{1,2},{2,1},{3,0},{4,7},{5,6},{6,5},{7,4},{8,11},{9,10},{10,... | collective-permute-start | bytes 3080 | tf_op jit(solution)/shard_map/ppermute | solution.py:407
  129.5 231.1 %all-gather.9.cloned.1.call-start = ((), (), s32[]{:S(2)}) async-start(), calls=%async_computation.6 | async-start | bytes 10485760 | tf_op jit(solution)/shard_map/all_gather | solution.py:456
  133.8 341.2 %all-gather.11.cloned.1.call-start = ((), (), s32[]{:S(2)}) async-start(), calls=%async_computation.7 | async-start | bytes 10485760 | tf_op jit(solution)/shard_map/all_gather | solution.py:456
  139.3 47.1 %collective-permute-start.16 = (bf16[640,512]{1,0:T(8,128)(2,1)}, bf16[640,512]{1,0:T(8,128)(2,1)S(1)}, u32[]{:S(2)}, u32[]{:S(2)}) collective-permute-start(bf16[640,512]{1,0:T(8,128)(2,1)} %get-tuple-element.68), channel_id=1, source_target_pairs={{0,4},{4,0},{8,12},{12,8},{1,5},{5,1},{9,13},{13,9},{2,6},{6,2},{1... | collective-permute-start | bytes 1966088 | tf_op jit(solution)/shard_map/ppermute | solution.py:407
  224.6 108.0 %collective-permute-start.37 = (bf16[2,512,128]{2,1,0:T(8,128)(2,1)}, bf16[2,512,128]{2,1,0:T(8,128)(2,1)}, u32[]{:S(2)}, u32[]{:S(2)}) collective-permute-start(bf16[2,512,128]{2,1,0:T(8,128)(2,1)} %get-tuple-element.207), channel_id=1, source_target_pairs={{0,2},{1,3},{2,0},{3,1},{4,6},{5,7},{6,4},{7,5},{8,10},{9,11},{10,... | collective-permute-start | bytes 786440 | tf_op jit(solution)/shard_map/ppermute | solution.py:407
  227.5 105.0 %collective-permute-start.36 = (bf16[2,512,128]{2,1,0:T(8,128)(2,1)}, bf16[2,512,128]{2,1,0:T(8,128)(2,1)}, u32[]{:S(2)}, u32[]{:S(2)}) collective-permute-start(bf16[2,512,128]{2,1,0:T(8,128)(2,1)} %get-tuple-element.214), channel_id=1, source_target_pairs={{0,2},{1,3},{2,0},{3,1},{4,6},{5,7},{6,4},{7,5},{8,10},{9,11},{10,... | collective-permute-start | bytes 786440 | tf_op jit(solution)/shard_map/ppermute | solution.py:407
  234.8 97.8 %collective-permute-start.38 = (bf16[640,2048]{1,0:T(8,128)(2,1)}, bf16[640,2048]{1,0:T(8,128)(2,1)}, u32[]{:S(2)}, u32[]{:S(2)}) collective-permute-start(bf16[640,2048]{1,0:T(8,128)(2,1)} %get-tuple-element.156.refs_4_.refs_2_), channel_id=1, source_target_pairs={{0,1},{1,0},{2,3},{3,2},{4,5},{5,4},{6,7},{7,6},{8,9},{9,8},{10,11... | collective-permute-start | bytes 7864328 | tf_op jit(solution)/shard_map/ppermute | solution.py:407
  336.1 250.8 %reduce-scatter.5.cloned.1.call-start = ((), (), s32[]{:S(2)}) async-start(), calls=%async_computation.8 | async-start | bytes 10485760 | tf_op jit(solution)/shard_map/reduce_scatter | solution.py:530
  359.2 59.5 %collective-permute-start.39 = (bf16[640,2048]{1,0:T(8,128)(2,1)}, bf16[640,2048]{1,0:T(8,128)(2,1)}, u32[]{:S(2)}, u32[]{:S(2)}) collective-permute-start(bf16[640,2048]{1,0:T(8,128)(2,1)} %add_convert_fusion.5.refs_0_), channel_id=1, source_target_pairs={{0,1},{1,0},{2,3},{3,2},{4,5},{5,4},{6,7},{7,6},{8,9},{9,8},{10,11... | collective-permute-start | bytes 7864328 | tf_op jit(solution)/shard_map/ppermute | solution.py:407
  360.6 58.2 %collective-permute-start.41 = (bf16[640,2048]{1,0:T(8,128)(2,1)}, bf16[640,2048]{1,0:T(8,128)(2,1)}, u32[]{:S(2)}, u32[]{:S(2)}) collective-permute-start(bf16[640,2048]{1,0:T(8,128)(2,1)} %get-tuple-element.86.refs_2_.refs_6_), channel_id=1, source_target_pairs={{0,16},{16,0},{1,17},{17,1},{2,18},{18,2},{3,19},{19,3},{4,20},{20... | collective-permute-start | bytes 7864328 | tf_op jit(solution)/shard_map/ppermute | solution.py:407
  474.9 205.8 %reduce-scatter.7.cloned.1.call-start = ((), (), s32[]{:S(2)}) async-start(), calls=%async_computation.9 | async-start | bytes 10485760 | tf_op jit(solution)/shard_map/reduce_scatter | solution.py:530
  586.9 314.4 %reduce-scatter.11.cloned.1.call-start = ((), (), s32[]{:S(2)}) async-start(), calls=%async_computation.11 | async-start | bytes 5242880 | tf_op jit(solution)/shard_map/reduce_scatter | solution.py:530
  587.0 59.6 %collective-permute-start.45 = (bf16[640,2048]{1,0:T(8,128)(2,1)}, bf16[640,2048]{1,0:T(8,128)(2,1)}, u32[]{:S(2)}, u32[]{:S(2)}) collective-permute-start(bf16[640,2048]{1,0:T(8,128)(2,1)} %hold.26.refs_12_), channel_id=1, source_target_pairs={{0,1},{1,0},{2,3},{3,2},{4,5},{5,4},{6,7},{7,6},{8,9},{9,8},{10,11... | collective-permute-start | bytes 7864328 | tf_op jit(solution)/shard_map/ppermute | solution.py:407
  588.1 58.4 %collective-permute-start.47 = (bf16[640,2048]{1,0:T(8,128)(2,1)}, bf16[640,2048]{1,0:T(8,128)(2,1)}, u32[]{:S(2)}, u32[]{:S(2)}) collective-permute-start(bf16[640,2048]{1,0:T(8,128)(2,1)} %get-tuple-element.100), channel_id=1, source_target_pairs={{0,16},{16,0},{1,17},{17,1},{2,18},{18,2},{3,19},{19,3},{4,20},{20... | collective-permute-start | bytes 7864328 | tf_op jit(solution)/shard_map/ppermute | solution.py:407
  672.5 135.4 %collective-permute-start.43 = (bf16[640,2048]{1,0:T(8,128)(2,1)}, bf16[640,2048]{1,0:T(8,128)(2,1)}, u32[]{:S(2)}, u32[]{:S(2)}) collective-permute-start(bf16[640,2048]{1,0:T(8,128)(2,1)} %get-tuple-element.98), channel_id=1, source_target_pairs={{0,16},{16,0},{1,17},{17,1},{2,18},{18,2},{3,19},{19,3},{4,20},{20... | collective-permute-start | bytes 7864328 | tf_op jit(solution)/shard_map/ppermute | solution.py:407
  680.6 295.7 %reduce-scatter.9.cloned.1.call-start = ((), (), s32[]{:S(2)}) async-start(), calls=%async_computation.10 | async-start | bytes 5242880 | tf_op jit(solution)/shard_map/reduce_scatter | solution.py:530
  680.7 98.0 %collective-permute-start.48 = (bf16[2,512,1024]{2,1,0:T(8,128)(2,1)}, bf16[2,512,1024]{2,1,0:T(8,128)(2,1)}, u32[]{:S(2)}, u32[]{:S(2)}) collective-permute-start(bf16[2,512,1024]{2,1,0:T(8,128)(2,1)} %reduce-scatter.7.cloned.1.call-done.refs_9_), channel_id=1, source_target_pairs={{0,2},{1,3},{2,0},{3,1},{4,6},{5,7},{6,4},{7,5},{8,10},{9,11},{10,... | collective-permute-start | bytes 6291464 | tf_op jit(solution)/shard_map/ppermute | solution.py:407
  701.1 106.8 %collective-permute-start.46 = (bf16[640,2048]{1,0:T(8,128)(2,1)}, bf16[640,2048]{1,0:T(8,128)(2,1)}, u32[]{:S(2)}, u32[]{:S(2)}) collective-permute-start(bf16[640,2048]{1,0:T(8,128)(2,1)} %hold.29), channel_id=1, source_target_pairs={{0,1},{1,0},{2,3},{3,2},{4,5},{5,4},{6,7},{7,6},{8,9},{9,8},{10,11... | collective-permute-start | bytes 7864328 | tf_op jit(solution)/shard_map/ppermute | solution.py:407
  782.7 107.3 %collective-permute-start.83 = (bf16[1024,512]{0,1:T(8,128)(2,1)}, bf16[1024,512]{0,1:T(8,128)(2,1)}, u32[]{:S(2)}, u32[]{:S(2)}) collective-permute-start(bf16[1024,512]{0,1:T(8,128)(2,1)} %get-tuple-element.205), channel_id=1, source_target_pairs={{0,16},{16,0},{1,17},{17,1},{2,18},{18,2},{3,19},{19,3},{4,20},{20... | collective-permute-start | bytes 3145736 | tf_op jit(solution)/shard_map/ppermute | solution.py:407
  953.3 51.9 %collective-permute-start.64 = (bf16[640,512]{1,0:T(8,128)(2,1)}, bf16[640,512]{1,0:T(8,128)(2,1)S(1)}, u32[]{:S(2)}, u32[]{:S(2)}) collective-permute-start(bf16[640,512]{1,0:T(8,128)(2,1)} %get-tuple-element.179), channel_id=1, source_target_pairs={{0,4},{4,0},{8,12},{12,8},{1,5},{5,1},{9,13},{13,9},{2,6},{6,2},{1... | collective-permute-start | bytes 1966088 | tf_op jit(solution)/shard_map/ppermute | solution.py:407
  955.1 50.1 %collective-permute-start.63 = (bf16[640,512]{1,0:T(8,128)(2,1)}, bf16[640,512]{1,0:T(8,128)(2,1)S(1)}, u32[]{:S(2)}, u32[]{:S(2)}) collective-permute-start(bf16[640,512]{1,0:T(8,128)(2,1)} %get-tuple-element.180), channel_id=1, source_target_pairs={{0,8},{4,12},{8,0},{12,4},{1,9},{5,13},{9,1},{13,5},{2,10},{6,14},... | collective-permute-start | bytes 1966088 | tf_op jit(solution)/shard_map/ppermute | solution.py:407
  (162 other events, 2279.4 us)
Sparse Core Ops, SparseCore 0:
  50.1 66.4 all-gather.4
  129.6 81.1 all-gather.6
  212.7 87.3 all-gather.8
  336.2 90.9 all-gather.10
  475.0 89.4 reduce-scatter.4
  587.0 90.1 reduce-scatter.6
  680.7 55.6 reduce-scatter.10
  848.4 59.8 reduce-scatter.8

commit v4 on v3

--- a/solution.py
+++ b/solution.py
@@ -479,11 +479,9 @@
     normed = ((x - mean_one) * inv_one * gain_one + shift_one).astype(BF)
     kv_shift = jnp.concatenate([jnp.zeros((HD,), F32), value_bias.astype(F32)])[None]
     kv = (dot(normed, kv_weight) + kv_shift).astype(BF)
-    out_blocks[1:] = hold(out_blocks[1:], kv, up_bias[1], pieces[1], *q_parts[1:])
-    wo_t = gather_square(out_blocks)
     odd = z % 2
     kv_pair = jnp.stack(absolute([kv, z_one(kv)], odd))
-    halves = hold([kv_pair[:, : tokens // 2], kv_pair[:, tokens // 2 :]], pieces[2], dy_parts[-1])
+    halves = hold([kv_pair[:, : tokens // 2], kv_pair[:, tokens // 2 :]], pieces[1], pieces[2], dy_parts[-1], up_bias[1], *q_parts[1:])
     halves = [[h] for h in halves]
     bits = [1 << i for i in range(rows.bit_length() - 1)]
     for step in range(len(bits)):
@@ -500,6 +498,8 @@
     kv_all = jnp.concatenate(halves, axis=2)
     kv_all = kv_all.reshape(rows, 2, blocks, bs, 2 * HD).transpose(1, 2, 0, 3, 4).reshape(2 * local, 2 * HD)
     keys, values = kv_all[:, :HD], kv_all[:, HD:]
+    out_blocks[1:] = hold(out_blocks[1:], keys)
+    wo_t = gather_square(out_blocks)
     hidden_near = hold([half_of(expand_weight, core, fh, 1), half_of(shrink_weight, core, fh, 0).T], out_blocks[1])
     hidden_near = gather_rows(jnp.stack(hidden_near), 1)
     (wq_own,) = hold([wq_own], keys, pieces[4], *dy_parts[2:-1])

time: 1030 us -> 1010 us (0.981)
  Pallas kernels: 357 us -> 323 us
  starting transfers between devices: 106 us -> 121 us
    pallas_call x2, Pallas kernels: 84.7 us -> 66.4 us  [attention_backward(): pl.pallas_call(functools.partial(bwd_kernel, bs=bs, heads=heads, hg=heads...]
    pallas_call x1, Pallas kernels: 61.5 us -> 45.9 us  [attention_forward(): pl.pallas_call(functools.partial(fwd_kernel, bs=bs, heads=heads, hg=heads...]
    ppermute x84, starting transfers between devices: 105 us -> 121 us  [send(): return lax.ppermute(x, axis, [(i, i ^ bits) for i in range(n)])]
    unnamed x212 -> x190, local copies, waits for them, and re-layouts: 37.4 us -> 39.3 us
  transfers between devices with their start and end apart: 92 -> 92, of which waited for: 37 -> 30; matrix products, arithmetic and copies ran while one was open for 24% -> 25% of each run, Pallas kernels for 35% -> 32%
where the time goes in v4:
time: 1010 us; the launch traced here: 1000 us
  Pallas kernels  323 us (32%)
  waiting for transfers between devices  273 us (27%)
  starting transfers between devices  121 us (12%)
  other arithmetic  105 us (10%)
  matrix products  83.5 us (8%)
  local copies, waits for them, and re-layouts  80.8 us (8%)
  between operations  16.3 us (2%)
    ppermute x84, waiting for transfers between devices, send(): return lax.ppermute(x, axis, [(i, i ^ bits) for i in range(n)])  273 us
    ppermute x84, starting transfers between devices, send(): return lax.ppermute(x, axis, [(i, i ^ bits) for i in range(n)])  121 us
    pallas_call x4, Pallas kernels, up(): pl.pallas_call(functools.partial(up_kernel, half=half, step=512), grid=(2...  74.4 us
    pallas_call x4, Pallas kernels, down(): pl.pallas_call(functools.partial(down_kernel, half=half, step=512), grid=...  71.8 us
    pallas_call x2, Pallas kernels, attention_backward(): pl.pallas_call(functools.partial(bwd_kernel, bs=bs, heads=heads, hg=heads...  66.4 us
    pallas_call x2, Pallas kernels, weight_grads(): pl.pallas_call(grads_kernel, grid=(2, width // tm), in_specs=[xs] * 4 + [...  64.4 us
    pallas_call x1, Pallas kernels, attention_forward(): pl.pallas_call(functools.partial(fwd_kernel, bs=bs, heads=heads, hg=heads...  45.9 us
    unnamed x190, local copies, waits for them, and re-layouts  39.3 us
  transfers between devices with their start and end apart: 92, of which 30 were waited for; matrix products, arithmetic and copies ran while one was open for 25% of the time, Pallas kernels for 32%

profile of v4, /device:TPU:0, one launch (start us, length us, event | category | flops | bytes accessed | tf_op | source)
XLA Modules:
  0.0 1002.6 jit_solution(16860473416231822029)
XLA Ops:
  88.6 16.9 %collective-permute-done.14.refs_5_ = f32[1,1024]{1,0:T(1,128)S(1)} collective-permute-done((f32[1,1024]{1,0:T(1,128)S(1)}, f32[1,1024]{1,0:T(1,128)S(1)}, u32[]{:S(2)}, u32[]{:S(2)}) %collective-permute-start.14) | collective-permute-done | bytes 4128 | tf_op jit(solution)/shard_map/ppermute | solution.py:407
  110.9 13.2 %collective-permute-done.20.refs_4_ = bf16[2,512,128]{2,1,0:T(8,128)(2,1)S(1)} collective-permute-done((bf16[2,512,128]{2,1,0:T(8,128)(2,1)}, bf16[2,512,128]{2,1,0:T(8,128)(2,1)S(1)}, u32[]{:S(2)}, u32[]{:S(2)}) %collective-permute-start.20) | collective-permute-done | bytes 262176 | tf_op jit(solution)/shard_map/ppermute | solution.py:407
  171.0 13.5 %collective-permute-done.26.refs_2_ = bf16[2,512,128]{2,1,0:T(8,128)(2,1)} collective-permute-done((bf16[2,512,128]{2,1,0:T(8,128)(2,1)}, bf16[2,512,128]{2,1,0:T(8,128)(2,1)}, u32[]{:S(2)}, u32[]{:S(2)}) %collective-permute-start.26) | collective-permute-done | bytes 262176 | tf_op jit(solution)/shard_map/ppermute | solution.py:407
  215.0 13.5 %collective-permute-done.29.refs_5_ = bf16[2,512,128]{2,1,0:T(8,128)(2,1)} collective-permute-done((bf16[2,512,128]{2,1,0:T(8,128)(2,1)}, bf16[2,512,128]{2,1,0:T(8,128)(2,1)}, u32[]{:S(2)}, u32[]{:S(2)}) %collective-permute-start.29) | collective-permute-done | bytes 262176 | tf_op jit(solution)/shard_map/ppermute | solution.py:407
  242.3 45.9 %attn_fwd.1 = (bf16[640,1024]{1,0:T(8,128)(2,1)}, bf16[640,1024]{1,0:T(8,128)(2,1)}, f32[5,16,128]{2,1,0:T(8,128)}) custom-call(s32[6,5]{1,0:T(8,128)} %stack.197.tab, bf16[640,1024]{1,0:T(8,128)(2,1)} %add_convert_fusion.8.refs_0_, bf16[640,1024]{1,0:T(8,128)(2,1)} %add_convert_fusion.7.refs_1_, ...), custom_call_target="tpu_custom_call" | custom-call | flops 1000000 | bytes 1000000 | tf_op jit(solution)/shard_map/attn_fwd/pallas_call | solution.py:88
  291.8 25.7 %collective-permute-start.33 = (bf16[2048,1024]{1,0:T(8,128)(2,1)}, bf16[2048,1024]{1,0:T(8,128)(2,1)S(1)}, u32[]{:S(2)}, u32[]{:S(2)}) collective-permute-start(bf16[2048,1024]{1,0:T(8,128)(2,1)} %all-gather.7.cloned.1.call-done), channel_id=1, source_target_pairs={{0,16},{16,0},{1,17},{17,1},{2,18},{18,2},{3,19},{19,3},{4,20},{20... | collective-permute-start | bytes 12582920 | tf_op jit(solution)/shard_map/ppermute | solution.py:407
  345.3 18.4 %hidden_up.4 = (bf16[1280,1024]{1,0:T(8,128)(2,1)}, bf16[1280,1024]{1,0:T(8,128)(2,1)}) custom-call(bf16[640,2048]{1,0:T(8,128)(2,1)} %add_convert_fusion.5.refs_0_, bf16[640,2048]{1,0:T(8,128)(2,1)} %collective-permute-done.34.refs_1_, bf16[640,2048]{1,0:T(8,128)(2,1)} %get-tuple-element.156.refs_4_.refs_2_, ...), custom_call_target="tpu_custom_call" | custom-call | flops 1000000 | bytes 1000000 | tf_op jit(solution)/shard_map/hidden_up/pallas_call | solution.py:273
  363.7 36.0 %collective-permute-done.39.refs_0_ = bf16[640,2048]{1,0:T(8,128)(2,1)} collective-permute-done((bf16[640,2048]{1,0:T(8,128)(2,1)}, bf16[640,2048]{1,0:T(8,128)(2,1)}, u32[]{:S(2)}, u32[]{:S(2)}) %collective-permute-start.39) | collective-permute-done | bytes 2621472 | tf_op jit(solution)/shard_map/ppermute | solution.py:407
  404.9 18.6 %hidden_up.5 = (bf16[1280,1024]{1,0:T(8,128)(2,1)}, bf16[1280,1024]{1,0:T(8,128)(2,1)}) custom-call(bf16[640,2048]{1,0:T(8,128)(2,1)} %hold.25.refs_0_.refs_2_, bf16[640,2048]{1,0:T(8,128)(2,1)} %collective-permute-done.40.refs_1_.refs_3_, bf16[640,2048]{1,0:T(8,128)(2,1)} %get-tuple-element.86.refs_2_.refs_6_, ...), custom_call_target="tpu_custom_call" | custom-call | flops 1000000 | bytes 1000000 | tf_op jit(solution)/shard_map/hidden_up/pallas_call | solution.py:273
  423.4 32.2 %hidden_grads.2.refs_6_ = bf16[2,2048,1024]{2,1,0:T(8,128)(2,1)} custom-call(bf16[640,2048]{1,0:T(8,128)(2,1)} %add_convert_fusion.5.refs_0_, bf16[640,2048]{1,0:T(8,128)(2,1)} %collective-permute-done.34.refs_1_, bf16[640,2048]{1,0:T(8,128)(2,1)} %hold.25.refs_0_.refs_2_, bf16[640,2048]{1,0:T(8,128)(2,1)} %collective-permute-done.40.refs_1_.refs_3_, ...), custom_call_target="tpu_custom_call" | custom-call | flops 1000000 | bytes 1000000 | tf_op jit(solution)/shard_map/hidden_grads/pallas_call | solution.py:341
  455.7 18.7 %hidden_up.6 = (bf16[1280,1024]{1,0:T(8,128)(2,1)}, bf16[1280,1024]{1,0:T(8,128)(2,1)}) custom-call(bf16[640,2048]{1,0:T(8,128)(2,1)} %add_convert_fusion.5.refs_0_, bf16[640,2048]{1,0:T(8,128)(2,1)} %collective-permute-done.34.refs_1_, bf16[640,2048]{1,0:T(8,128)(2,1)} %get-tuple-element.156.refs_4_.refs_2_, ...), custom_call_target="tpu_custom_call" | custom-call | flops 1000000 | bytes 1000000 | tf_op jit(solution)/shard_map/hidden_up/pallas_call | solution.py:273
  474.3 18.8 %hidden_up.7 = (bf16[1280,1024]{1,0:T(8,128)(2,1)}, bf16[1280,1024]{1,0:T(8,128)(2,1)}) custom-call(bf16[640,2048]{1,0:T(8,128)(2,1)} %hold.25.refs_0_.refs_2_, bf16[640,2048]{1,0:T(8,128)(2,1)} %collective-permute-done.40.refs_1_.refs_3_, bf16[640,2048]{1,0:T(8,128)(2,1)} %get-tuple-element.86.refs_2_.refs_6_, ...), custom_call_target="tpu_custom_call" | custom-call | flops 1000000 | bytes 1000000 | tf_op jit(solution)/shard_map/hidden_up/pallas_call | solution.py:273
  493.2 18.3 %hidden_down.4 = (f32[640,2048]{1,0:T(8,128)}, bf16[640,2048]{1,0:T(8,128)(2,1)}) custom-call(bf16[1280,1024]{1,0:T(8,128)(2,1)} %get-tuple-element.87.refs_9_.refs_12_.refs_0_, bf16[1280,1024]{1,0:T(8,128)(2,1)} %get-tuple-element.92.refs_1_.refs_9_, bf16[2,2048,1024]{2,1,0:T(8,128)(2,1)} %all-gather.9.cloned.1.call-done.refs_4_.refs_2_, ...), custom_call_target="tpu_custom_call" | custom-call | flops 1000000 | bytes 1000000 | tf_op jit(solution)/shard_map/hidden_down/pallas_call | solution.py:306
  511.7 17.9 %hidden_down.5 = (f32[640,2048]{1,0:T(8,128)}, bf16[640,2048]{1,0:T(8,128)(2,1)}) custom-call(bf16[1280,1024]{1,0:T(8,128)(2,1)} %get-tuple-element.85.refs_1_.refs_6_.refs_8_.refs_0_, bf16[1280,1024]{1,0:T(8,128)(2,1)} %get-tuple-element.90.refs_6_.refs_1_.refs_8_, bf16[2,2048,1024]{2,1,0:T(8,128)(2,1)} %all-gather.9.cloned.1.call-done.refs_4_.refs_2_, ...), custom_call_target="tpu_custom_call" | custom-call | flops 1000000 | bytes 1000000 | tf_op jit(solution)/shard_map/hidden_down/pallas_call | solution.py:306
  535.5 32.2 %hidden_grads.3.refs_0_ = bf16[2,2048,1024]{2,1,0:T(8,128)(2,1)} custom-call(bf16[640,2048]{1,0:T(8,128)(2,1)} %add_convert_fusion.5.refs_0_, bf16[640,2048]{1,0:T(8,128)(2,1)} %collective-permute-done.34.refs_1_, bf16[640,2048]{1,0:T(8,128)(2,1)} %hold.25.refs_0_.refs_2_, bf16[640,2048]{1,0:T(8,128)(2,1)} %collective-permute-done.40.refs_1_.refs_3_, ...), custom_call_target="tpu_custom_call" | custom-call | flops 1000000 | bytes 1000000 | tf_op jit(solution)/shard_map/hidden_grads/pallas_call | solution.py:341
  568.1 17.7 %hidden_down.6 = (f32[640,2048]{1,0:T(8,128)}, bf16[640,2048]{1,0:T(8,128)(2,1)}) custom-call(bf16[1280,1024]{1,0:T(8,128)(2,1)} %get-tuple-element.88.refs_11_.refs_0_, bf16[1280,1024]{1,0:T(8,128)(2,1)} %get-tuple-element.91.refs_11_.refs_1_, bf16[2,2048,1024]{2,1,0:T(8,128)(2,1)} %all-gather.9.cloned.1.call-done.refs_4_.refs_2_, ...), custom_call_target="tpu_custom_call" | custom-call | flops 1000000 | bytes 1000000 | tf_op jit(solution)/shard_map/hidden_down/pallas_call | solution.py:306
  585.8 17.9 %hidden_down.7 = (f32[640,2048]{1,0:T(8,128)}, bf16[640,2048]{1,0:T(8,128)(2,1)}) custom-call(bf16[1280,1024]{1,0:T(8,128)(2,1)} %get-tuple-element.82.refs_10_.refs_0_, bf16[1280,1024]{1,0:T(8,128)(2,1)} %get-tuple-element.89.refs_10_.refs_1_, bf16[2,2048,1024]{2,1,0:T(8,128)(2,1)} %all-gather.9.cloned.1.call-done.refs_4_.refs_2_, ...), custom_call_target="tpu_custom_call" | custom-call | flops 1000000 | bytes 1000000 | tf_op jit(solution)/shard_map/hidden_down/pallas_call | solution.py:306
  603.7 23.4 %collective-permute-done.45.refs_0_ = bf16[640,2048]{1,0:T(8,128)(2,1)} collective-permute-done((bf16[640,2048]{1,0:T(8,128)(2,1)}, bf16[640,2048]{1,0:T(8,128)(2,1)}, u32[]{:S(2)}, u32[]{:S(2)}) %collective-permute-start.45) | collective-permute-done | bytes 2621472 | tf_op jit(solution)/shard_map/ppermute | solution.py:407
  682.1 45.7 %attn_bwd.2 = (bf16[512,1024]{1,0:T(8,128)(2,1)}, bf16[512,1024]{1,0:T(8,128)(2,1)}, f32[5120,256]{1,0:T(8,128)}) custom-call(s32[6,4]{1,0:T(8,128)} %bitcast.325, bf16[640,1024]{1,0:T(8,128)(2,1)} %add_convert_fusion.8.refs_0_, bf16[640,1024]{1,0:T(8,128)(2,1)} %add_convert_fusion.7.refs_1_, bf16[640,1024]{1,0:T(8,128)(2,1)} %convolution_convert_fusion.4.refs_2_, ...), custom_call_target="tpu_custom_call" | custom-call | flops 1000000 | bytes 1000000 | tf_op jit(solution)/shard_map/attn_bwd/pallas_call | solution.py:186
  731.5 23.7 %collective-permute-done.48.refs_10_ = bf16[2,512,1024]{2,1,0:T(8,128)(2,1)} collective-permute-done((bf16[2,512,1024]{2,1,0:T(8,128)(2,1)}, bf16[2,512,1024]{2,1,0:T(8,128)(2,1)}, u32[]{:S(2)}, u32[]{:S(2)}) %collective-permute-start.48) | collective-permute-done | bytes 2097184 | tf_op jit(solution)/shard_map/ppermute | solution.py:407
  763.3 20.7 %attn_bwd.3 = (bf16[128,1024]{1,0:T(8,128)(2,1)}, bf16[128,1024]{1,0:T(8,128)(2,1)}, f32[5120,256]{1,0:T(8,128)}) custom-call(s32[6,1]{1,0:T(8,128)} %slice.184.tab, bf16[640,1024]{1,0:T(8,128)(2,1)} %add_convert_fusion.8.refs_0_, bf16[640,1024]{1,0:T(8,128)(2,1)} %add_convert_fusion.7.refs_1_, bf16[640,1024]{1,0:T(8,128)(2,1)} %convolution_convert_fusion.4.refs_2_, ...), custom_call_target="tpu_custom_call" | custom-call | flops 1000000 | bytes 1000000 | tf_op jit(solution)/shard_map/attn_bwd/pallas_call | solution.py:186
  830.2 15.8 %collective-permute-done.50 = bf16[640,512]{1,0:T(8,128)(2,1)} collective-permute-done((bf16[640,512]{1,0:T(8,128)(2,1)}, bf16[640,512]{1,0:T(8,128)(2,1)}, u32[]{:S(2)}, u32[]{:S(2)}) %collective-permute-start.50) | collective-permute-done | bytes 655392 | tf_op jit(solution)/shard_map/ppermute | solution.py:407
  942.7 13.9 %collective-permute-done.70 = bf16[576,256]{1,0:T(8,128)(2,1)} collective-permute-done((bf16[576,256]{1,0:T(8,128)(2,1)S(1)}, bf16[576,256]{1,0:T(8,128)(2,1)}, u32[]{:S(2)}, u32[]{:S(2)}) %collective-permute-start.70) | collective-permute-done | bytes 294944 | tf_op jit(solution)/shard_map/ppermute | solution.py:407
  961.3 17.7 %collective-permute-done.73 = bf16[512,256]{0,1:T(8,128)(2,1)S(1)} collective-permute-done((bf16[512,256]{0,1:T(8,128)(2,1)S(1)}, bf16[512,256]{0,1:T(8,128)(2,1)S(1)}, u32[]{:S(2)}, u32[]{:S(2)}) %collective-permute-start.73) | collective-permute-done | bytes 262176 | tf_op jit(solution)/shard_map/ppermute | solution.py:407
  (565 shorter events, 450.3 us)
Async XLA Ops:
  7.2 189.1 %all-gather.5.cloned.1.call-start = ((), (), s32[]{:S(2)}) async-start(), calls=%async_computation.4 | async-start | bytes 5242880 | tf_op jit(solution)/shard_map/all_gather | solution.py:456
  64.2 227.7 %all-gather.7.cloned.1.call-start = ((), (), s32[]{:S(2)}) async-start(), calls=%async_computation.5 | async-start | bytes 5242880 | tf_op jit(solution)/shard_map/all_gather | solution.py:456
  84.4 39.7 %collective-permute-start.21 = (bf16[640,512]{1,0:T(8,128)(2,1)}, bf16[640,512]{1,0:T(8,128)(2,1)S(1)}, u32[]{:S(2)}, u32[]{:S(2)}) collective-permute-start(bf16[640,512]{1,0:T(8,128)(2,1)} %get-tuple-element.68), channel_id=1, source_target_pairs={{0,4},{4,0},{8,12},{12,8},{1,5},{5,1},{9,13},{13,9},{2,6},{6,2},{1... | collective-permute-start | bytes 1966088 | tf_op jit(solution)/shard_map/ppermute | solution.py:407
  165.6 175.0 %all-gather.9.cloned.1.call-start = ((), (), s32[]{:S(2)}) async-start(), calls=%async_computation.6 | async-start | bytes 10485760 | tf_op jit(solution)/shard_map/all_gather | solution.py:456
  169.8 285.8 %all-gather.11.cloned.1.call-start = ((), (), s32[]{:S(2)}) async-start(), calls=%async_computation.7 | async-start | bytes 10485760 | tf_op jit(solution)/shard_map/all_gather | solution.py:456
  197.1 38.4 %collective-permute-start.28 = (bf16[2048,1024]{1,0:T(8,128)(2,1)}, bf16[2048,1024]{1,0:T(8,128)(2,1)}, u32[]{:S(2)}, u32[]{:S(2)}) collective-permute-start(bf16[2048,1024]{1,0:T(8,128)(2,1)} %hold.21), channel_id=1, source_target_pairs={{0,16},{16,0},{1,17},{17,1},{2,18},{18,2},{3,19},{19,3},{4,20},{20... | collective-permute-start | bytes 12582920 | tf_op jit(solution)/shard_map/ppermute | solution.py:407
  197.1 91.1 %collective-permute-start.37 = (bf16[2,512,128]{2,1,0:T(8,128)(2,1)}, bf16[2,512,128]{2,1,0:T(8,128)(2,1)}, u32[]{:S(2)}, u32[]{:S(2)}) collective-permute-start(bf16[2,512,128]{2,1,0:T(8,128)(2,1)} %get-tuple-element.207), channel_id=1, source_target_pairs={{0,2},{1,3},{2,0},{3,1},{4,6},{5,7},{6,4},{7,5},{8,10},{9,11},{10,... | collective-permute-start | bytes 786440 | tf_op jit(solution)/shard_map/ppermute | solution.py:407
  200.0 88.2 %collective-permute-start.36 = (bf16[2,512,128]{2,1,0:T(8,128)(2,1)}, bf16[2,512,128]{2,1,0:T(8,128)(2,1)}, u32[]{:S(2)}, u32[]{:S(2)}) collective-permute-start(bf16[2,512,128]{2,1,0:T(8,128)(2,1)} %get-tuple-element.214), channel_id=1, source_target_pairs={{0,2},{1,3},{2,0},{3,1},{4,6},{5,7},{6,4},{7,5},{8,10},{9,11},{10,... | collective-permute-start | bytes 786440 | tf_op jit(solution)/shard_map/ppermute | solution.py:407
  205.5 82.8 %collective-permute-start.38 = (bf16[640,2048]{1,0:T(8,128)(2,1)}, bf16[640,2048]{1,0:T(8,128)(2,1)}, u32[]{:S(2)}, u32[]{:S(2)}) collective-permute-start(bf16[640,2048]{1,0:T(8,128)(2,1)} %get-tuple-element.156.refs_4_.refs_2_), channel_id=1, source_target_pairs={{0,1},{1,0},{2,3},{3,2},{4,5},{5,4},{6,7},{7,6},{8,9},{9,8},{10,11... | collective-permute-start | bytes 7864328 | tf_op jit(solution)/shard_map/ppermute | solution.py:407
  291.8 276.0 %reduce-scatter.5.cloned.1.call-start = ((), (), s32[]{:S(2)}) async-start(), calls=%async_computation.8 | async-start | bytes 10485760 | tf_op jit(solution)/shard_map/reduce_scatter | solution.py:530
  340.4 59.2 %collective-permute-start.39 = (bf16[640,2048]{1,0:T(8,128)(2,1)}, bf16[640,2048]{1,0:T(8,128)(2,1)}, u32[]{:S(2)}, u32[]{:S(2)}) collective-permute-start(bf16[640,2048]{1,0:T(8,128)(2,1)} %add_convert_fusion.5.refs_0_), channel_id=1, source_target_pairs={{0,1},{1,0},{2,3},{3,2},{4,5},{5,4},{6,7},{7,6},{8,9},{9,8},{10,11... | collective-permute-start | bytes 7864328 | tf_op jit(solution)/shard_map/ppermute | solution.py:407
  340.4 59.2 %collective-permute-start.41 = (bf16[640,2048]{1,0:T(8,128)(2,1)}, bf16[640,2048]{1,0:T(8,128)(2,1)}, u32[]{:S(2)}, u32[]{:S(2)}) collective-permute-start(bf16[640,2048]{1,0:T(8,128)(2,1)} %get-tuple-element.86.refs_2_.refs_6_), channel_id=1, source_target_pairs={{0,16},{16,0},{1,17},{17,1},{2,18},{18,2},{3,19},{19,3},{4,20},{20... | collective-permute-start | bytes 7864328 | tf_op jit(solution)/shard_map/ppermute | solution.py:407
  455.6 205.6 %reduce-scatter.7.cloned.1.call-start = ((), (), s32[]{:S(2)}) async-start(), calls=%async_computation.9 | async-start | bytes 10485760 | tf_op jit(solution)/shard_map/reduce_scatter | solution.py:530
  567.8 316.3 %reduce-scatter.11.cloned.1.call-start = ((), (), s32[]{:S(2)}) async-start(), calls=%async_computation.11 | async-start | bytes 5242880 | tf_op jit(solution)/shard_map/reduce_scatter | solution.py:530
  567.9 59.2 %collective-permute-start.45 = (bf16[640,2048]{1,0:T(8,128)(2,1)}, bf16[640,2048]{1,0:T(8,128)(2,1)}, u32[]{:S(2)}, u32[]{:S(2)}) collective-permute-start(bf16[640,2048]{1,0:T(8,128)(2,1)} %hold.26.refs_12_), channel_id=1, source_target_pairs={{0,1},{1,0},{2,3},{3,2},{4,5},{5,4},{6,7},{7,6},{8,9},{9,8},{10,11... | collective-permute-start | bytes 7864328 | tf_op jit(solution)/shard_map/ppermute | solution.py:407
  568.0 59.2 %collective-permute-start.47 = (bf16[640,2048]{1,0:T(8,128)(2,1)}, bf16[640,2048]{1,0:T(8,128)(2,1)}, u32[]{:S(2)}, u32[]{:S(2)}) collective-permute-start(bf16[640,2048]{1,0:T(8,128)(2,1)} %get-tuple-element.100), channel_id=1, source_target_pairs={{0,16},{16,0},{1,17},{17,1},{2,18},{18,2},{3,19},{19,3},{4,20},{20... | collective-permute-start | bytes 7864328 | tf_op jit(solution)/shard_map/ppermute | solution.py:407
  653.2 144.0 %collective-permute-start.43 = (bf16[640,2048]{1,0:T(8,128)(2,1)}, bf16[640,2048]{1,0:T(8,128)(2,1)}, u32[]{:S(2)}, u32[]{:S(2)}) collective-permute-start(bf16[640,2048]{1,0:T(8,128)(2,1)} %get-tuple-element.98), channel_id=1, source_target_pairs={{0,16},{16,0},{1,17},{17,1},{2,18},{18,2},{3,19},{19,3},{4,20},{20... | collective-permute-start | bytes 7864328 | tf_op jit(solution)/shard_map/ppermute | solution.py:407
  661.1 296.7 %reduce-scatter.9.cloned.1.call-start = ((), (), s32[]{:S(2)}) async-start(), calls=%async_computation.10 | async-start | bytes 5242880 | tf_op jit(solution)/shard_map/reduce_scatter | solution.py:530
  661.2 94.0 %collective-permute-start.48 = (bf16[2,512,1024]{2,1,0:T(8,128)(2,1)}, bf16[2,512,1024]{2,1,0:T(8,128)(2,1)}, u32[]{:S(2)}, u32[]{:S(2)}) collective-permute-start(bf16[2,512,1024]{2,1,0:T(8,128)(2,1)} %reduce-scatter.7.cloned.1.call-done.refs_9_), channel_id=1, source_target_pairs={{0,2},{1,3},{2,0},{3,1},{4,6},{5,7},{6,4},{7,5},{8,10},{9,11},{10,... | collective-permute-start | bytes 6291464 | tf_op jit(solution)/shard_map/ppermute | solution.py:407
  681.2 116.1 %collective-permute-start.46 = (bf16[640,2048]{1,0:T(8,128)(2,1)}, bf16[640,2048]{1,0:T(8,128)(2,1)}, u32[]{:S(2)}, u32[]{:S(2)}) collective-permute-start(bf16[640,2048]{1,0:T(8,128)(2,1)} %hold.29), channel_id=1, source_target_pairs={{0,1},{1,0},{2,3},{3,2},{4,5},{5,4},{6,7},{7,6},{8,9},{9,8},{10,11... | collective-permute-start | bytes 7864328 | tf_op jit(solution)/shard_map/ppermute | solution.py:407
  759.2 113.1 %collective-permute-start.83 = (bf16[1024,512]{0,1:T(8,128)(2,1)}, bf16[1024,512]{0,1:T(8,128)(2,1)}, u32[]{:S(2)}, u32[]{:S(2)}) collective-permute-start(bf16[1024,512]{0,1:T(8,128)(2,1)} %get-tuple-element.205), channel_id=1, source_target_pairs={{0,16},{16,0},{1,17},{17,1},{2,18},{18,2},{3,19},{19,3},{4,20},{20... | collective-permute-start | bytes 3145736 | tf_op jit(solution)/shard_map/ppermute | solution.py:407
  936.0 52.3 %collective-permute-start.64 = (bf16[640,512]{1,0:T(8,128)(2,1)}, bf16[640,512]{1,0:T(8,128)(2,1)S(1)}, u32[]{:S(2)}, u32[]{:S(2)}) collective-permute-start(bf16[640,512]{1,0:T(8,128)(2,1)} %get-tuple-element.179), channel_id=1, source_target_pairs={{0,4},{4,0},{8,12},{12,8},{1,5},{5,1},{9,13},{13,9},{2,6},{6,2},{1... | collective-permute-start | bytes 1966088 | tf_op jit(solution)/shard_map/ppermute | solution.py:407
  937.9 50.5 %collective-permute-start.63 = (bf16[640,512]{1,0:T(8,128)(2,1)}, bf16[640,512]{1,0:T(8,128)(2,1)S(1)}, u32[]{:S(2)}, u32[]{:S(2)}) collective-permute-start(bf16[640,512]{1,0:T(8,128)(2,1)} %get-tuple-element.180), channel_id=1, source_target_pairs={{0,8},{4,12},{8,0},{12,4},{1,9},{5,13},{9,1},{13,5},{2,10},{6,14},... | collective-permute-start | bytes 1966088 | tf_op jit(solution)/shard_map/ppermute | solution.py:407
  941.0 47.4 %collective-permute-start.62 = (bf16[640,512]{1,0:T(8,128)(2,1)}, bf16[640,512]{1,0:T(8,128)(2,1)}, u32[]{:S(2)}, u32[]{:S(2)}) collective-permute-start(bf16[640,512]{1,0:T(8,128)(2,1)} %get-tuple-element.181), channel_id=1, source_target_pairs={{0,12},{4,8},{8,4},{12,0},{1,13},{5,9},{9,5},{13,1},{2,14},{6,10},... | collective-permute-start | bytes 1966088 | tf_op jit(solution)/shard_map/ppermute | solution.py:407
  (151 other events, 2110.4 us)
Sparse Core Ops, SparseCore 0:
  64.3 80.5 all-gather.4
  165.7 62.5 all-gather.6
  230.1 87.5 all-gather.8
  319.5 87.5 all-gather.10
  455.7 85.4 reduce-scatter.4
  568.0 86.2 reduce-scatter.6
  661.2 52.2 reduce-scatter.10
  830.2 59.0 reduce-scatter.8
